TPU v7x, 512 devices: a whole 4x8x8 slice. The times are simulated.
512 devices in a mesh: section: 8 (over y_lo, x), peer: 64 (over y_hi, z, core).
Axes of the slice: x: 4, y: 8 (y_hi: 4, y_lo: 2; y = y_hi * 2 + y_lo), z: 8, core: 2. Of those that a mesh axis runs over, the one named last changes fastest.
Arguments:
- placing: int32 [8, 64, 1], replicated, may hold values from 0 to 63; in each aligned block of 64 rows (0 to 63, 64 to 127, ..., all dimensions but the last counted through in order) at most 2 rows name the same one
- acts: bfloat16 [8, 64, 2, 2, 5120], P('section', 'peer'), may hold values from -6 to 6
- cotan: bfloat16 [8, 64, 2, 2, 5120], P('section', 'peer'), may hold values from -48 to 48
- gain: bfloat16 [8, 5120], P('section'), may hold values from 0.5 to 1.5
- w_value: bfloat16 [8, 2560, 5120], P('section', 'peer'), may hold values from -0.078125 to 0.078125
- w_out: bfloat16 [8, 5120, 2560], P('section', 'peer'), may hold values from -1 to 1
- moment_one: float32 [8, 2560, 5120], P('section', 'peer'), may hold values from -0.0006 to 0.0006
- moment_two: float32 [8, 2560, 5120], P('section', 'peer'), may hold values from 1e-07 to 1e-05
Outputs:
- passed: bfloat16 [8, 64, 2, 2, 5120], P('section', 'peer')
- returned: bfloat16 [8, 64, 2, 2, 5120], P('section', 'peer')
- new_value: bfloat16 [8, 2560, 5120], P('section', 'peer')
- new_first: float32 [8, 2560, 5120], P('section', 'peer')
- new_second: float32 [8, 2560, 5120], P('section', 'peer')
Inputs may be any that keep to these rules, and one draw needn't show every extreme that they name: `placing`: at every section no peer holds more than 2 micro-batches, and some peer holds exactly 2.
All inputs are finite; a program needn't handle non-finite values.
Results may differ from a plain program's by a relative error of at most 0.011.
Values may be sent and summed in bfloat16 or wider, within the bound.
No kernel may reach another device: no remote copies, remote signals or barrier semaphores. Data moves between devices by JAX's collectives and lax.ppermute only.
A program may use at most 64 MiB of HBM per device.

v0:
```python
import jax
import jax.numpy as jnp
from jax import lax
from jax.sharding import PartitionSpec as P

NORM_EPS = 1e-05
CLIP_NORM = 1.0
LEARN_RATE = 0.001
BETA_ONE = 0.9
BETA_TWO = 0.95
ADAM_EPS = 1e-08
DECAY = 0.1


def from_behind(block, axis, distance):
    devices = range(lax.axis_size(axis))
    route = [((i - distance) % len(devices), i) for i in devices]
    return lax.ppermute(block, axis, route)


def slot_table(placed, section_at, peer_count, capacity):
    current = lax.dynamic_index_in_dim(placed, section_at, 0, keepdims=False)
    micro_ids = jnp.arange(peer_count, dtype=jnp.int32)
    same_place = current[:, None] == current[None, :]
    earlier = micro_ids[None, :] < micro_ids[:, None]
    ranks = jnp.sum(jnp.where(same_place & earlier, 1, 0), axis=1).astype(jnp.int32)
    slots = current * capacity + ranks
    every_slot = jnp.arange(peer_count * capacity, dtype=jnp.int32)
    return (every_slot[:, None] == slots[None, :]).astype(jnp.bfloat16)


def compact(slot_map, blocks):
    shaped = blocks.reshape(slot_map.shape[0], -1)
    picked = jnp.einsum("am,af->mf", slot_map, shaped, preferred_element_type=jnp.float32)
    return picked.astype(jnp.bfloat16).reshape(-1, blocks.shape[1])


def spread(slot_map, blocks):
    shaped = blocks.reshape(slot_map.shape[1], -1)
    placed_rows = jnp.einsum("am,mf->af", slot_map, shaped, preferred_element_type=jnp.float32)
    return placed_rows.astype(jnp.bfloat16).reshape(-1, blocks.shape[1])


def projections(normed_all, cot_all, value_rows, out_rows, value_cols, out_cols):
    values = jnp.einsum(
        "rd,cd->rc", normed_all, value_rows, preferred_element_type=jnp.float32
    ).astype(jnp.bfloat16)
    values_all = lax.all_gather(values, "peer", axis=1, tiled=True)
    mixed = jnp.einsum("rh,fh->rf", values_all, out_rows, preferred_element_type=jnp.float32)
    value_grads = jnp.einsum(
        "rd,dc->rc", cot_all, out_cols, preferred_element_type=jnp.float32
    ).astype(jnp.bfloat16)
    gradient = jnp.einsum("rc,rd->cd", value_grads, normed_all, preferred_element_type=jnp.float32)
    grads_all = lax.all_gather(value_grads, "peer", axis=1, tiled=True)
    norm_grads = jnp.einsum("rh,hf->rf", grads_all, value_cols, preferred_element_type=jnp.float32)
    return (mixed, gradient, norm_grads)


def body(placing, acts, cotan, gain, w_value, w_out, moment_one, moment_two):
    peer_count = lax.axis_size("peer")
    section_now = lax.axis_index("section")
    peer_now = lax.axis_index("peer")
    capacity = acts.shape[2]
    micro_rows = acts.shape[3]
    model_width = acts.shape[4]
    placed = placing[:, :, 0]
    slot_map = slot_table(placed, section_now, peer_count, capacity)
    value_cols, out_cols = (
        lax.all_to_all(w_value[0], "peer", split_axis=1, concat_axis=0, tiled=True),
        lax.all_to_all(w_out[0], "peer", split_axis=1, concat_axis=0, tiled=True),
    )
    stream = acts[0, 0].reshape(capacity * micro_rows, model_width)
    cotangent = cotan[0, 0].reshape(capacity * micro_rows, model_width)
    gains = gain[0].astype(jnp.float32)
    own_slots = lax.dynamic_slice_in_dim(slot_map, peer_now * capacity, capacity, 0)
    live_slots = (
        jnp.repeat(jnp.sum(own_slots.astype(jnp.float32), axis=1), micro_rows)[:, None] > 0.5
    )
    inputs = stream.astype(jnp.float32)
    inverse_rms = lax.rsqrt(jnp.mean(inputs * inputs, axis=1, keepdims=True) + NORM_EPS)
    unit = inputs * inverse_rms
    normed = jnp.where(live_slots, unit * gains, 0.0).astype(jnp.bfloat16)
    kept_cot = jnp.where(live_slots, cotangent, jnp.zeros_like(cotangent))
    normed_all = lax.all_gather(normed, "peer", axis=0, tiled=True)
    cot_all = lax.all_gather(kept_cot, "peer", axis=0, tiled=True)
    stream_cols = lax.all_to_all(stream, "peer", split_axis=1, concat_axis=0, tiled=True)
    mixed, gradient, norm_grads = projections(
        normed_all, cot_all, w_value[0], w_out[0], value_cols, out_cols
    )
    output_cols = (stream_cols.astype(jnp.float32) + mixed).astype(jnp.bfloat16)
    norm_rows = lax.all_to_all(
        norm_grads.astype(jnp.bfloat16), "peer", split_axis=0, concat_axis=1, tiled=True
    ).astype(norm_grads.dtype)
    unit_grads = norm_rows * gains
    inner = jnp.mean(unit_grads * unit, axis=1, keepdims=True)
    back = (cotangent.astype(jnp.float32) + inverse_rms * (unit_grads - unit * inner)).astype(
        jnp.bfloat16
    )
    back_cols = lax.all_to_all(back, "peer", split_axis=1, concat_axis=0, tiled=True)
    forward_ids = compact(slot_map, output_cols)
    backward_ids = compact(slot_map, back_cols)
    arrived = from_behind(forward_ids, "section", 1)
    handed = from_behind(backward_ids, "section", -1)
    passed_rows, returned_rows = (
        lax.all_to_all(spread(slot_map, arrived), "peer", split_axis=0, concat_axis=1, tiled=True),
        lax.all_to_all(spread(slot_map, handed), "peer", split_axis=0, concat_axis=1, tiled=True),
    )
    totals = lax.psum(jnp.sum(gradient * gradient), ("section", "peer"))
    clip_scale = jnp.minimum(1.0, CLIP_NORM / jnp.sqrt(totals + 1e-06))
    clipped = gradient * clip_scale
    first = BETA_ONE * moment_one[0] + (1.0 - BETA_ONE) * clipped
    second = BETA_TWO * moment_two[0] + (1.0 - BETA_TWO) * clipped * clipped
    weights = w_value[0].astype(jnp.float32)
    updated = weights - LEARN_RATE * (first / (jnp.sqrt(second) + ADAM_EPS) + DECAY * weights)
    slot_shape = (1, 1, capacity, micro_rows, model_width)
    return (
        passed_rows.reshape(slot_shape),
        returned_rows.reshape(slot_shape),
        updated.astype(jnp.bfloat16)[None],
        first[None],
        second[None],
    )


def solution(mesh):
    placed = (
        P(),
        P("section", "peer", None, None, None),
        P("section", "peer", None, None, None),
        P("section", None),
        P("section", "peer", None),
        P("section", "peer", None),
        P("section", "peer", None),
        P("section", "peer", None),
    )
    return jax.shard_map(
        body,
        mesh=mesh,
        in_specs=placed,
        out_specs=(
            P("section", "peer", None, None, None),
            P("section", "peer", None, None, None),
            P("section", "peer", None),
            P("section", "peer", None),
            P("section", "peer", None),
        ),
        check_vma=False,
    )
```

profile of v0, /device:TPU:1, one launch (start us, length us, event | category | flops | bytes accessed | tf_op | source)
XLA Modules:
  0.0 544.9 jit_solution(103129973696406943)
XLA Ops:
  7.2 0.7 dynamic-slice_bitcast_fusion
  7.9 0.2 select_reduce_fusion
  8.1 0.7 multiply_add_fusion
  8.7 0.1 convert_reduce_fusion
  9.0 0.8 reshape_squeeze.4
  9.8 0.7 select_bitcast_fusion
  10.6 0.8 reshape.160
  11.4 0.9 multiply_reduce_fusion.1
  12.5 0.8 convert_element_type.90
  13.2 0.7 fusion.14
  14.0 1.3 copy.56
  15.3 39.9 %all_to_all.109 = bf16[80,64,40]{0,2,1:T(8,128)(2,1)S(1)} all-to-all(bf16[80,64,40]{0,2,1:T(8,128)(2,1)S(1)} %bitcast.74), channel_id=1, replica_groups=mesh['section'=8,'peer'=64] {'peer'}, dimensions={1} | all-to-all | bytes 819200 | tf_op jit(solution)/shard_map/all_to_all | solution.py:70
  55.2 0.1 copy.57
  55.4 1.1 all_to_all.90
  56.5 54.5 %all-gather.13.cloned.1.call-done = bf16[64,4,5120]{2,1,0:T(4,128)(2,1)} async-done(((bf16[1,4,5120]{2,1,0:T(4,128)(2,1)}), bf16[64,4,5120]{2,1,0:T(4,128)(2,1)}) %all-gather.13.cloned.1.call-update) | async-done | bytes 2621456 | tf_op jit(solution)/shard_map/all_gather | solution.py:85
  111.0 4.0 reshape.165
  115.0 1.5 convolution_convert_fusion.5
  116.6 79.4 %all-gather.11.cloned.1.call-done = bf16[64,4,5120]{2,1,0:T(4,128)(2,1)} async-done(((bf16[1,4,5120]{2,1,0:T(4,128)(2,1)}), bf16[64,4,5120]{2,1,0:T(4,128)(2,1)}) %all-gather.11.cloned.1.call-update) | async-done | bytes 2621456 | tf_op jit(solution)/shard_map/all_gather | solution.py:84
  196.0 4.0 reshape.163
  200.1 1.5 convolution_convert_fusion.6
  201.6 0.1 all_to_all.82
  201.7 0.7 copy.51
  202.4 7.6 %all-to-all-start = ((bf16[4,64,80]{2,0,1:T(4,128)(2,1)}), bf16[4,64,80]{2,0,1:T(4,128)(2,1)}, u32[]{:S(2)}, u32[]{:S(2)}) async-start(bf16[4,64,80]{2,0,1:T(4,128)(2,1)} %copy.51), calls=%async_computation | async-start | bytes 131072 | tf_op jit(solution)/shard_map/all_to_all | solution.py:86
  210.0 1.7 all_to_all.91
  211.6 2.4 copy.58
  214.0 8.1 %all-to-all-done = bf16[4,64,80]{2,0,1:T(4,128)(2,1)} async-done(((bf16[4,64,80]{2,0,1:T(4,128)(2,1)}), bf16[4,64,80]{2,0,1:T(4,128)(2,1)}, u32[]{:S(2)}, u32[]{:S(2)}) %all-to-all-start) | async-done | bytes 40992 | tf_op jit(solution)/shard_map/all_to_all | solution.py:86
  222.1 5.2 all-to-all-start.3
  227.4 0.8 reshape.161
  228.1 1.4 convert_reduce_fusion.1
  229.5 0.8 mul.134
  230.3 1.5 convert_element_type.110
  231.8 1.6 copy.52
  233.5 15.1 %all-to-all-done.3 = bf16[40,64,80]{2,0,1:T(8,128)(2,1)} async-done(((bf16[40,64,80]{2,0,1:T(8,128)(2,1)}), bf16[40,64,80]{2,0,1:T(8,128)(2,1)}, u32[]{:S(2)}, u32[]{:S(2)}) %all-to-all-start.3) | async-done | bytes 409632 | tf_op jit(solution)/shard_map/all_to_all | solution.py:69
  248.5 43.0 %all-gather.9.cloned.1.call-done = bf16[256,2560]{0,1:T(8,128)(2,1)} async-done(((bf16[256,40]{0,1:T(8,128)(2,1)}), bf16[256,2560]{0,1:T(8,128)(2,1)}) %all-gather.9.cloned.1.call-update) | async-done | bytes 1310736 | tf_op jit(solution)/shard_map/all_gather | solution.py:54
  291.6 2.5 convolution_convert_fusion.1
  294.0 1.5 copy.59
  295.6 8.3 %all-to-all-start.4 = ((bf16[64,4,80]{2,1,0:T(4,128)(2,1)}), bf16[64,4,80]{2,1,0:T(4,128)(2,1)}, u32[]{:S(2)}, u32[]{:S(2)}) async-start(bf16[64,4,80]{2,1,0:T(4,128)(2,1)} %bitcast.79), calls=%async_computation.4 | async-start | bytes 131072 | tf_op jit(solution)/shard_map/all_to_all | solution.py:91
  303.9 71.2 %all-gather.7.cloned.1.call-done = bf16[256,2560]{0,1:T(8,128)(2,1)} async-done(((bf16[256,40]{0,1:T(8,128)(2,1)}), bf16[256,2560]{0,1:T(8,128)(2,1)}) %all-gather.7.cloned.1.call-update) | async-done | bytes 1310736 | tf_op jit(solution)/shard_map/all_gather | solution.py:48
  375.0 2.3 fusion
  377.3 0.9 copy.53
  378.2 0.1 reshape.151
  378.3 0.2 convolution_convert_fusion.4
  378.6 3.1 collective-permute-start
  381.7 1.0 fusion.10
  382.8 1.0 fusion.13
  383.8 0.7 copy.61
  384.5 8.4 %all-to-all-start.5 = ((bf16[4,64,80]{2,0,1:T(4,128)(2,1)}), bf16[4,64,80]{2,0,1:T(4,128)(2,1)S(1)}, u32[]{:S(2)}, u32[]{:S(2)}) async-start(bf16[4,64,80]{2,0,1:T(4,128)(2,1)} %copy.61), calls=%async_computation.5 | async-start | bytes 131072 | tf_op jit(solution)/shard_map/all_to_all | solution.py:99
  392.9 2.8 multiply_reduce_fusion
  395.6 98.5 %psum.7 = f32[]{:T(128)} all-reduce(f32[]{:T(128)} %get-tuple-element.8), channel_id=1, replica_groups=mesh['section'=8,'peer'=64] {'section','peer'}, use_global_device_ids=true, to_apply=%region_5.6 | all-reduce | flops 1 | bytes 8 | tf_op jit(solution)/shard_map/psum | solution.py:108
  495.0 0.2 convolution_convert_fusion.3
  495.3 3.1 collective-permute-start.1
  498.4 0.2 convolution_convert_fusion.2
  498.6 0.1 copy.54
  498.7 0.7 all_to_all.84
  499.5 9.0 %all-to-all-start.1 = ((bf16[64,4,80]{2,1,0:T(4,128)(2,1)}), bf16[64,4,80]{2,1,0:T(4,128)(2,1)S(1)}, u32[]{:S(2)}, u32[]{:S(2)}) async-start(bf16[64,4,80]{2,1,0:T(4,128)(2,1)} %all_to_all.84), calls=%async_computation.1 | async-start | bytes 131072 | tf_op jit(solution)/shard_map/all_to_all | solution.py:105
  508.6 0.2 convolution_convert_fusion
  508.8 0.1 copy.62
  508.9 0.7 all_to_all.99
  509.6 11.0 %all-to-all-done.1 = bf16[64,4,80]{2,1,0:T(4,128)(2,1)S(1)} async-done(((bf16[64,4,80]{2,1,0:T(4,128)(2,1)}), bf16[64,4,80]{2,1,0:T(4,128)(2,1)S(1)}, u32[]{:S(2)}, u32[]{:S(2)}) %all-to-all-start.1) | async-done | bytes 40992 | tf_op jit(solution)/shard_map/all_to_all | solution.py:105
  520.6 4.5 all-to-all-start.6
  525.1 3.6 fusion.9
  528.7 0.8 reshape.154
  529.5 8.1 %all-to-all-done.6 = bf16[64,4,80]{2,1,0:T(4,128)(2,1)S(1)} async-done(((bf16[64,4,80]{2,1,0:T(4,128)(2,1)}), bf16[64,4,80]{2,1,0:T(4,128)(2,1)S(1)}, u32[]{:S(2)}, u32[]{:S(2)}) %all-to-all-start.6) | async-done | bytes 40992 | tf_op jit(solution)/shard_map/all_to_all | solution.py:106
  537.6 0.8 reshape.158
  (34 shorter events, 1.0 us)
Async XLA Ops:
  7.2 103.8 %all-gather.13.cloned.1.call-start = ((), (), s32[]{:S(2)}) async-start(), calls=%async_computation.10 | async-start | bytes 2662400 | tf_op jit(solution)/shard_map/all_gather | solution.py:85
  10.6 185.4 %all-gather.11.cloned.1.call-start = ((), (), s32[]{:S(2)}) async-start(), calls=%async_computation.9 | async-start | bytes 2662400 | tf_op jit(solution)/shard_map/all_gather | solution.py:84
  13.9 277.6 %all-gather.9.cloned.1.call-start = ((), (), s32[]{:S(2)}) async-start(), calls=%async_computation.8 | async-start | bytes 1331200 | tf_op jit(solution)/shard_map/all_gather | solution.py:54
  116.6 83.5 %copy-start = (bf16[1,40,5120]{2,1,0:T(8,128)(2,1)S(1)}, bf16[1,40,5120]{2,1,0:T(8,128)(2,1)}, u32[]{:S(2)}) copy-start(bf16[1,40,5120]{2,1,0:T(8,128)(2,1)} %param.12) | copy-start | bytes 1228804
  116.6 258.4 %all-gather.7.cloned.1.call-start = ((), (), s32[]{:S(2)}) async-start(), calls=%async_computation.7 | async-start | bytes 1331200 | tf_op jit(solution)/shard_map/all_gather | solution.py:48
  200.1 1.5 copy-start.2
  201.6 25.8 %copy-start.3 = (bf16[1,1,2,2,5120]{4,3,2,1,0:T(2,128)(2,1)S(1)}, bf16[1,1,2,2,5120]{4,3,2,1,0:T(2,128)(2,1)}, u32[]{:S(2)}) copy-start(bf16[1,1,2,2,5120]{4,3,2,1,0:T(2,128)(2,1)} %param.10) | copy-start | bytes 122884
  202.4 19.7 %all-to-all-start = ((bf16[4,64,80]{2,0,1:T(4,128)(2,1)}), bf16[4,64,80]{2,0,1:T(4,128)(2,1)}, u32[]{:S(2)}, u32[]{:S(2)}) async-start(bf16[4,64,80]{2,0,1:T(4,128)(2,1)} %copy.51), calls=%async_computation | async-start | bytes 131072 | tf_op jit(solution)/shard_map/all_to_all | solution.py:86
  211.6 163.4 %copy-start.1 = (bf16[1,80,2560]{2,1,0:T(8,128)(2,1)S(1)}, bf16[1,80,2560]{2,1,0:T(8,128)(2,1)}, u32[]{:S(2)}) copy-start(bf16[1,80,2560]{2,1,0:T(8,128)(2,1)} %param.13) | copy-start | bytes 1228804
  222.1 26.4 %all-to-all-start.3 = ((bf16[40,64,80]{2,0,1:T(8,128)(2,1)}), bf16[40,64,80]{2,0,1:T(8,128)(2,1)}, u32[]{:S(2)}, u32[]{:S(2)}) async-start(bf16[40,64,80]{2,0,1:T(8,128)(2,1)} %copy.58), calls=%async_computation.3 | async-start | bytes 1310720 | tf_op jit(solution)/shard_map/all_to_all | solution.py:69
  295.6 86.2 %all-to-all-start.4 = ((bf16[64,4,80]{2,1,0:T(4,128)(2,1)}), bf16[64,4,80]{2,1,0:T(4,128)(2,1)}, u32[]{:S(2)}, u32[]{:S(2)}) async-start(bf16[64,4,80]{2,1,0:T(4,128)(2,1)} %bitcast.79), calls=%async_computation.4 | async-start | bytes 131072 | tf_op jit(solution)/shard_map/all_to_all | solution.py:91
  378.6 116.2 %collective-permute-start = (bf16[128,80]{1,0:T(8,128)(2,1)S(1)}, bf16[128,80]{1,0:T(8,128)(2,1)S(1)}, u32[]{:S(2)}, u32[]{:S(2)}) collective-permute-start(bf16[128,80]{1,0:T(8,128)(2,1)S(1)} %reshape.152), channel_id=1, source_target_pairs={{448,0},{0,64},{64,128},{128,192},{192,256},{256,320},{320,384},{3... | collective-permute-start | bytes 61448 | tf_op jit(solution)/shard_map/ppermute | solution.py:18
  384.5 110.5 %all-to-all-start.5 = ((bf16[4,64,80]{2,0,1:T(4,128)(2,1)}), bf16[4,64,80]{2,0,1:T(4,128)(2,1)S(1)}, u32[]{:S(2)}, u32[]{:S(2)}) async-start(bf16[4,64,80]{2,0,1:T(4,128)(2,1)} %copy.61), calls=%async_computation.5 | async-start | bytes 131072 | tf_op jit(solution)/shard_map/all_to_all | solution.py:99
  495.3 13.1 %collective-permute-start.1 = (bf16[128,80]{1,0:T(8,128)(2,1)S(1)}, bf16[128,80]{1,0:T(8,128)(2,1)S(1)}, u32[]{:S(2)}, u32[]{:S(2)}) collective-permute-start(bf16[128,80]{1,0:T(8,128)(2,1)S(1)} %reshape.156), channel_id=1, source_target_pairs={{64,0},{128,64},{192,128},{256,192},{320,256},{384,320},{448,384},... | collective-permute-start | bytes 61448 | tf_op jit(solution)/shard_map/ppermute | solution.py:18
  499.5 21.1 %all-to-all-start.1 = ((bf16[64,4,80]{2,1,0:T(4,128)(2,1)}), bf16[64,4,80]{2,1,0:T(4,128)(2,1)S(1)}, u32[]{:S(2)}, u32[]{:S(2)}) async-start(bf16[64,4,80]{2,1,0:T(4,128)(2,1)} %all_to_all.84), calls=%async_computation.1 | async-start | bytes 131072 | tf_op jit(solution)/shard_map/all_to_all | solution.py:105
  520.6 17.0 %all-to-all-start.6 = ((bf16[64,4,80]{2,1,0:T(4,128)(2,1)}), bf16[64,4,80]{2,1,0:T(4,128)(2,1)S(1)}, u32[]{:S(2)}, u32[]{:S(2)}) async-start(bf16[64,4,80]{2,1,0:T(4,128)(2,1)} %all_to_all.99), calls=%async_computation.6 | async-start | bytes 131072 | tf_op jit(solution)/shard_map/all_to_all | solution.py:106
Sparse Core Ops, SparseCore 0:
  11.9 99.0 all-gather.12
  114.9 81.0 all-gather.10
  199.3 92.2 all-gather.8
  295.3 79.7 all-gather.6
where the time goes:
time: 546 us; the launch traced here: 545 us
  waiting for transfers between devices  290 us (53%)
  blocking collectives  138 us (25%)
  starting transfers between devices  49.3 us (9%)
  local copies, waits for them, and re-layouts  28.1 us (5%)
  between operations  14.8 us (3%)
  other arithmetic  12.6 us (2%)
  matrix products  11.4 us (2%)
    psum x1, blocking collectives, body(): totals = lax.psum(jnp.sum(gradient * gradient), ('section', 'peer'))  98.5 us
    all_gather x1, waiting for transfers between devices, body(): normed_all = lax.all_gather(normed, 'peer', axis=0, tiled=True)  79.4 us
    all_gather x1, waiting for transfers between devices, projections(): values_all = lax.all_gather(values, 'peer', axis=1, tiled=True)  71.2 us
    all_gather x1, waiting for transfers between devices, body(): cot_all = lax.all_gather(kept_cot, 'peer', axis=0, tiled=True)  54.5 us
    all_gather x1, waiting for transfers between devices, projections(): grads_all = lax.all_gather(value_grads, 'peer', axis=1, tiled=True)  43 us
    all_to_all x1, blocking collectives, body(): lax.all_to_all(w_out[0], 'peer', split_axis=1, concat_axis=0, tiled=True)  39.9 us
    all_to_all x1, waiting for transfers between devices, body(): lax.all_to_all(w_value[0], 'peer', split_axis=1, concat_axis=0, tiled=True)  15.1 us
    all_to_all x1, waiting for transfers between devices, body(): lax.all_to_all(spread(slot_map, arrived), 'peer', split_axis=0, concat_ax...  11 us
  transfers between devices with their start and end apart: 12, of which 8 were waited for; matrix products, arithmetic and copies ran while one was open for 8% of the time, Pallas kernels for 0%

commit v1 on v0

v1 whole, which is shorter than its diff:
```python
import jax
import jax.numpy as jnp
from jax import lax
from jax.sharding import Mesh, PartitionSpec as P

NORM_EPS = 1e-05
CLIP_NORM = 1.0
LEARN_RATE = 0.001
BETA_ONE = 0.9
BETA_TWO = 0.95
ADAM_EPS = 1e-08
DECAY = 0.1
PEER = ("chip", "core")
SPARE = 8


def matmul(equation, left, right):
    return jnp.einsum(equation, left, right, preferred_element_type=jnp.float32)


def swap(blocks, axis):
    return lax.all_to_all(blocks, axis, split_axis=0, concat_axis=0, tiled=True)


def moved(block, axis, distance):
    count = lax.axis_size(axis)
    return lax.ppermute(block, axis, [(i, (i + distance) % count) for i in range(count)])


def to_all(block, count):
    return jnp.broadcast_to(block[None], (count,) + block.shape)


def three_parts(values):
    high = lax.reduce_precision(values, 8, 7)
    rest = values - high
    middle = lax.reduce_precision(rest, 8, 7)
    return [part.astype(jnp.bfloat16) for part in (high, middle, rest - middle)]


def selection(placed, capacity, micro_rows):
    count = placed.shape[0]
    ids = jnp.arange(count, dtype=jnp.int32)
    twins = (placed[:, None] == placed[None, :]) & (ids[:, None] < ids[None, :])
    slots = placed * capacity + jnp.sum(twins.astype(jnp.int32), axis=0)
    rows = (slots[:, None] * micro_rows + jnp.arange(micro_rows, dtype=jnp.int32)).reshape(-1)
    every = jnp.arange(count * capacity * micro_rows, dtype=jnp.int32)
    return (every[:, None] == rows[None, :]).astype(jnp.bfloat16)


def body(placing, acts, cotan, gain, w_value, w_out, moment_one, moment_two):
    chips = lax.axis_size("chip")
    peers = 2 * chips
    section_now = lax.axis_index("section")
    peer_now = lax.axis_index(PEER)
    _, _, capacity, micro_rows, model = acts.shape
    slot_rows = capacity * micro_rows
    width = model // peers
    heads = w_value.shape[1]
    rows = peers * micro_rows
    weights, out_weights = w_value[0], w_out[0]

    held = jnp.concatenate(
        [acts[0, 0].reshape(slot_rows, model), cotan[0, 0].reshape(slot_rows, model)]
    )
    cols = swap(held.reshape(2 * slot_rows, peers, width).transpose(1, 0, 2), PEER)
    placed = lax.dynamic_index_in_dim(placing[:, :, 0], section_now, 0, keepdims=False)
    select = selection(placed, capacity, micro_rows)
    gain_col = jnp.broadcast_to(gain[0][:, None], (model, rows))
    cols = cols.reshape(peers, 2, slot_rows, width).transpose(1, 0, 2, 3)
    stacked = matmul("ksf,sr->kfr", cols.reshape(2, peers * slot_rows, width), select)
    stream, cotangent = stacked[0].astype(jnp.bfloat16), stacked[1].astype(jnp.bfloat16)

    grads = matmul("fh,fr->hr", out_weights, cotangent).astype(jnp.bfloat16)
    grads = swap(grads.reshape(chips, 2, heads, rows).transpose(1, 0, 2, 3), "core")
    grads = jnp.sum(grads.astype(jnp.float32), axis=0).astype(jnp.bfloat16)
    first_trip = swap(jnp.concatenate([to_all(stream, chips), grads], axis=1), "chip")
    value_grads = jnp.sum(first_trip[:, width:].astype(jnp.float32), axis=0).astype(jnp.bfloat16)
    streams = lax.all_gather(first_trip[:, :width], "core", axis=1).reshape(model, rows)

    inputs = streams.astype(jnp.float32)
    inverse_rms = lax.rsqrt(jnp.mean(inputs * inputs, axis=0, keepdims=True) + NORM_EPS)
    normed = (inputs * inverse_rms * gain_col.astype(jnp.float32)).astype(jnp.bfloat16)
    values = matmul("hd,dr->hr", weights, normed)
    norm_grads = matmul("hd,hr->dr", weights, value_grads).astype(jnp.bfloat16)
    norm_grads = swap(norm_grads.reshape(chips, 2, width, rows).transpose(1, 0, 2, 3), "core")
    norm_grads = jnp.sum(norm_grads.astype(jnp.float32), axis=0).astype(jnp.bfloat16)
    gradient = matmul("hr,dr->hd", value_grads, normed)

    inner = jnp.sum(value_grads.astype(jnp.float32) * values, axis=0)
    square = jnp.broadcast_to(jnp.sum(gradient * gradient), inner.shape)
    extra = jnp.stack(three_parts(inner) + three_parts(square))
    extra = jnp.pad(extra, ((0, SPARE - extra.shape[0]), (0, 0)))
    own = jnp.concatenate([values.astype(jnp.bfloat16), extra])
    second_trip = swap(jnp.concatenate([norm_grads, to_all(own, chips)], axis=1), "chip")
    norm_grads = jnp.sum(second_trip[:, :width].astype(jnp.float32), axis=0)
    gathered = lax.all_gather(second_trip[:, width:], "core", axis=1)
    extra = jnp.sum(gathered[:, :, heads:].astype(jnp.float32), axis=(0, 1))
    inner = jnp.sum(extra[0:3], axis=0, keepdims=True) / model
    square = jnp.sum(extra[3:6], axis=0)
    squares = swap(jnp.broadcast_to(square, (lax.axis_size("section"), SPARE, rows)), "section")
    totals = jnp.sum(squares[:, 0, 0])

    mixed = matmul("fh,hr->fr", out_weights, gathered[:, :, :heads].reshape(-1, rows))
    outputs = (stream.astype(jnp.float32) + mixed).astype(jnp.bfloat16)
    own_gain = lax.dynamic_slice_in_dim(gain_col, peer_now * width, width, 0).astype(jnp.float32)
    unit = stream.astype(jnp.float32) * inverse_rms
    back = (
        cotangent.astype(jnp.float32) + inverse_rms * (norm_grads * own_gain - unit * inner)
    ).astype(jnp.bfloat16)
    arrived = jnp.stack([moved(outputs, "section", 1), moved(back, "section", -1)])

    spread = matmul("sr,kfr->ksf", select, arrived).astype(jnp.bfloat16)
    spread = spread.reshape(2, peers, slot_rows, width).transpose(1, 0, 2, 3)
    final = swap(spread.reshape(peers, 2 * slot_rows, width), PEER)
    final = final.transpose(1, 0, 2).reshape((2, 1, 1, capacity, micro_rows, model))

    clip_scale = jnp.minimum(1.0, CLIP_NORM / jnp.sqrt(totals + 1e-06))
    clipped = gradient * clip_scale
    first = BETA_ONE * moment_one[0] + (1.0 - BETA_ONE) * clipped
    second = BETA_TWO * moment_two[0] + (1.0 - BETA_TWO) * clipped * clipped
    wide = weights.astype(jnp.float32)
    updated = wide - LEARN_RATE * (first / (jnp.sqrt(second) + ADAM_EPS) + DECAY * wide)
    return final[0], final[1], updated.astype(jnp.bfloat16)[None], first[None], second[None]


def solution(mesh):
    sections, peers = mesh.devices.shape
    fine = Mesh(mesh.devices.reshape(sections, peers // 2, 2), ("section",) + PEER)
    slots = P("section", PEER, None, None, None)
    matrix = P("section", PEER, None)
    return jax.shard_map(
        body,
        mesh=fine,
        in_specs=(P(), slots, slots, P("section", None), matrix, matrix, matrix, matrix),
        out_specs=(slots, slots, matrix, matrix, matrix),
        check_vma=False,
    )
```

time: 546 us -> 206 us (0.38)
  waiting for transfers between devices: 290 us -> 58.9 us
  blocking collectives: 138 us -> 47.6 us
  local copies, waits for them, and re-layouts: 28.1 us -> 9.77 us
  matrix products: 11.4 us -> 4.24 us
    all_gather x4 -> x1, waiting for transfers between devices: 248 us -> 6.79 us  [body(): lax.all_gather(first_trip[:, :width], 'core', axis=1).reshape(model, rows)]
    psum x1 -> x0, blocking collectives: 98.5 us -> none  [body(): totals = lax.psum(jnp.sum(gradient * gradient), ('section', 'peer'))]
    all_to_all x6 -> x4, waiting for transfers between devices: 42.2 us -> 52.1 us  [swap(): return lax.all_to_all(blocks, axis, split_axis=0, concat_axis=0, tiled=True)]
    unnamed x11 -> x16, local copies, waits for them, and re-layouts: 9.41 us -> 0.64 us
    all_to_all x10 -> x1, local copies, waits for them, and re-layouts: 7.6 us -> 0.02 us  [swap(): return lax.all_to_all(blocks, axis, split_axis=0, concat_axis=0, tiled=True)]
    dot_general x9 -> x7, matrix products: 11.4 us -> 4.24 us  [matmul(): return jnp.einsum(equation, left, right, preferred_element_type=jnp.float32)]
    all_to_all x1 -> x3, blocking collectives: 39.9 us -> 43.6 us  [swap(): return lax.all_to_all(blocks, axis, split_axis=0, concat_axis=0, tiled=True)]
    all_to_all x6 -> x4, starting transfers between devices: 43 us -> 45 us  [swap(): return lax.all_to_all(blocks, axis, split_axis=0, concat_axis=0, tiled=True)]
  transfers between devices with their start and end apart: 12 -> 7, of which waited for: 8 -> 5; matrix products, arithmetic and copies ran while one was open for 8% -> 6% of each run, Pallas kernels for 0% -> 0%
where the time goes in v1:
time: 206 us; the launch traced here: 205 us
  waiting for transfers between devices  58.9 us (29%)
  starting transfers between devices  50.4 us (24%)
  blocking collectives  47.6 us (23%)
  between operations  20.1 us (10%)
  other arithmetic  14 us (7%)
  local copies, waits for them, and re-layouts  9.77 us (5%)
  matrix products  4.24 us (2%)
    all_to_all x4, waiting for transfers between devices, swap(): return lax.all_to_all(blocks, axis, split_axis=0, concat_axis=0, tiled=True)  52.1 us
    all_to_all x4, starting transfers between devices, swap(): return lax.all_to_all(blocks, axis, split_axis=0, concat_axis=0, tiled=True)  45 us
    all_to_all x3, blocking collectives, swap(): return lax.all_to_all(blocks, axis, split_axis=0, concat_axis=0, tiled=True)  43.6 us
    all_gather x1, waiting for transfers between devices, body(): lax.all_gather(first_trip[:, :width], 'core', axis=1).reshape(model, rows)  6.79 us
    ppermute x2, starting transfers between devices, moved(): lax.ppermute(block, axis, [(i, (i + distance) % count) for i in range(cou...  5.41 us
    dot_general x7, matrix products, matmul(): return jnp.einsum(equation, left, right, preferred_element_type=jnp.float32)  4.24 us
  transfers between devices with their start and end apart: 7, of which 5 were waited for; matrix products, arithmetic and copies ran while one was open for 6% of the time, Pallas kernels for 0%

profile of v1, /device:TPU:1, one launch (start us, length us, event | category | flops | bytes accessed | tf_op | source)
XLA Modules:
  0.0 204.9 jit_solution(6332931383181338580)
XLA Ops:
  7.2 0.0 copy-start
  7.2 1.0 concatenate.18
  8.1 0.9 concatenate.17
  9.1 0.7 copy.55
  9.8 17.6 %all-to-all-start = ((bf16[64,8,80]{2,1,0:T(8,128)(2,1)}), bf16[64,8,80]{2,1,0:T(8,128)(2,1)S(1)}, u32[]{:S(2)}, u32[]{:S(2)}) async-start(bf16[64,8,80]{2,1,0:T(8,128)(2,1)} %copy.55), calls=%async_computation | async-start | bytes 262144 | tf_op jit(solution)/shard_map/all_to_all | solution.py:22
  27.5 0.0 all-gather.4.cloned.1.call-start
  27.5 0.7 dynamic-slice_bitcast_fusion
  28.2 0.1 convert_reduce_fusion.2
  28.3 0.7 add_multiply_fusion
  28.9 0.1 iota_add_fusion
  29.0 0.1 add.79
  29.2 10.8 %all-to-all-done = bf16[64,8,80]{2,1,0:T(8,128)(2,1)S(1)} async-done(((bf16[64,8,80]{2,1,0:T(8,128)(2,1)}), bf16[64,8,80]{2,1,0:T(8,128)(2,1)S(1)}, u32[]{:S(2)}, u32[]{:S(2)}) %all-to-all-start) | async-done | bytes 81952 | tf_op jit(solution)/shard_map/all_to_all | solution.py:22
  40.0 0.1 copy.57
  40.2 0.2 fusion.20
  40.4 0.4 fusion.1
  40.7 0.3 copy.59
  41.1 0.1 copy.60
  41.1 4.4 %all_to_all.35 = bf16[2,32,40,128]{3,2,1,0:T(8,128)(2,1)S(1)} all-to-all(bf16[2,32,40,128]{3,2,1,0:T(8,128)(2,1)S(1)} %copy.60), channel_id=1, replica_groups=mesh['section'=8,'chip'=32,'core'=2] {'core'}, dimensions={0} | all-to-all | bytes 1310720 | tf_op jit(solution)/shard_map/all_to_all | solution.py:22
  45.5 0.1 reduce_sum.120
  45.6 0.1 broadcast_in_dim.22
  45.7 0.1 pad_maximum_fusion.1
  45.8 32.8 %all_to_all.36 = bf16[32,120,128]{2,1,0:T(8,128)(2,1)S(1)} all-to-all(bf16[32,120,128]{2,1,0:T(8,128)(2,1)S(1)} %pad_maximum_fusion.1), channel_id=1, replica_groups=mesh['section'=8,'chip'=32,'core'=2] {'chip'}, dimensions={0} | all-to-all | bytes 1966080 | tf_op jit(solution)/shard_map/all_to_all | solution.py:22
  78.7 0.9 slice.57
  79.6 0.0 all-gather.4.cloned.1.call-update
  79.6 0.1 convert_reduce_fusion.3
  79.7 0.1 reshape.156
  79.8 0.1 slice_reduce_fusion
  79.9 0.5 fusion
  80.4 0.8 copy.61
  81.2 0.1 copy.62
  81.3 6.4 %all_to_all.37 = bf16[2,32,80,128]{3,2,1,0:T(8,128)(2,1)S(1)} all-to-all(bf16[2,32,80,128]{3,2,1,0:T(8,128)(2,1)S(1)} %copy.62), channel_id=1, replica_groups=mesh['section'=8,'chip'=32,'core'=2] {'core'}, dimensions={0} | all-to-all | bytes 2621440 | tf_op jit(solution)/shard_map/all_to_all | solution.py:22
  87.7 1.2 reduce_sum.122
  88.9 6.8 %all-gather.4.cloned.1.call-done = bf16[32,160,128]{2,1,0:T(8,128)(2,1)} async-done(((bf16[32,80,128]{2,1,0:T(8,128)(2,1)}), bf16[32,160,128]{2,1,0:T(8,128)(2,1)}) %all-gather.4.cloned.1.call-update) | async-done | bytes 1310736 | tf_op jit(solution)/shard_map/all_gather | solution.py:79
  95.7 2.1 %multiply_reduce_fusion = (f32[128]{0:T(128)S(1)}, f32[32,2,80,128]{3,2,1,0:T(8,128)S(1)}) fusion(bf16[32,2,80,128]{3,2,1,0:T(8,128)(2,1)} %bitcast.113), kind=kLoop, calls=%fused_computation.8 | loop fusion | flops 1965952 | bytes 3932672 | tf_op jit(solution)/shard_map/reduce_sum | solution.py:82
  97.9 2.2 %fusion.3 = bf16[5120,128]{1,0:T(8,128)(2,1)S(1)} fusion(f32[5120]{0:T(1024)S(1)} %bitcast.125, f32[128]{0:T(128)S(1)} %add_rsqrt_fusion, bf16[32,160,128]{2,1,0:T(8,128)(2,1)S(1)} %copy-done.1), kind=kLoop, calls=%fused_computation.6 | loop fusion | flops 2621440 | bytes 2642432 | tf_op jit(solution)/shard_map/convert_element_type | solution.py:83
  100.1 2.4 %multiply_reduce_fusion.1 = (f32[]{:T(128)}, f32[40,5120]{1,0:T(8,128)}) fusion(bf16[40,128]{1,0:T(8,128)(2,1)S(1)} %slice_reduce_fusion, bf16[5120,128]{1,0:T(8,128)(2,1)S(1)} %fusion.3), kind=kOutput, calls=%fused_computation.26 | convolution fusion | flops 52838400 | bytes 2140164 | tf_op jit(solution)/shard_map/hr,dr->hd/dot_general | solution.py:18
  107.4 0.9 multiply_convert_fusion
  108.2 0.3 fusion.41
  108.7 0.1 broadcast_in_dim.52
  108.7 0.6 copy-done.4
  109.3 1.1 pad_maximum_fusion
  110.4 11.4 %all-to-all-start.4 = ((bf16[32,128,128]{2,1,0:T(8,128)(2,1)}), bf16[32,128,128]{2,1,0:T(8,128)(2,1)S(1)}, u32[]{:S(2)}, u32[]{:S(2)}) async-start(bf16[32,128,128]{2,1,0:T(8,128)(2,1)} %pad_maximum_fusion), calls=%async_computation.4 | async-start | bytes 2097152 | tf_op jit(solution)/shard_map/all_to_all | solution.py:22
  121.8 1.3 bitcast_convert_fusion
  123.1 29.1 %all-to-all-done.4 = bf16[32,128,128]{2,1,0:T(8,128)(2,1)S(1)} async-done(((bf16[32,128,128]{2,1,0:T(8,128)(2,1)}), bf16[32,128,128]{2,1,0:T(8,128)(2,1)S(1)}, u32[]{:S(2)}, u32[]{:S(2)}) %all-to-all-start.4) | async-done | bytes 1048608 | tf_op jit(solution)/shard_map/all_to_all | solution.py:22
  152.2 3.9 %all-gather.1 = bf16[32,96,128]{2,1,0:T(8,128)(2,1)S(1)} all-gather(bf16[32,48,128]{2,1,0:T(8,128)(2,1)S(1)} %slice.58), channel_id=3, replica_groups=mesh['section'=8,'chip'=32,'core'=2] {'core'}, dimensions={1}, use_global_device_ids=true | all-gather | bytes 1179648 | tf_op jit(solution)/shard_map/all_gather | solution.py:97
  156.2 0.1 convert_reduce_fusion.1
  156.3 0.1 slice.59
  156.4 0.1 convert_reduce_fusion
  156.5 0.1 fusion.28
  156.6 2.6 %collective-permute-start.1 = (bf16[80,128]{1,0:T(8,128)(2,1)S(1)}, bf16[80,128]{1,0:T(8,128)(2,1)S(1)}, u32[]{:S(2)}, u32[]{:S(2)}) collective-permute-start(bf16[80,128]{1,0:T(8,128)(2,1)S(1)} %fusion.28), channel_id=1, source_target_pairs={{0,448},{64,0},{128,64},{192,128},{256,192},{320,256},{384,320},{4... | collective-permute-start | bytes 61448 | tf_op jit(solution)/shard_map/ppermute | solution.py:27
  159.2 0.3 fusion.6
  159.5 2.8 %collective-permute-start = (bf16[80,128]{1,0:T(8,128)(2,1)S(1)}, bf16[80,128]{1,0:T(8,128)(2,1)S(1)}, u32[]{:S(2)}, u32[]{:S(2)}) collective-permute-start(bf16[80,128]{1,0:T(8,128)(2,1)S(1)} %fusion.6), channel_id=1, source_target_pairs={{0,64},{64,128},{128,192},{192,256},{256,320},{320,384},{384,448},... | collective-permute-start | bytes 61448 | tf_op jit(solution)/shard_map/ppermute | solution.py:27
  162.3 0.6 broadcast_in_dim.54
  162.9 5.8 %all-to-all-start.6 = ((f32[8,8,128]{2,1,0:T(8,128)}), f32[8,8,128]{2,1,0:T(8,128)S(1)}, u32[]{:S(2)}, u32[]{:S(2)}) async-start(f32[8,8,128]{2,1,0:T(8,128)} %broadcast_in_dim.54), calls=%async_computation.6 | async-start | bytes 65536 | tf_op jit(solution)/shard_map/all_to_all | solution.py:22
  168.7 0.2 fusion.4
  168.8 0.1 copy.63
  169.0 0.7 copy.65
  169.7 4.0 %all-to-all-done.6 = f32[8,8,128]{2,1,0:T(8,128)S(1)} async-done(((f32[8,8,128]{2,1,0:T(8,128)}), f32[8,8,128]{2,1,0:T(8,128)S(1)}, u32[]{:S(2)}, u32[]{:S(2)}) %all-to-all-start.6) | async-done | bytes 32800 | tf_op jit(solution)/shard_map/all_to_all | solution.py:22
  173.7 10.2 %all-to-all-start.5 = ((bf16[64,8,80]{2,1,0:T(8,128)(2,1)}), bf16[64,8,80]{2,1,0:T(8,128)(2,1)S(1)}, u32[]{:S(2)}, u32[]{:S(2)}) async-start(bf16[64,8,80]{2,1,0:T(8,128)(2,1)} %copy.65), calls=%async_computation.5 | async-start | bytes 262144 | tf_op jit(solution)/shard_map/all_to_all | solution.py:22
  183.9 0.6 slice_reduce_fusion.1
  185.3 3.1 %fusion.17 = (f32[1,40,5120]{2,1,0:T(8,128)}, bf16[1,40,5120]{2,1,0:T(8,128)(2,1)}, f32[1,40,5120]{2,1,0:T(8,128)}) fusion(f32[40,5120]{1,0:T(8,128)S(1)} %copy-done.3, f32[]{:T(128)S(6)} %min.3, f32[1,40,5120]{2,1,0:T(8,128)S(1)} %copy-done.5, f32[1,40,5120]{2,1,0:T(8,128)} %param.14, bf16[1,40,5120]{2,1,0:T(8,128)(2,1)S(1)} %copy-done.2), kind=kLoop, calls=%fused_computation.35 | loop fusion | flops 3276800 | bytes 4915204 | tf_op jit(solution)/shard_map/broadcast_in_dim | solution.py:124
  188.3 8.2 %all-to-all-done.5 = bf16[64,8,80]{2,1,0:T(8,128)(2,1)S(1)} async-done(((bf16[64,8,80]{2,1,0:T(8,128)(2,1)}), bf16[64,8,80]{2,1,0:T(8,128)(2,1)S(1)}, u32[]{:S(2)}, u32[]{:S(2)}) %all-to-all-start.5) | async-done | bytes 81952 | tf_op jit(solution)/shard_map/all_to_all | solution.py:22
  196.5 0.8 squeeze.25
  197.3 0.8 squeeze.26
  (34 shorter events, 0.3 us)
Async XLA Ops:
  7.2 33.2 %copy-start = (bf16[1,80,2560]{2,1,0:T(8,128)(2,1)S(1)}, bf16[1,80,2560]{2,1,0:T(8,128)(2,1)}, u32[]{:S(2)}) copy-start(bf16[1,80,2560]{2,1,0:T(8,128)(2,1)} %param.13) | copy-start | bytes 1228804
  9.8 30.2 %all-to-all-start = ((bf16[64,8,80]{2,1,0:T(8,128)(2,1)}), bf16[64,8,80]{2,1,0:T(8,128)(2,1)S(1)}, u32[]{:S(2)}, u32[]{:S(2)}) async-start(bf16[64,8,80]{2,1,0:T(8,128)(2,1)} %copy.55), calls=%async_computation | async-start | bytes 262144 | tf_op jit(solution)/shard_map/all_to_all | solution.py:22
  27.5 68.3 %all-gather.4.cloned.1.call-start = ((), (), s32[]{:S(2)}) async-start(), calls=%async_computation.7 | async-start | bytes 1966080 | tf_op jit(solution)/shard_map/all_gather | solution.py:79
  45.8 33.8 %copy-start.6 = (bf16[1,5120]{1,0:T(2,128)(2,1)S(1)}, bf16[1,5120]{1,0:T(2,128)(2,1)}, u32[]{:S(2)}) copy-start(bf16[1,5120]{1,0:T(2,128)(2,1)} %param.11) | copy-start | bytes 30724
  45.8 34.0 %copy-start.2 = (bf16[1,40,5120]{2,1,0:T(8,128)(2,1)S(1)}, bf16[1,40,5120]{2,1,0:T(8,128)(2,1)}, u32[]{:S(2)}) copy-start(bf16[1,40,5120]{2,1,0:T(8,128)(2,1)} %param.12) | copy-start | bytes 1228804
  95.7 2.1 %copy-start.1 = (bf16[32,160,128]{2,1,0:T(8,128)(2,1)S(1)}, bf16[32,160,128]{2,1,0:T(8,128)(2,1)}, u32[]{:S(2)}) copy-start(bf16[32,160,128]{2,1,0:T(8,128)(2,1)} %all-gather.4.cloned.1.call-done) | copy-start | bytes 3932164
  108.2 1.1 copy-start.4
  110.4 41.8 %all-to-all-start.4 = ((bf16[32,128,128]{2,1,0:T(8,128)(2,1)}), bf16[32,128,128]{2,1,0:T(8,128)(2,1)S(1)}, u32[]{:S(2)}, u32[]{:S(2)}) async-start(bf16[32,128,128]{2,1,0:T(8,128)(2,1)} %pad_maximum_fusion), calls=%async_computation.4 | async-start | bytes 2097152 | tf_op jit(solution)/shard_map/all_to_all | solution.py:22
  152.2 4.3 %copy-start.7 = (f32[80]{0:T(128)S(1)}, f32[80]{0:T(128)}, u32[]{:S(2)}) copy-start(f32[80]{0:T(128)} %bitcast_convert_fusion) | copy-start | bytes 964
  156.2 29.0 %copy-start.3 = (f32[40,5120]{1,0:T(8,128)S(1)}, f32[40,5120]{1,0:T(8,128)}, u32[]{:S(2)}) copy-start(f32[40,5120]{1,0:T(8,128)} %get-tuple-element.20) | copy-start | bytes 2457604
  156.2 29.0 %copy-start.5 = (f32[1,40,5120]{2,1,0:T(8,128)S(1)}, f32[1,40,5120]{2,1,0:T(8,128)}, u32[]{:S(2)}) copy-start(f32[1,40,5120]{2,1,0:T(8,128)} %param.15) | copy-start | bytes 2457604
  156.6 12.1 %collective-permute-start.1 = (bf16[80,128]{1,0:T(8,128)(2,1)S(1)}, bf16[80,128]{1,0:T(8,128)(2,1)S(1)}, u32[]{:S(2)}, u32[]{:S(2)}) collective-permute-start(bf16[80,128]{1,0:T(8,128)(2,1)S(1)} %fusion.28), channel_id=1, source_target_pairs={{0,448},{64,0},{128,64},{192,128},{256,192},{320,256},{384,320},{4... | collective-permute-start | bytes 61448 | tf_op jit(solution)/shard_map/ppermute | solution.py:27
  159.5 9.2 %collective-permute-start = (bf16[80,128]{1,0:T(8,128)(2,1)S(1)}, bf16[80,128]{1,0:T(8,128)(2,1)S(1)}, u32[]{:S(2)}, u32[]{:S(2)}) collective-permute-start(bf16[80,128]{1,0:T(8,128)(2,1)S(1)} %fusion.6), channel_id=1, source_target_pairs={{0,64},{64,128},{128,192},{192,256},{256,320},{320,384},{384,448},... | collective-permute-start | bytes 61448 | tf_op jit(solution)/shard_map/ppermute | solution.py:27
  162.9 10.9 %all-to-all-start.6 = ((f32[8,8,128]{2,1,0:T(8,128)}), f32[8,8,128]{2,1,0:T(8,128)S(1)}, u32[]{:S(2)}, u32[]{:S(2)}) async-start(f32[8,8,128]{2,1,0:T(8,128)} %broadcast_in_dim.54), calls=%async_computation.6 | async-start | bytes 65536 | tf_op jit(solution)/shard_map/all_to_all | solution.py:22
  173.7 22.7 %all-to-all-start.5 = ((bf16[64,8,80]{2,1,0:T(8,128)(2,1)}), bf16[64,8,80]{2,1,0:T(8,128)(2,1)S(1)}, u32[]{:S(2)}, u32[]{:S(2)}) async-start(bf16[64,8,80]{2,1,0:T(8,128)(2,1)} %copy.65), calls=%async_computation.5 | async-start | bytes 262144 | tf_op jit(solution)/shard_map/all_to_all | solution.py:22
Sparse Core Ops, SparseCore 0:
  79.7 15.9 all-gather.3

commit v2 on v1

--- a/solution.py
+++ b/solution.py
@@ -1,6 +1,10 @@
+import functools
+
 import jax
 import jax.numpy as jnp
 from jax import lax
+from jax.experimental import pallas as pl
+from jax.experimental.pallas import tpu as pltpu
 from jax.sharding import Mesh, PartitionSpec as P
 
 NORM_EPS = 1e-05
@@ -31,13 +35,6 @@
     return jnp.broadcast_to(block[None], (count,) + block.shape)
 
 
-def three_parts(values):
-    high = lax.reduce_precision(values, 8, 7)
-    rest = values - high
-    middle = lax.reduce_precision(rest, 8, 7)
-    return [part.astype(jnp.bfloat16) for part in (high, middle, rest - middle)]
-
-
 def selection(placed, capacity, micro_rows):
     count = placed.shape[0]
     ids = jnp.arange(count, dtype=jnp.int32)
@@ -46,6 +43,107 @@
     rows = (slots[:, None] * micro_rows + jnp.arange(micro_rows, dtype=jnp.int32)).reshape(-1)
     every = jnp.arange(count * capacity * micro_rows, dtype=jnp.int32)
     return (every[:, None] == rows[None, :]).astype(jnp.bfloat16)
+
+
+def on_core(kernel, out_shape, scalars, arrays, scratch=(), flops=0):
+    size = sum(a.size * a.dtype.itemsize for a in arrays)
+    size += sum(o.size * o.dtype.itemsize for o in out_shape)
+    return pl.pallas_call(
+        kernel,
+        out_shape=out_shape,
+        in_specs=[pl.BlockSpec(memory_space=pltpu.SMEM)] * len(scalars)
+        + [pl.BlockSpec(memory_space=pltpu.VMEM)] * len(arrays),
+        out_specs=[pl.BlockSpec(memory_space=pltpu.VMEM)] * len(out_shape),
+        scratch_shapes=list(scratch),
+        compiler_params=pltpu.CompilerParams(vmem_limit_bytes=24 * 2**20),
+        cost_estimate=pl.CostEstimate(flops=flops, bytes_accessed=size, transcendentals=0),
+    )(*scalars, *arrays)
+
+
+def dnormed_kernel(width, heads, core_ref, trip_ref, weight_ref, grads_ref, mine_ref, other_ref):
+    chips = trip_ref.shape[0]
+    total = trip_ref[0, width : width + heads, :].astype(jnp.float32)
+    for chip in range(1, chips):
+        total += trip_ref[chip, width : width + heads, :].astype(jnp.float32)
+    grads = total.astype(jnp.bfloat16)
+    grads_ref[...] = grads
+    first_core = core_ref[0] == 0
+    group = 4
+    span = group * 2 * width
+    for step in range(chips // group):
+        part = lax.dot_general(
+            weight_ref[:, step * span : (step + 1) * span],
+            grads,
+            (((0,), (0,)), ((), ())),
+            preferred_element_type=jnp.float32,
+        )
+        for local in range(group):
+            low = part[2 * local * width : (2 * local + 1) * width]
+            high = part[(2 * local + 1) * width : (2 * local + 2) * width]
+            chip = step * group + local
+            mine_ref[chip] = jnp.where(first_core, low, high).astype(jnp.bfloat16)
+            other_ref[chip] = jnp.where(first_core, high, low).astype(jnp.bfloat16)
+
+
+def parts_of(values):
+    high = values.astype(jnp.bfloat16).astype(jnp.float32)
+    middle = (values - high).astype(jnp.bfloat16).astype(jnp.float32)
+    return [high, middle, values - high - middle]
+
+
+def values_kernel(
+    width, heads, core_ref, mine_ref, other_ref, gain_ref, weight_ref, grads_ref,
+    own_ref, gradient_ref, inverse_ref, normed_ref,
+):
+    chips = mine_ref.shape[0]
+    model = 2 * chips * width
+    squares = jnp.zeros((width, mine_ref.shape[2]), jnp.float32)
+    for chip in range(chips):
+        for ref in (mine_ref, other_ref):
+            block = ref[chip, :width, :].astype(jnp.float32)
+            squares += block * block
+    mean = jnp.sum(squares, axis=0, keepdims=True) / model
+    inverse = lax.rsqrt(mean + NORM_EPS)
+    inverse_ref[...] = jnp.broadcast_to(inverse, inverse_ref.shape)
+    first_core = core_ref[0] == 0
+    for chip in range(chips):
+        mine, other = mine_ref[chip, :width, :], other_ref[chip, :width, :]
+        for core, block in ((0, jnp.where(first_core, mine, other)), (1, jnp.where(first_core, other, mine))):
+            at = (2 * chip + core) * width
+            unit = block.astype(jnp.float32) * inverse
+            scaled = unit * gain_ref[at : at + width, :].astype(jnp.float32)
+            normed_ref[at : at + width, :] = scaled.astype(jnp.bfloat16)
+    values = jnp.dot(weight_ref[...], normed_ref[...], preferred_element_type=jnp.float32)
+    grads = grads_ref[...]
+    span = 8 * width
+    lanes = mine_ref.shape[2]
+    norms = jnp.zeros((heads, lanes), jnp.float32)
+    for step in range(model // span):
+        block = lax.dot_general(
+            grads,
+            normed_ref[step * span : (step + 1) * span, :],
+            (((1,), (1,)), ((), ())),
+            preferred_element_type=jnp.float32,
+        )
+        gradient_ref[:, step * span : (step + 1) * span] = block
+        for lane in range(span // lanes):
+            piece = block[:, lane * lanes : (lane + 1) * lanes]
+            norms += piece * piece
+    inner = jnp.sum(grads.astype(jnp.float32) * values, axis=0, keepdims=True)
+    norm = jnp.sum(norms, axis=0, keepdims=True)
+    line = lax.broadcasted_iota(jnp.int32, (SPARE, values.shape[1]), 0)
+    extra = jnp.zeros((SPARE, values.shape[1]), jnp.float32)
+    for index, part in enumerate(parts_of(inner) + parts_of(norm)):
+        extra = jnp.where(line == index, part, extra)
+    own_ref[...] = jnp.concatenate([values, extra], axis=0).astype(jnp.bfloat16)
+
+
+def payload_kernel(width, mine_ref, arrived_ref, own_ref, out_ref):
+    own = own_ref[...]
+    for chip in range(mine_ref.shape[0]):
+        block = mine_ref[chip].astype(jnp.float32) + arrived_ref[chip].astype(jnp.float32)
+        out_ref[chip, :width, :] = block.astype(jnp.bfloat16)
+        out_ref[chip, width:, :] = own
 
 
 def body(placing, acts, cotan, gain, w_value, w_out, moment_one, moment_two):
@@ -67,6 +165,7 @@
     placed = lax.dynamic_index_in_dim(placing[:, :, 0], section_now, 0, keepdims=False)
     select = selection(placed, capacity, micro_rows)
     gain_col = jnp.broadcast_to(gain[0][:, None], (model, rows))
+    own_gain = lax.dynamic_slice_in_dim(gain_col, peer_now * width, width, 0)
     cols = cols.reshape(peers, 2, slot_rows, width).transpose(1, 0, 2, 3)
     stacked = matmul("ksf,sr->kfr", cols.reshape(2, peers * slot_rows, width), select)
     stream, cotangent = stacked[0].astype(jnp.bfloat16), stacked[1].astype(jnp.bfloat16)
@@ -75,38 +174,57 @@
     grads = swap(grads.reshape(chips, 2, heads, rows).transpose(1, 0, 2, 3), "core")
     grads = jnp.sum(grads.astype(jnp.float32), axis=0).astype(jnp.bfloat16)
     first_trip = swap(jnp.concatenate([to_all(stream, chips), grads], axis=1), "chip")
-    value_grads = jnp.sum(first_trip[:, width:].astype(jnp.float32), axis=0).astype(jnp.bfloat16)
-    streams = lax.all_gather(first_trip[:, :width], "core", axis=1).reshape(model, rows)
-
-    inputs = streams.astype(jnp.float32)
-    inverse_rms = lax.rsqrt(jnp.mean(inputs * inputs, axis=0, keepdims=True) + NORM_EPS)
-    normed = (inputs * inverse_rms * gain_col.astype(jnp.float32)).astype(jnp.bfloat16)
-    values = matmul("hd,dr->hr", weights, normed)
-    norm_grads = matmul("hd,hr->dr", weights, value_grads).astype(jnp.bfloat16)
-    norm_grads = swap(norm_grads.reshape(chips, 2, width, rows).transpose(1, 0, 2, 3), "core")
-    norm_grads = jnp.sum(norm_grads.astype(jnp.float32), axis=0).astype(jnp.bfloat16)
-    gradient = matmul("hr,dr->hd", value_grads, normed)
-
-    inner = jnp.sum(value_grads.astype(jnp.float32) * values, axis=0)
-    square = jnp.broadcast_to(jnp.sum(gradient * gradient), inner.shape)
-    extra = jnp.stack(three_parts(inner) + three_parts(square))
-    extra = jnp.pad(extra, ((0, SPARE - extra.shape[0]), (0, 0)))
-    own = jnp.concatenate([values.astype(jnp.bfloat16), extra])
-    second_trip = swap(jnp.concatenate([norm_grads, to_all(own, chips)], axis=1), "chip")
+    core = lax.axis_index("core").astype(jnp.int32).reshape(1)
+    other_trip = moved(first_trip, "core", 1)
+    brief, full = jnp.bfloat16, jnp.float32
+    half = jax.ShapeDtypeStruct((chips, width, rows), brief)
+    value_grads, mine, other = on_core(
+        functools.partial(dnormed_kernel, width, heads),
+        [jax.ShapeDtypeStruct((heads, rows), brief), half, half],
+        [core],
+        [first_trip, weights],
+        flops=2 * model * heads * rows,
+    )
+    arrived = moved(other, "core", 1)
+    own, gradient, inverse = on_core(
+        functools.partial(values_kernel, width, heads),
+        [
+            jax.ShapeDtypeStruct((heads + SPARE, rows), brief),
+            jax.ShapeDtypeStruct((heads, model), full),
+            jax.ShapeDtypeStruct((SPARE, rows), full),
+        ],
+        [core],
+        [first_trip, other_trip, gain_col, weights, value_grads],
+        [pltpu.VMEM((model, rows), brief)],
+        flops=4 * model * heads * rows,
+    )
+    (payload,) = on_core(
+        functools.partial(payload_kernel, width),
+        [jax.ShapeDtypeStruct((chips, width + heads + SPARE, rows), brief)],
+        [],
+        [mine, arrived, own],
+    )
+    inverse_rms = inverse[:1]
+    payload, own_gain, inverse_rms = lax.optimization_barrier((payload, own_gain, inverse_rms))
+    second_trip = swap(payload, "chip")
     norm_grads = jnp.sum(second_trip[:, :width].astype(jnp.float32), axis=0)
     gathered = lax.all_gather(second_trip[:, width:], "core", axis=1)
     extra = jnp.sum(gathered[:, :, heads:].astype(jnp.float32), axis=(0, 1))
     inner = jnp.sum(extra[0:3], axis=0, keepdims=True) / model
-    square = jnp.sum(extra[3:6], axis=0)
-    squares = swap(jnp.broadcast_to(square, (lax.axis_size("section"), SPARE, rows)), "section")
-    totals = jnp.sum(squares[:, 0, 0])
+    square = jnp.sum(extra[3:6], axis=0, keepdims=True)
+    sections = lax.axis_size("section")
+    distance = 1
+    while distance < sections:
+        route = [(i, i ^ distance) for i in range(sections)]
+        square = square + lax.ppermute(square, "section", route)
+        distance *= 2
+    totals = jnp.sum(square)
 
     mixed = matmul("fh,hr->fr", out_weights, gathered[:, :, :heads].reshape(-1, rows))
     outputs = (stream.astype(jnp.float32) + mixed).astype(jnp.bfloat16)
-    own_gain = lax.dynamic_slice_in_dim(gain_col, peer_now * width, width, 0).astype(jnp.float32)
     unit = stream.astype(jnp.float32) * inverse_rms
     back = (
-        cotangent.astype(jnp.float32) + inverse_rms * (norm_grads * own_gain - unit * inner)
+        cotangent.astype(jnp.float32) + inverse_rms * (norm_grads * own_gain.astype(jnp.float32) - unit * inner)
     ).astype(jnp.bfloat16)
     arrived = jnp.stack([moved(outputs, "section", 1), moved(back, "section", -1)])
 

time: 206 us -> 175 us (0.85)
  waiting for transfers between devices: 58.9 us -> 25.7 us
  blocking collectives: 47.6 us -> 78 us
  between operations: 20.1 us -> 1.74 us
  other arithmetic: 14 us -> 3.87 us
  Pallas kernels: 0 us -> 4.68 us
  matrix products: 4.24 us -> 0.99 us
    all_to_all x3, blocking collectives: 43.6 us -> 75.4 us  [swap(): return lax.all_to_all(blocks, axis, split_axis=0, concat_axis=0, tiled=True)]
    all_to_all x4 -> x2, waiting for transfers between devices: 52.1 us -> 21.5 us  [swap(): return lax.all_to_all(blocks, axis, split_axis=0, concat_axis=0, tiled=True)]
    all_to_all x4 -> x2, starting transfers between devices: 45 us -> 28.3 us  [swap(): return lax.all_to_all(blocks, axis, split_axis=0, concat_axis=0, tiled=True)]
    ppermute x0 -> x3, starting transfers between devices: none -> 12 us  [body(): square = square + lax.ppermute(square, 'section', route)]
    all_gather x1 -> x0, waiting for transfers between devices: 6.79 us -> none  [body(): lax.all_gather(first_trip[:, :width], 'core', axis=1).reshape(model, rows)]
    ppermute x2 -> x4, starting transfers between devices: 5.41 us -> 10.2 us  [moved(): lax.ppermute(block, axis, [(i, (i + distance) % count) for i in range(cou...]
    pallas_call x0 -> x3, Pallas kernels: none -> 4.68 us  [on_core(): pl.pallas_call(kernel, out_shape=out_shape, in_specs=[pl.BlockSpec(memory...]
    convert_element_type x6 -> x0, other arithmetic: 4.41 us -> none  [the longest x2 3.05 us: body(): (inputs * inverse_rms * gain_col.astype(jnp.float32)).astype(jnp.bfloat16)]
  transfers between devices with their start and end apart: 7 -> 9, of which waited for: 5 -> 4; matrix products, arithmetic and copies ran while one was open for 6% -> 4% of each run, Pallas kernels for 0% -> 2%
where the time goes in v2:
time: 175 us
  blocking collectives  78 us (45%)
  starting transfers between devices  50.5 us (29%)
  waiting for transfers between devices  25.7 us (15%)
  local copies, waits for them, and re-layouts  9.25 us (5%)
  Pallas kernels  4.68 us (3%)
  other arithmetic  3.87 us (2%)
    all_to_all x3, blocking collectives, swap(): return lax.all_to_all(blocks, axis, split_axis=0, concat_axis=0, tiled=True)  75.4 us
    all_to_all x2, starting transfers between devices, swap(): return lax.all_to_all(blocks, axis, split_axis=0, concat_axis=0, tiled=True)  28.3 us
    all_to_all x2, waiting for transfers between devices, swap(): return lax.all_to_all(blocks, axis, split_axis=0, concat_axis=0, tiled=True)  21.5 us
    ppermute x3, starting transfers between devices, body(): square = square + lax.ppermute(square, 'section', route)  12 us
    ppermute x4, starting transfers between devices, moved(): lax.ppermute(block, axis, [(i, (i + distance) % count) for i in range(cou...  10.2 us
    pallas_call x3, Pallas kernels, on_core(): pl.pallas_call(kernel, out_shape=out_shape, in_specs=[pl.BlockSpec(memory...  4.68 us
  transfers between devices with their start and end apart: 9, of which 4 were waited for; matrix products, arithmetic and copies ran while one was open for 4% of the time, Pallas kernels for 2%

profile of v2, /device:TPU:1, one launch (start us, length us, event | category | flops | bytes accessed | tf_op | source)
XLA Modules:
  0.0 174.8 jit_solution(11012067568331919839)
XLA Ops:
  0.6 0.0 copy-start
  0.6 1.0 concatenate.12
  1.6 0.9 concatenate.11
  2.6 0.7 copy.37
  3.3 17.6 %all-to-all-start = ((bf16[64,8,80]{2,1,0:T(8,128)(2,1)}), bf16[64,8,80]{2,1,0:T(8,128)(2,1)S(1)}, u32[]{:S(2)}, u32[]{:S(2)}) async-start(bf16[64,8,80]{2,1,0:T(8,128)(2,1)} %copy.37), calls=%async_computation | async-start | bytes 262144 | tf_op jit(solution)/shard_map/all_to_all | solution.py:26
  20.9 0.7 dynamic-slice_bitcast_fusion.1
  21.6 0.1 convert_reduce_fusion.2
  21.7 0.7 add_multiply_fusion
  22.4 0.1 iota_add_fusion
  22.4 0.1 add.75
  22.6 10.9 %all-to-all-done = bf16[64,8,80]{2,1,0:T(8,128)(2,1)S(1)} async-done(((bf16[64,8,80]{2,1,0:T(8,128)(2,1)}), bf16[64,8,80]{2,1,0:T(8,128)(2,1)S(1)}, u32[]{:S(2)}, u32[]{:S(2)}) %all-to-all-start) | async-done | bytes 81952 | tf_op jit(solution)/shard_map/all_to_all | solution.py:26
  33.5 0.1 copy.39
  33.6 0.2 fusion.15
  33.8 0.0 copy-done
  33.9 0.3 fusion
  34.2 0.3 copy.41
  34.5 0.1 copy.42
  34.6 4.4 %all_to_all.25 = bf16[2,32,40,128]{3,2,1,0:T(8,128)(2,1)S(1)} all-to-all(bf16[2,32,40,128]{3,2,1,0:T(8,128)(2,1)S(1)} %copy.42), channel_id=1, replica_groups=mesh['section'=8,'chip'=32,'core'=2] {'core'}, dimensions={0} | all-to-all | bytes 1310720 | tf_op jit(solution)/shard_map/all_to_all | solution.py:26
  39.0 0.1 reduce_sum.67
  39.1 0.1 broadcast_in_dim.16
  39.2 0.1 pad_maximum_fusion
  39.3 0.0 copy-start.1
  39.3 0.0 copy-start.6
  39.3 32.8 %all_to_all.26.trip_ref.mine_ref = bf16[32,120,128]{2,1,0:T(8,128)(2,1)S(1)} all-to-all(bf16[32,120,128]{2,1,0:T(8,128)(2,1)S(1)} %pad_maximum_fusion), channel_id=1, replica_groups=mesh['section'=8,'chip'=32,'core'=2] {'chip'}, dimensions={0} | all-to-all | bytes 1966080 | tf_op jit(solution)/shard_map/all_to_all | solution.py:26
  72.1 3.9 %collective-permute-start.1 = (bf16[32,120,128]{2,1,0:T(8,128)(2,1)S(1)}, bf16[32,120,128]{2,1,0:T(8,128)(2,1)S(1)}, u32[]{:S(2)}, u32[]{:S(2)}) collective-permute-start(bf16[32,120,128]{2,1,0:T(8,128)(2,1)S(1)} %all_to_all.26.trip_ref.mine_ref), channel_id=1, source_target_pairs={{0,1},{1,0},{2,3},{3,2},{4,5},{5,4},{6,7},{7,6},{8,9},{9,8},{10,11... | collective-permute-start | bytes 2949128 | tf_op jit(solution)/shard_map/ppermute | solution.py:31
  76.1 1.4 shard_map.119
  77.5 1.9 %collective-permute-start = (bf16[32,80,128]{2,1,0:T(8,128)(2,1)}, bf16[32,80,128]{2,1,0:T(8,128)(2,1)}, u32[]{:S(2)}, u32[]{:S(2)}) collective-permute-start(bf16[32,80,128]{2,1,0:T(8,128)(2,1)} %get-tuple-element.15), channel_id=1, source_target_pairs={{0,1},{1,0},{2,3},{3,2},{4,5},{5,4},{6,7},{7,6},{8,9},{9,8},{10,11... | collective-permute-start | bytes 1966088 | tf_op jit(solution)/shard_map/ppermute | solution.py:31
  79.4 0.1 reduce.1
  79.5 0.1 dynamic-slice_bitcast_fusion
  79.6 0.0 collective-permute-done.1.other_ref
  79.6 2.5 %broadcast_in_dim.18.gain_ref = bf16[5120,128]{1,0:T(8,128)(2,1)S(1)} broadcast(bf16[5120]{0:T(1024)(128)(2,1)S(1)} %reduce.1), dimensions={0} | broadcast | bytes 1320960 | tf_op jit(solution)/shard_map/broadcast_in_dim | solution.py:167
  82.1 1.7 shard_map.120
  83.7 0.0 copy-start.2
  83.7 0.0 collective-permute-done.arrived_ref
  83.8 1.6 shard_map.121
  85.4 0.1 broadcast_in_dim.38
  85.4 38.2 %all_to_all.27 = bf16[32,128,128]{2,1,0:T(8,128)(2,1)S(1)} all-to-all(bf16[32,128,128]{2,1,0:T(8,128)(2,1)S(1)} %shard_map.121), channel_id=1, replica_groups=mesh['section'=8,'chip'=32,'core'=2] {'chip'}, dimensions={0} | all-to-all | bytes 2097152 | tf_op jit(solution)/shard_map/all_to_all | solution.py:26
  123.7 2.6 %all-gather = bf16[32,96,128]{2,1,0:T(8,128)(2,1)S(1)} all-gather(bf16[32,48,128]{2,1,0:T(8,128)(2,1)S(1)} %slice.48), channel_id=2, replica_groups=mesh['section'=8,'chip'=32,'core'=2] {'core'}, dimensions={1}, use_global_device_ids=true | all-gather | bytes 1179648 | tf_op jit(solution)/shard_map/all_gather | solution.py:211
  126.3 0.1 convert_reduce_fusion.1
  126.4 3.6 %collective-permute-start.4 = (f32[1,128]{1,0:T(1,128)S(1)}, f32[1,128]{1,0:T(1,128)S(1)}, u32[]{:S(2)}, u32[]{:S(2)}) collective-permute-start(f32[1,128]{1,0:T(1,128)S(1)} %bitcast.94), channel_id=1, source_target_pairs={{0,64},{64,0},{128,192},{192,128},{256,320},{320,256},{384,448},{4... | collective-permute-start | bytes 1544 | tf_op jit(solution)/shard_map/ppermute | solution.py:219
  130.0 0.1 convert_reduce_fusion
  130.1 0.8 collective-permute-done.4
  130.9 5.5 %collective-permute-start.5 = (f32[1,128]{1,0:T(1,128)S(1)}, f32[1,128]{1,0:T(1,128)S(1)}, u32[]{:S(2)}, u32[]{:S(2)}) collective-permute-start(f32[1,128]{1,0:T(1,128)S(1)} %bitcast_add_fusion.1), channel_id=1, source_target_pairs={{0,128},{64,192},{128,0},{192,64},{256,384},{320,448},{384,256},{4... | collective-permute-start | bytes 1544 | tf_op jit(solution)/shard_map/ppermute | solution.py:219
  136.4 0.0 copy-start.5
  136.4 0.1 slice.49
  136.5 0.0 copy-start.3
  136.5 0.0 copy-start.4
  136.5 2.4 %collective-permute-start.3 = (bf16[80,128]{1,0:T(8,128)(2,1)S(1)}, bf16[80,128]{1,0:T(8,128)(2,1)S(1)}, u32[]{:S(2)}, u32[]{:S(2)}) collective-permute-start(bf16[80,128]{1,0:T(8,128)(2,1)S(1)} %fusion.23), channel_id=1, source_target_pairs={{0,448},{64,0},{128,64},{192,128},{256,192},{320,256},{384,320},{4... | collective-permute-start | bytes 61448 | tf_op jit(solution)/shard_map/ppermute | solution.py:31
  138.9 0.0 collective-permute-done.5
  139.0 3.0 %collective-permute-start.6 = (f32[1,128]{1,0:T(1,128)S(1)}, f32[1,128]{1,0:T(1,128)S(1)}, u32[]{:S(2)}, u32[]{:S(2)}) collective-permute-start(f32[1,128]{1,0:T(1,128)S(1)} %add.81), channel_id=1, source_target_pairs={{0,256},{64,320},{128,384},{192,448},{256,0},{320,64},{384,128},{4... | collective-permute-start | bytes 1544 | tf_op jit(solution)/shard_map/ppermute | solution.py:219
  142.0 0.3 fusion.3
  142.2 1.9 %collective-permute-start.2 = (bf16[80,128]{1,0:T(8,128)(2,1)S(1)}, bf16[80,128]{1,0:T(8,128)(2,1)S(1)}, u32[]{:S(2)}, u32[]{:S(2)}) collective-permute-start(bf16[80,128]{1,0:T(8,128)(2,1)S(1)} %fusion.3), channel_id=1, source_target_pairs={{0,64},{64,128},{128,192},{192,256},{256,320},{320,384},{384,448},... | collective-permute-start | bytes 61448 | tf_op jit(solution)/shard_map/ppermute | solution.py:31
  144.2 0.0 collective-permute-done.6
  144.2 0.6 add_reduce_fusion
  145.5 0.0 collective-permute-done.3
  145.5 3.4 %collective-permute-done.2 = bf16[80,128]{1,0:T(8,128)(2,1)S(1)} collective-permute-done((bf16[80,128]{1,0:T(8,128)(2,1)S(1)}, bf16[80,128]{1,0:T(8,128)(2,1)S(1)}, u32[]{:S(2)}, u32[]{:S(2)}) %collective-permute-start.2) | collective-permute-done | bytes 20512 | tf_op jit(solution)/shard_map/ppermute | solution.py:31
  148.9 0.2 fusion.1
  149.0 0.1 copy.43
  149.2 0.7 copy.45
  149.9 10.7 %all-to-all-start.4 = ((bf16[64,8,80]{2,1,0:T(8,128)(2,1)}), bf16[64,8,80]{2,1,0:T(8,128)(2,1)S(1)}, u32[]{:S(2)}, u32[]{:S(2)}) async-start(bf16[64,8,80]{2,1,0:T(8,128)(2,1)} %copy.45), calls=%async_computation.4 | async-start | bytes 262144 | tf_op jit(solution)/shard_map/all_to_all | solution.py:26
  160.7 1.9 %fusion.12 = (f32[1,40,5120]{2,1,0:T(8,128)}, bf16[1,40,5120]{2,1,0:T(8,128)(2,1)}, f32[1,40,5120]{2,1,0:T(8,128)}) fusion(f32[40,5120]{1,0:T(8,128)S(1)} %copy-done.3, f32[]{:T(128)S(6)} %min.3, f32[1,40,5120]{2,1,0:T(8,128)S(1)} %copy-done.4, f32[1,40,5120]{2,1,0:T(8,128)S(1)} %copy-done.5, bf16[1,40,5120]{2,1,0:T(8,128)(2,1)S(1)} %copy-done.1), kind=kLoop, calls=%fused_computation.22 | loop fusion | flops 3276800 | bytes 4915204 | tf_op jit(solution)/shard_map/broadcast_in_dim | solution.py:242
  162.6 10.6 %all-to-all-done.4 = bf16[64,8,80]{2,1,0:T(8,128)(2,1)S(1)} async-done(((bf16[64,8,80]{2,1,0:T(8,128)(2,1)}), bf16[64,8,80]{2,1,0:T(8,128)(2,1)S(1)}, u32[]{:S(2)}, u32[]{:S(2)}) %all-to-all-start.4) | async-done | bytes 81952 | tf_op jit(solution)/shard_map/all_to_all | solution.py:26
  173.2 0.8 squeeze.24
  174.0 0.8 squeeze.25
  (20 shorter events, 0.3 us)
Async XLA Ops:
  0.6 33.2 %copy-start = (bf16[1,80,2560]{2,1,0:T(8,128)(2,1)S(1)}, bf16[1,80,2560]{2,1,0:T(8,128)(2,1)}, u32[]{:S(2)}) copy-start(bf16[1,80,2560]{2,1,0:T(8,128)(2,1)} %param.13) | copy-start | bytes 1228804
  3.3 30.2 %all-to-all-start = ((bf16[64,8,80]{2,1,0:T(8,128)(2,1)}), bf16[64,8,80]{2,1,0:T(8,128)(2,1)S(1)}, u32[]{:S(2)}, u32[]{:S(2)}) async-start(bf16[64,8,80]{2,1,0:T(8,128)(2,1)} %copy.37), calls=%async_computation | async-start | bytes 262144 | tf_op jit(solution)/shard_map/all_to_all | solution.py:26
  39.3 36.8 %copy-start.1 = (bf16[1,40,5120]{2,1,0:T(8,128)(2,1)S(1)}, bf16[1,40,5120]{2,1,0:T(8,128)(2,1)}, u32[]{:S(2)}) copy-start(bf16[1,40,5120]{2,1,0:T(8,128)(2,1)} %param.12) | copy-start | bytes 1228804
  39.3 40.1 %copy-start.6 = (bf16[1,5120]{1,0:T(2,128)(2,1)S(1)}, bf16[1,5120]{1,0:T(2,128)(2,1)}, u32[]{:S(2)}) copy-start(bf16[1,5120]{1,0:T(2,128)(2,1)} %param.11) | copy-start | bytes 30724
  72.1 7.4 %collective-permute-start.1 = (bf16[32,120,128]{2,1,0:T(8,128)(2,1)S(1)}, bf16[32,120,128]{2,1,0:T(8,128)(2,1)S(1)}, u32[]{:S(2)}, u32[]{:S(2)}) collective-permute-start(bf16[32,120,128]{2,1,0:T(8,128)(2,1)S(1)} %all_to_all.26.trip_ref.mine_ref), channel_id=1, source_target_pairs={{0,1},{1,0},{2,3},{3,2},{4,5},{5,4},{6,7},{7,6},{8,9},{9,8},{10,11... | collective-permute-start | bytes 2949128 | tf_op jit(solution)/shard_map/ppermute | solution.py:31
  77.5 6.3 %collective-permute-start = (bf16[32,80,128]{2,1,0:T(8,128)(2,1)}, bf16[32,80,128]{2,1,0:T(8,128)(2,1)}, u32[]{:S(2)}, u32[]{:S(2)}) collective-permute-start(bf16[32,80,128]{2,1,0:T(8,128)(2,1)} %get-tuple-element.15), channel_id=1, source_target_pairs={{0,1},{1,0},{2,3},{3,2},{4,5},{5,4},{6,7},{7,6},{8,9},{9,8},{10,11... | collective-permute-start | bytes 1966088 | tf_op jit(solution)/shard_map/ppermute | solution.py:31
  83.7 39.9 %copy-start.2 = (f32[40,5120]{1,0:T(8,128)}, f32[40,5120]{1,0:T(8,128)S(1)}, u32[]{:S(2)}) copy-start(f32[40,5120]{1,0:T(8,128)S(1)} %get-tuple-element.22) | copy-start | bytes 2457604
  126.4 4.5 %collective-permute-start.4 = (f32[1,128]{1,0:T(1,128)S(1)}, f32[1,128]{1,0:T(1,128)S(1)}, u32[]{:S(2)}, u32[]{:S(2)}) collective-permute-start(f32[1,128]{1,0:T(1,128)S(1)} %bitcast.94), channel_id=1, source_target_pairs={{0,64},{64,0},{128,192},{192,128},{256,320},{320,256},{384,448},{4... | collective-permute-start | bytes 1544 | tf_op jit(solution)/shard_map/ppermute | solution.py:219
  130.9 8.0 %collective-permute-start.5 = (f32[1,128]{1,0:T(1,128)S(1)}, f32[1,128]{1,0:T(1,128)S(1)}, u32[]{:S(2)}, u32[]{:S(2)}) collective-permute-start(f32[1,128]{1,0:T(1,128)S(1)} %bitcast_add_fusion.1), channel_id=1, source_target_pairs={{0,128},{64,192},{128,0},{192,64},{256,384},{320,448},{384,256},{4... | collective-permute-start | bytes 1544 | tf_op jit(solution)/shard_map/ppermute | solution.py:219
  136.4 24.2 %copy-start.5 = (f32[1,40,5120]{2,1,0:T(8,128)S(1)}, f32[1,40,5120]{2,1,0:T(8,128)}, u32[]{:S(2)}) copy-start(f32[1,40,5120]{2,1,0:T(8,128)} %param.14) | copy-start | bytes 2457604
  136.5 24.2 %copy-start.3 = (f32[40,5120]{1,0:T(8,128)S(1)}, f32[40,5120]{1,0:T(8,128)}, u32[]{:S(2)}) copy-start(f32[40,5120]{1,0:T(8,128)} %copy-done.2) | copy-start | bytes 2457604
  136.5 24.1 %copy-start.4 = (f32[1,40,5120]{2,1,0:T(8,128)S(1)}, f32[1,40,5120]{2,1,0:T(8,128)}, u32[]{:S(2)}) copy-start(f32[1,40,5120]{2,1,0:T(8,128)} %param.15) | copy-start | bytes 2457604
  136.5 9.0 %collective-permute-start.3 = (bf16[80,128]{1,0:T(8,128)(2,1)S(1)}, bf16[80,128]{1,0:T(8,128)(2,1)S(1)}, u32[]{:S(2)}, u32[]{:S(2)}) collective-permute-start(bf16[80,128]{1,0:T(8,128)(2,1)S(1)} %fusion.23), channel_id=1, source_target_pairs={{0,448},{64,0},{128,64},{192,128},{256,192},{320,256},{384,320},{4... | collective-permute-start | bytes 61448 | tf_op jit(solution)/shard_map/ppermute | solution.py:31
  139.0 5.2 %collective-permute-start.6 = (f32[1,128]{1,0:T(1,128)S(1)}, f32[1,128]{1,0:T(1,128)S(1)}, u32[]{:S(2)}, u32[]{:S(2)}) collective-permute-start(f32[1,128]{1,0:T(1,128)S(1)} %add.81), channel_id=1, source_target_pairs={{0,256},{64,320},{128,384},{192,448},{256,0},{320,64},{384,128},{4... | collective-permute-start | bytes 1544 | tf_op jit(solution)/shard_map/ppermute | solution.py:219
  142.2 6.6 %collective-permute-start.2 = (bf16[80,128]{1,0:T(8,128)(2,1)S(1)}, bf16[80,128]{1,0:T(8,128)(2,1)S(1)}, u32[]{:S(2)}, u32[]{:S(2)}) collective-permute-start(bf16[80,128]{1,0:T(8,128)(2,1)S(1)} %fusion.3), channel_id=1, source_target_pairs={{0,64},{64,128},{128,192},{192,256},{256,320},{320,384},{384,448},... | collective-permute-start | bytes 61448 | tf_op jit(solution)/shard_map/ppermute | solution.py:31
  149.9 23.2 %all-to-all-start.4 = ((bf16[64,8,80]{2,1,0:T(8,128)(2,1)}), bf16[64,8,80]{2,1,0:T(8,128)(2,1)S(1)}, u32[]{:S(2)}, u32[]{:S(2)}) async-start(bf16[64,8,80]{2,1,0:T(8,128)(2,1)} %copy.45), calls=%async_computation.4 | async-start | bytes 262144 | tf_op jit(solution)/shard_map/all_to_all | solution.py:26

commit v3 on v2

--- a/solution.py
+++ b/solution.py
@@ -85,9 +85,30 @@
             other_ref[chip] = jnp.where(first_core, high, low).astype(jnp.bfloat16)
 
 
+def split_kernel(acts_ref, cotan_ref, out_ref):
+    peers, _, width = out_ref.shape
+    _, _, capacity, _, _ = acts_ref.shape
+    held = [ref[0, 0, slot] for ref in (acts_ref, cotan_ref) for slot in range(capacity)]
+    held = jnp.concatenate([rows.astype(jnp.float32) for rows in held], axis=0)
+    for peer in range(peers):
+        out_ref[peer] = held[:, peer * width : (peer + 1) * width].astype(jnp.bfloat16)
+
+
+def join_kernel(trip_ref, passed_ref, returned_ref, rows_ref):
+    peers, _, width = trip_ref.shape
+    _, _, capacity, micro_rows, _ = passed_ref.shape
+    for peer in range(peers):
+        rows_ref[:, peer * width : (peer + 1) * width] = trip_ref[peer].astype(jnp.float32)
+    at = 0
+    for ref in (passed_ref, returned_ref):
+        for slot in range(capacity):
+            ref[0, 0, slot] = rows_ref[at : at + micro_rows, :].astype(jnp.bfloat16)
+            at += micro_rows
+
+
 def parts_of(values):
-    high = values.astype(jnp.bfloat16).astype(jnp.float32)
-    middle = (values - high).astype(jnp.bfloat16).astype(jnp.float32)
+    high = lax.reduce_precision(values, 8, 7)
+    middle = lax.reduce_precision(values - high, 8, 7)
     return [high, middle, values - high - middle]
 
 
@@ -158,14 +179,18 @@
     rows = peers * micro_rows
     weights, out_weights = w_value[0], w_out[0]
 
-    held = jnp.concatenate(
-        [acts[0, 0].reshape(slot_rows, model), cotan[0, 0].reshape(slot_rows, model)]
-    )
-    cols = swap(held.reshape(2 * slot_rows, peers, width).transpose(1, 0, 2), PEER)
+    (held,) = on_core(
+        split_kernel,
+        [jax.ShapeDtypeStruct((peers, 2 * slot_rows, width), jnp.bfloat16)],
+        [],
+        [acts, cotan],
+    )
+    cols = swap(held, PEER)
     placed = lax.dynamic_index_in_dim(placing[:, :, 0], section_now, 0, keepdims=False)
     select = selection(placed, capacity, micro_rows)
     gain_col = jnp.broadcast_to(gain[0][:, None], (model, rows))
     own_gain = lax.dynamic_slice_in_dim(gain_col, peer_now * width, width, 0)
+    cols, gain_col, own_gain = lax.optimization_barrier((cols, gain_col, own_gain))
     cols = cols.reshape(peers, 2, slot_rows, width).transpose(1, 0, 2, 3)
     stacked = matmul("ksf,sr->kfr", cols.reshape(2, peers * slot_rows, width), select)
     stream, cotangent = stacked[0].astype(jnp.bfloat16), stacked[1].astype(jnp.bfloat16)
@@ -205,33 +230,41 @@
         [mine, arrived, own],
     )
     inverse_rms = inverse[:1]
-    payload, own_gain, inverse_rms = lax.optimization_barrier((payload, own_gain, inverse_rms))
     second_trip = swap(payload, "chip")
     norm_grads = jnp.sum(second_trip[:, :width].astype(jnp.float32), axis=0)
     gathered = lax.all_gather(second_trip[:, width:], "core", axis=1)
     extra = jnp.sum(gathered[:, :, heads:].astype(jnp.float32), axis=(0, 1))
     inner = jnp.sum(extra[0:3], axis=0, keepdims=True) / model
     square = jnp.sum(extra[3:6], axis=0, keepdims=True)
-    sections = lax.axis_size("section")
-    distance = 1
-    while distance < sections:
-        route = [(i, i ^ distance) for i in range(sections)]
-        square = square + lax.ppermute(square, "section", route)
-        distance *= 2
-    totals = jnp.sum(square)
-
     mixed = matmul("fh,hr->fr", out_weights, gathered[:, :, :heads].reshape(-1, rows))
     outputs = (stream.astype(jnp.float32) + mixed).astype(jnp.bfloat16)
     unit = stream.astype(jnp.float32) * inverse_rms
     back = (
         cotangent.astype(jnp.float32) + inverse_rms * (norm_grads * own_gain.astype(jnp.float32) - unit * inner)
     ).astype(jnp.bfloat16)
-    arrived = jnp.stack([moved(outputs, "section", 1), moved(back, "section", -1)])
+
+    sections = lax.axis_size("section")
+    parts = jnp.concatenate(parts_of(square)).astype(jnp.bfloat16)
+    parts = jnp.pad(parts, ((0, SPARE - parts.shape[0]), (0, 0)))
+    ahead = jnp.arange(sections)[:, None, None] == (section_now + 1) % sections
+    both = jnp.where(ahead, jnp.concatenate([outputs, parts]), jnp.concatenate([back, parts]))
+    third_trip = swap(both, "section")
+    totals = jnp.sum(third_trip[:, width : width + 3].astype(jnp.float32))
+    behind = [(section_now + sections - 1) % sections, (section_now + 1) % sections]
+    arrived = jnp.stack(
+        [lax.dynamic_index_in_dim(third_trip, at, 0, keepdims=False)[:width] for at in behind]
+    )
 
     spread = matmul("sr,kfr->ksf", select, arrived).astype(jnp.bfloat16)
     spread = spread.reshape(2, peers, slot_rows, width).transpose(1, 0, 2, 3)
     final = swap(spread.reshape(peers, 2 * slot_rows, width), PEER)
-    final = final.transpose(1, 0, 2).reshape((2, 1, 1, capacity, micro_rows, model))
+    passed, returned = on_core(
+        join_kernel,
+        [jax.ShapeDtypeStruct(acts.shape, brief)] * 2,
+        [],
+        [final],
+        [pltpu.VMEM((2 * slot_rows, model), full)],
+    )
 
     clip_scale = jnp.minimum(1.0, CLIP_NORM / jnp.sqrt(totals + 1e-06))
     clipped = gradient * clip_scale
@@ -239,7 +272,7 @@
     second = BETA_TWO * moment_two[0] + (1.0 - BETA_TWO) * clipped * clipped
     wide = weights.astype(jnp.float32)
     updated = wide - LEARN_RATE * (first / (jnp.sqrt(second) + ADAM_EPS) + DECAY * wide)
-    return final[0], final[1], updated.astype(jnp.bfloat16)[None], first[None], second[None]
+    return passed, returned, updated.astype(jnp.bfloat16)[None], first[None], second[None]
 
 
 def solution(mesh):

time: 175 us -> 165 us (0.943)
  blocking collectives: 78 us -> 39.8 us
  waiting for transfers between devices: 25.7 us -> 58.2 us
  starting transfers between devices: 50.5 us -> 44.6 us
  other arithmetic: 3.87 us -> 6.74 us
  local copies, waits for them, and re-layouts: 9.25 us -> 7.19 us
    all_to_all x3 -> x2, blocking collectives: 75.4 us -> 37.2 us  [swap(): return lax.all_to_all(blocks, axis, split_axis=0, concat_axis=0, tiled=True)]
    all_to_all x2 -> x4, waiting for transfers between devices: 21.5 us -> 57.8 us  [swap(): return lax.all_to_all(blocks, axis, split_axis=0, concat_axis=0, tiled=True)]
    ppermute x3 -> x0, starting transfers between devices: 12 us -> none  [body(): square = square + lax.ppermute(square, 'section', route)]
    all_to_all x2 -> x4, starting transfers between devices: 28.3 us -> 38.8 us  [swap(): return lax.all_to_all(blocks, axis, split_axis=0, concat_axis=0, tiled=True)]
    ppermute x4 -> x2, starting transfers between devices: 10.2 us -> 5.86 us  [moved(): lax.ppermute(block, axis, [(i, (i + distance) % count) for i in range(cou...]
    ppermute x4 -> x2, waiting for transfers between devices: 3.4 us -> 0.39 us  [moved(): lax.ppermute(block, axis, [(i, (i + distance) % count) for i in range(cou...]
    concatenate x2 -> x0, local copies, waits for them, and re-layouts: 1.85 us -> none  [body(): jnp.concatenate([acts[0, 0].reshape(slot_rows, model), cotan[0, 0].reshap...]
    pallas_call x3 -> x5, Pallas kernels: 4.68 us -> 5.03 us  [on_core(): pl.pallas_call(kernel, out_shape=out_shape, in_specs=[pl.BlockSpec(memory...]
  transfers between devices with their start and end apart: 9 -> 6, of which waited for: 4 -> 5; matrix products, arithmetic and copies ran while one was open for 4% -> 4% of each run, Pallas kernels for 2% -> 1%
where the time goes in v3:
time: 165 us; the launch traced here: 164 us
  waiting for transfers between devices  58.2 us (35%)
  starting transfers between devices  44.6 us (27%)
  blocking collectives  39.8 us (24%)
  local copies, waits for them, and re-layouts  7.19 us (4%)
  other arithmetic  6.74 us (4%)
  Pallas kernels  5.03 us (3%)
    all_to_all x4, waiting for transfers between devices, swap(): return lax.all_to_all(blocks, axis, split_axis=0, concat_axis=0, tiled=True)  57.8 us
    all_to_all x4, starting transfers between devices, swap(): return lax.all_to_all(blocks, axis, split_axis=0, concat_axis=0, tiled=True)  38.8 us
    all_to_all x2, blocking collectives, swap(): return lax.all_to_all(blocks, axis, split_axis=0, concat_axis=0, tiled=True)  37.2 us
    ppermute x2, starting transfers between devices, moved(): lax.ppermute(block, axis, [(i, (i + distance) % count) for i in range(cou...  5.86 us
    pallas_call x5, Pallas kernels, on_core(): pl.pallas_call(kernel, out_shape=out_shape, in_specs=[pl.BlockSpec(memory...  5.03 us
    broadcast_in_dim x1, other arithmetic, body(): second[None]  3.3 us
  transfers between devices with their start and end apart: 6, of which 5 were waited for; matrix products, arithmetic and copies ran while one was open for 4% of the time, Pallas kernels for 1%

profile of v3, /device:TPU:1, one launch (start us, length us, event | category | flops | bytes accessed | tf_op | source)
XLA Modules:
  0.0 164.2 jit_solution(11740634581221465938)
XLA Ops:
  0.6 0.0 copy-start
  0.6 0.0 copy-start.2
  0.7 0.8 copy-done.2
  1.5 0.0 copy-start.3
  1.5 0.8 copy-done.3
  2.3 0.8 shard_map.119
  3.1 17.6 %all-to-all-start = ((bf16[64,8,80]{2,1,0:T(8,128)(2,1)}), bf16[64,8,80]{2,1,0:T(8,128)(2,1)S(1)}, u32[]{:S(2)}, u32[]{:S(2)}) async-start(bf16[64,8,80]{2,1,0:T(8,128)(2,1)} %shard_map.119), calls=%async_computation | async-start | bytes 262144 | tf_op jit(solution)/shard_map/all_to_all | solution.py:26
  20.7 0.7 fusion.38
  21.4 0.1 convert_reduce_fusion.2
  21.5 0.7 add_multiply_fusion
  22.1 0.1 iota_add_fusion
  22.2 0.1 add.95
  22.4 0.8 reduce.1
  23.1 0.8 fusion.37
  23.9 9.3 %all-to-all-done = bf16[64,8,80]{2,1,0:T(8,128)(2,1)S(1)} async-done(((bf16[64,8,80]{2,1,0:T(8,128)(2,1)}), bf16[64,8,80]{2,1,0:T(8,128)(2,1)S(1)}, u32[]{:S(2)}, u32[]{:S(2)}) %all-to-all-start) | async-done | bytes 81952 | tf_op jit(solution)/shard_map/all_to_all | solution.py:26
  33.2 0.1 broadcast_in_dim.53
  33.3 2.5 %broadcast_in_dim.52.gain_ref = bf16[5120,128]{1,0:T(8,128)(2,1)S(1)} broadcast(bf16[5120]{0:T(1024)(128)(2,1)S(1)} %reduce.1), dimensions={0} | broadcast | bytes 1320960 | tf_op jit(solution)/shard_map/broadcast_in_dim | solution.py:191
  35.9 0.2 fusion.15
  36.1 0.0 copy-done
  36.1 0.3 fusion
  36.5 0.3 copy.28
  36.8 0.1 copy.29
  36.9 4.4 %all_to_all.30 = bf16[2,32,40,128]{3,2,1,0:T(8,128)(2,1)S(1)} all-to-all(bf16[2,32,40,128]{3,2,1,0:T(8,128)(2,1)S(1)} %copy.29), channel_id=1, replica_groups=mesh['section'=8,'chip'=32,'core'=2] {'core'}, dimensions={0} | all-to-all | bytes 1310720 | tf_op jit(solution)/shard_map/all_to_all | solution.py:26
  41.2 0.1 reduce_sum.69
  41.4 0.1 broadcast_in_dim.54
  41.4 0.1 pad_maximum_fusion
  41.5 0.0 copy-start.1
  41.5 32.8 %all_to_all.31.trip_ref.mine_ref = bf16[32,120,128]{2,1,0:T(8,128)(2,1)S(1)} all-to-all(bf16[32,120,128]{2,1,0:T(8,128)(2,1)S(1)} %pad_maximum_fusion), channel_id=1, replica_groups=mesh['section'=8,'chip'=32,'core'=2] {'chip'}, dimensions={0} | all-to-all | bytes 1966080 | tf_op jit(solution)/shard_map/all_to_all | solution.py:26
  74.4 3.9 %collective-permute-start.1 = (bf16[32,120,128]{2,1,0:T(8,128)(2,1)S(1)}, bf16[32,120,128]{2,1,0:T(8,128)(2,1)S(1)}, u32[]{:S(2)}, u32[]{:S(2)}) collective-permute-start(bf16[32,120,128]{2,1,0:T(8,128)(2,1)S(1)} %all_to_all.31.trip_ref.mine_ref), channel_id=1, source_target_pairs={{0,1},{1,0},{2,3},{3,2},{4,5},{5,4},{6,7},{7,6},{8,9},{9,8},{10,11... | collective-permute-start | bytes 2949128 | tf_op jit(solution)/shard_map/ppermute | solution.py:31
  78.3 0.0 copy-done.1
  78.3 0.6 shard_map.120
  78.9 1.9 %collective-permute-start = (bf16[32,80,128]{2,1,0:T(8,128)(2,1)S(1)}, bf16[32,80,128]{2,1,0:T(8,128)(2,1)S(1)}, u32[]{:S(2)}, u32[]{:S(2)}) collective-permute-start(bf16[32,80,128]{2,1,0:T(8,128)(2,1)S(1)} %get-tuple-element.18), channel_id=1, source_target_pairs={{0,1},{1,0},{2,3},{3,2},{4,5},{5,4},{6,7},{7,6},{8,9},{9,8},{10,11... | collective-permute-start | bytes 1966088 | tf_op jit(solution)/shard_map/ppermute | solution.py:31
  80.8 0.0 collective-permute-done.1.other_ref
  80.8 1.7 %shard_map.121 = (bf16[48,128]{1,0:T(8,128)(2,1)S(1)}, f32[40,5120]{1,0:T(8,128)S(1)}, f32[8,128]{1,0:T(8,128)S(1)}) custom-call(s32[1]{0:T(128)} %bitcast.7.core_ref, bf16[32,120,128]{2,1,0:T(8,128)(2,1)S(1)} %all_to_all.31.trip_ref.mine_ref, bf16[32,120,128]{2,1,0:T(8,128)(2,1)S(1)} %collective-permute-done.1.other_ref, ...), custom_call_target="tpu_custom_call" | custom-call | flops 104857600 | bytes 4532224 | tf_op jit(solution)/shard_map/pallas_call | solution.py:51
  82.5 0.4 collective-permute-done.arrived_ref
  82.9 1.2 shard_map.122
  84.1 6.7 %all-to-all-start.3 = ((bf16[32,128,128]{2,1,0:T(8,128)(2,1)}), bf16[32,128,128]{2,1,0:T(8,128)(2,1)S(1)}, u32[]{:S(2)}, u32[]{:S(2)}) async-start(bf16[32,128,128]{2,1,0:T(8,128)(2,1)} %shard_map.122), calls=%async_computation.3 | async-start | bytes 2097152 | tf_op jit(solution)/shard_map/all_to_all | solution.py:26
  90.8 33.4 %all-to-all-done.3 = bf16[32,128,128]{2,1,0:T(8,128)(2,1)S(1)} async-done(((bf16[32,128,128]{2,1,0:T(8,128)(2,1)}), bf16[32,128,128]{2,1,0:T(8,128)(2,1)S(1)}, u32[]{:S(2)}, u32[]{:S(2)}) %all-to-all-start.3) | async-done | bytes 1048608 | tf_op jit(solution)/shard_map/all_to_all | solution.py:26
  124.3 2.6 %all-gather = bf16[32,96,128]{2,1,0:T(8,128)(2,1)S(1)} all-gather(bf16[32,48,128]{2,1,0:T(8,128)(2,1)S(1)} %slice.52), channel_id=2, replica_groups=mesh['section'=8,'chip'=32,'core'=2] {'core'}, dimensions={1}, use_global_device_ids=true | all-gather | bytes 1179648 | tf_op jit(solution)/shard_map/all_gather | solution.py:235
  126.9 0.1 convert_reduce_fusion.1
  127.0 0.1 slice.53
  127.1 0.3 fusion.3
  127.4 0.1 convert_reduce_fusion
  127.5 0.8 broadcast_select_fusion
  128.3 4.2 %all-to-all-start.4 = ((bf16[8,88,128]{2,1,0:T(8,128)(2,1)}), bf16[8,88,128]{2,1,0:T(8,128)(2,1)S(1)}, u32[]{:S(2)}, u32[]{:S(2)}) async-start(bf16[8,88,128]{2,1,0:T(8,128)(2,1)} %broadcast_select_fusion), calls=%async_computation.4 | async-start | bytes 360448 | tf_op jit(solution)/shard_map/all_to_all | solution.py:26
  132.5 5.8 %all-to-all-done.4 = bf16[8,88,128]{2,1,0:T(8,128)(2,1)S(1)} async-done(((bf16[8,88,128]{2,1,0:T(8,128)(2,1)}), bf16[8,88,128]{2,1,0:T(8,128)(2,1)S(1)}, u32[]{:S(2)}, u32[]{:S(2)}) %all-to-all-start.4) | async-done | bytes 180256 | tf_op jit(solution)/shard_map/all_to_all | solution.py:26
  138.3 0.6 convert_reduce_fusion.3
  139.6 0.2 fusion.1
  139.8 0.1 copy.30
  139.9 0.7 copy.31
  140.6 10.3 %all-to-all-start.5 = ((bf16[64,8,80]{2,1,0:T(8,128)(2,1)}), bf16[64,8,80]{2,1,0:T(8,128)(2,1)S(1)}, u32[]{:S(2)}, u32[]{:S(2)}) async-start(bf16[64,8,80]{2,1,0:T(8,128)(2,1)} %bitcast.22), calls=%async_computation.5 | async-start | bytes 262144 | tf_op jit(solution)/shard_map/all_to_all | solution.py:26
  150.9 3.3 %fusion.12 = (f32[1,40,5120]{2,1,0:T(8,128)}, bf16[1,40,5120]{2,1,0:T(8,128)(2,1)}, f32[1,40,5120]{2,1,0:T(8,128)}) fusion(f32[40,5120]{1,0:T(8,128)S(1)} %get-tuple-element.26, f32[]{:T(128)S(6)} %min.3, f32[1,40,5120]{2,1,0:T(8,128)} %param.15, f32[1,40,5120]{2,1,0:T(8,128)} %param.14, bf16[1,40,5120]{2,1,0:T(8,128)(2,1)S(1)} %copy-done.1), kind=kLoop, calls=%fused_computation.23 | loop fusion | flops 3276800 | bytes 4915204 | tf_op jit(solution)/shard_map/broadcast_in_dim | solution.py:275
  154.2 9.2 %all-to-all-done.5.trip_ref = bf16[64,8,80]{2,1,0:T(8,128)(2,1)S(1)} async-done(((bf16[64,8,80]{2,1,0:T(8,128)(2,1)}), bf16[64,8,80]{2,1,0:T(8,128)(2,1)S(1)}, u32[]{:S(2)}, u32[]{:S(2)}) %all-to-all-start.5) | async-done | bytes 81952 | tf_op jit(solution)/shard_map/all_to_all | solution.py:26
  163.4 0.8 shard_map.123
  (12 shorter events, 0.2 us)
Async XLA Ops:
  0.6 35.5 %copy-start = (bf16[1,80,2560]{2,1,0:T(8,128)(2,1)S(1)}, bf16[1,80,2560]{2,1,0:T(8,128)(2,1)}, u32[]{:S(2)}) copy-start(bf16[1,80,2560]{2,1,0:T(8,128)(2,1)} %param.13) | copy-start | bytes 1228804
  0.6 0.8 copy-start.2
  1.5 0.8 copy-start.3
  3.1 30.2 %all-to-all-start = ((bf16[64,8,80]{2,1,0:T(8,128)(2,1)}), bf16[64,8,80]{2,1,0:T(8,128)(2,1)S(1)}, u32[]{:S(2)}, u32[]{:S(2)}) async-start(bf16[64,8,80]{2,1,0:T(8,128)(2,1)} %shard_map.119), calls=%async_computation | async-start | bytes 262144 | tf_op jit(solution)/shard_map/all_to_all | solution.py:26
  41.5 36.8 %copy-start.1 = (bf16[1,40,5120]{2,1,0:T(8,128)(2,1)S(1)}, bf16[1,40,5120]{2,1,0:T(8,128)(2,1)}, u32[]{:S(2)}) copy-start(bf16[1,40,5120]{2,1,0:T(8,128)(2,1)} %param.12) | copy-start | bytes 1228804
  74.4 6.5 %collective-permute-start.1 = (bf16[32,120,128]{2,1,0:T(8,128)(2,1)S(1)}, bf16[32,120,128]{2,1,0:T(8,128)(2,1)S(1)}, u32[]{:S(2)}, u32[]{:S(2)}) collective-permute-start(bf16[32,120,128]{2,1,0:T(8,128)(2,1)S(1)} %all_to_all.31.trip_ref.mine_ref), channel_id=1, source_target_pairs={{0,1},{1,0},{2,3},{3,2},{4,5},{5,4},{6,7},{7,6},{8,9},{9,8},{10,11... | collective-permute-start | bytes 2949128 | tf_op jit(solution)/shard_map/ppermute | solution.py:31
  78.9 4.0 %collective-permute-start = (bf16[32,80,128]{2,1,0:T(8,128)(2,1)S(1)}, bf16[32,80,128]{2,1,0:T(8,128)(2,1)S(1)}, u32[]{:S(2)}, u32[]{:S(2)}) collective-permute-start(bf16[32,80,128]{2,1,0:T(8,128)(2,1)S(1)} %get-tuple-element.18), channel_id=1, source_target_pairs={{0,1},{1,0},{2,3},{3,2},{4,5},{5,4},{6,7},{7,6},{8,9},{9,8},{10,11... | collective-permute-start | bytes 1966088 | tf_op jit(solution)/shard_map/ppermute | solution.py:31
  84.1 40.2 %all-to-all-start.3 = ((bf16[32,128,128]{2,1,0:T(8,128)(2,1)}), bf16[32,128,128]{2,1,0:T(8,128)(2,1)S(1)}, u32[]{:S(2)}, u32[]{:S(2)}) async-start(bf16[32,128,128]{2,1,0:T(8,128)(2,1)} %shard_map.122), calls=%async_computation.3 | async-start | bytes 2097152 | tf_op jit(solution)/shard_map/all_to_all | solution.py:26
  128.3 10.0 %all-to-all-start.4 = ((bf16[8,88,128]{2,1,0:T(8,128)(2,1)}), bf16[8,88,128]{2,1,0:T(8,128)(2,1)S(1)}, u32[]{:S(2)}, u32[]{:S(2)}) async-start(bf16[8,88,128]{2,1,0:T(8,128)(2,1)} %broadcast_select_fusion), calls=%async_computation.4 | async-start | bytes 360448 | tf_op jit(solution)/shard_map/all_to_all | solution.py:26
  140.6 22.8 %all-to-all-start.5 = ((bf16[64,8,80]{2,1,0:T(8,128)(2,1)}), bf16[64,8,80]{2,1,0:T(8,128)(2,1)S(1)}, u32[]{:S(2)}, u32[]{:S(2)}) async-start(bf16[64,8,80]{2,1,0:T(8,128)(2,1)} %bitcast.22), calls=%async_computation.5 | async-start | bytes 262144 | tf_op jit(solution)/shard_map/all_to_all | solution.py:26

commit v4 on v3

--- a/solution.py
+++ b/solution.py
@@ -35,24 +35,21 @@
     return jnp.broadcast_to(block[None], (count,) + block.shape)
 
 
-def selection(placed, capacity, micro_rows):
-    count = placed.shape[0]
-    ids = jnp.arange(count, dtype=jnp.int32)
+def slot_rows_of(placed, capacity, micro_rows):
+    ids = jnp.arange(placed.shape[0], dtype=jnp.int32)
     twins = (placed[:, None] == placed[None, :]) & (ids[:, None] < ids[None, :])
     slots = placed * capacity + jnp.sum(twins.astype(jnp.int32), axis=0)
-    rows = (slots[:, None] * micro_rows + jnp.arange(micro_rows, dtype=jnp.int32)).reshape(-1)
-    every = jnp.arange(count * capacity * micro_rows, dtype=jnp.int32)
-    return (every[:, None] == rows[None, :]).astype(jnp.bfloat16)
-
-
-def on_core(kernel, out_shape, scalars, arrays, scratch=(), flops=0):
+    return (slots[:, None] * micro_rows + jnp.arange(micro_rows, dtype=jnp.int32)).reshape(-1)
+
+
+def on_core(kernel, out_shape, scalars, arrays, scratch=(), flops=0, held_in=pltpu.VMEM):
     size = sum(a.size * a.dtype.itemsize for a in arrays)
     size += sum(o.size * o.dtype.itemsize for o in out_shape)
     return pl.pallas_call(
         kernel,
         out_shape=out_shape,
         in_specs=[pl.BlockSpec(memory_space=pltpu.SMEM)] * len(scalars)
-        + [pl.BlockSpec(memory_space=pltpu.VMEM)] * len(arrays),
+        + [pl.BlockSpec(memory_space=held_in)] * len(arrays),
         out_specs=[pl.BlockSpec(memory_space=pltpu.VMEM)] * len(out_shape),
         scratch_shapes=list(scratch),
         compiler_params=pltpu.CompilerParams(vmem_limit_bytes=24 * 2**20),
@@ -85,13 +82,63 @@
             other_ref[chip] = jnp.where(first_core, high, low).astype(jnp.bfloat16)
 
 
-def split_kernel(acts_ref, cotan_ref, out_ref):
-    peers, _, width = out_ref.shape
-    _, _, capacity, _, _ = acts_ref.shape
-    held = [ref[0, 0, slot] for ref in (acts_ref, cotan_ref) for slot in range(capacity)]
+def split_kernel(acts_ref, cotan_ref, out_ref, acts_here, cotan_here, arrived):
+    chips, _, width = out_ref.shape
+    pairs = ((acts_ref, acts_here), (cotan_ref, cotan_here))
+    copies = [pltpu.make_async_copy(a, b, arrived.at[n]) for n, (a, b) in enumerate(pairs)]
+    for copy in copies:
+        copy.start()
+    for copy in copies:
+        copy.wait()
+    capacity = acts_here.shape[2]
+    held = [ref[0, 0, slot] for ref in (acts_here, cotan_here) for slot in range(capacity)]
     held = jnp.concatenate([rows.astype(jnp.float32) for rows in held], axis=0)
-    for peer in range(peers):
-        out_ref[peer] = held[:, peer * width : (peer + 1) * width].astype(jnp.bfloat16)
+    for chip in range(chips):
+        out_ref[chip] = held[:, chip * width : (chip + 1) * width].astype(jnp.bfloat16)
+
+
+def features_kernel(
+    heads, core_ref, cols_ref, at_ref, weight_ref, other_weight_ref,
+    out_ref, stream_ref, cotangent_ref,
+):
+    chips = out_ref.shape[0]
+    width, rows = stream_ref.shape
+    slot_rows = cols_ref.shape[0] // (4 * chips)
+    first_core = core_ref[0] == 0
+    line = lax.broadcasted_iota(jnp.int32, (cols_ref.shape[0], rows), 0)
+    cols = cols_ref[...]
+
+    def picked(first):
+        select = (line == at_ref[...] + first).astype(jnp.float32).astype(jnp.bfloat16)
+        both = lax.dot_general(
+            cols, select, (((0,), (0,)), ((), ())), preferred_element_type=jnp.float32
+        )
+        low, high = both[:width], both[width:]
+        own = jnp.where(first_core, low, high).astype(jnp.bfloat16)
+        return own, jnp.where(first_core, high, low).astype(jnp.bfloat16)
+
+    stream, _ = picked(0)
+    cotangent, other_cotangent = picked(slot_rows)
+    stream_ref[...] = stream
+    cotangent_ref[...] = cotangent
+    group = min(8, chips)
+    span = group * 2 * heads
+    for step in range(chips // group):
+        part = sum(
+            lax.dot_general(
+                ref[:, step * span : (step + 1) * span],
+                block,
+                (((0,), (0,)), ((), ())),
+                preferred_element_type=jnp.float32,
+            )
+            for ref, block in ((weight_ref, cotangent), (other_weight_ref, other_cotangent))
+        )
+        for local in range(group):
+            low = part[2 * local * heads : (2 * local + 1) * heads]
+            high = part[(2 * local + 1) * heads : (2 * local + 2) * heads]
+            chip = step * group + local
+            mine = jnp.where(first_core, low, high).astype(jnp.bfloat16)
+            out_ref[chip] = jnp.concatenate([stream, mine], axis=0)
 
 
 def join_kernel(trip_ref, passed_ref, returned_ref, rows_ref):
@@ -127,17 +174,28 @@
     inverse = lax.rsqrt(mean + NORM_EPS)
     inverse_ref[...] = jnp.broadcast_to(inverse, inverse_ref.shape)
     first_core = core_ref[0] == 0
-    for chip in range(chips):
-        mine, other = mine_ref[chip, :width, :], other_ref[chip, :width, :]
-        for core, block in ((0, jnp.where(first_core, mine, other)), (1, jnp.where(first_core, other, mine))):
-            at = (2 * chip + core) * width
-            unit = block.astype(jnp.float32) * inverse
-            scaled = unit * gain_ref[at : at + width, :].astype(jnp.float32)
-            normed_ref[at : at + width, :] = scaled.astype(jnp.bfloat16)
+    lanes = mine_ref.shape[2]
+    one = (lax.broadcasted_iota(jnp.int32, (16, lanes), 0) == 0).astype(jnp.float32)
+    group = 4
+    span = group * 2 * width
+    for step in range(chips // group):
+        gains = jnp.broadcast_to(gain_ref[:, step * span : (step + 1) * span], (16, span))
+        gains = lax.dot_general(
+            gains,
+            one.astype(jnp.bfloat16),
+            (((0,), (0,)), ((), ())),
+            preferred_element_type=jnp.float32,
+        )
+        for local in range(group):
+            mine, other = (ref[step * group + local, :width, :] for ref in (mine_ref, other_ref))
+            low, high = jnp.where(first_core, mine, other), jnp.where(first_core, other, mine)
+            for core, block in ((0, low), (1, high)):
+                at = (2 * local + core) * width
+                scaled = block.astype(jnp.float32) * inverse * gains[at : at + width]
+                normed_ref[pl.ds(step * span + at, width), :] = scaled.astype(jnp.bfloat16)
     values = jnp.dot(weight_ref[...], normed_ref[...], preferred_element_type=jnp.float32)
     grads = grads_ref[...]
     span = 8 * width
-    lanes = mine_ref.shape[2]
     norms = jnp.zeros((heads, lanes), jnp.float32)
     for step in range(model // span):
         block = lax.dot_general(
@@ -179,29 +237,40 @@
     rows = peers * micro_rows
     weights, out_weights = w_value[0], w_out[0]
 
+    core = lax.axis_index("core").astype(jnp.int32).reshape(1)
+    brief, full = jnp.bfloat16, jnp.float32
     (held,) = on_core(
         split_kernel,
-        [jax.ShapeDtypeStruct((peers, 2 * slot_rows, width), jnp.bfloat16)],
+        [jax.ShapeDtypeStruct((chips, 2 * slot_rows, 2 * width), brief)],
         [],
         [acts, cotan],
-    )
-    cols = swap(held, PEER)
+        [pltpu.VMEM(acts.shape, brief), pltpu.VMEM(cotan.shape, brief), pltpu.SemaphoreType.DMA((2,))],
+        held_in=pltpu.HBM,
+    )
+    other_out_weights = moved(out_weights, "core", 1)
+    cols = swap(held, "chip")
     placed = lax.dynamic_index_in_dim(placing[:, :, 0], section_now, 0, keepdims=False)
-    select = selection(placed, capacity, micro_rows)
-    gain_col = jnp.broadcast_to(gain[0][:, None], (model, rows))
-    own_gain = lax.dynamic_slice_in_dim(gain_col, peer_now * width, width, 0)
-    cols, gain_col, own_gain = lax.optimization_barrier((cols, gain_col, own_gain))
-    cols = cols.reshape(peers, 2, slot_rows, width).transpose(1, 0, 2, 3)
-    stacked = matmul("ksf,sr->kfr", cols.reshape(2, peers * slot_rows, width), select)
-    stream, cotangent = stacked[0].astype(jnp.bfloat16), stacked[1].astype(jnp.bfloat16)
-
-    grads = matmul("fh,fr->hr", out_weights, cotangent).astype(jnp.bfloat16)
-    grads = swap(grads.reshape(chips, 2, heads, rows).transpose(1, 0, 2, 3), "core")
-    grads = jnp.sum(grads.astype(jnp.float32), axis=0).astype(jnp.bfloat16)
-    first_trip = swap(jnp.concatenate([to_all(stream, chips), grads], axis=1), "chip")
-    core = lax.axis_index("core").astype(jnp.int32).reshape(1)
+    slots = slot_rows_of(placed, capacity, micro_rows)
+    holder = slots // slot_rows
+    at = ((holder % 2) * chips + holder // 2) * (2 * slot_rows) + slots % slot_rows
+    own_gain = lax.dynamic_slice_in_dim(gain[0], peer_now * width, width, 0).astype(full)
+    own_gain = jnp.broadcast_to(own_gain[:, None], (width, rows))
+    cols, at, slots, own_gain = lax.optimization_barrier((cols, at, slots, own_gain))
+    cols = lax.all_gather(cols, "core", axis=0).reshape(peers * 2 * slot_rows, 2 * width)
+
+    payload, stream, cotangent = on_core(
+        functools.partial(features_kernel, heads),
+        [
+            jax.ShapeDtypeStruct((chips, width + heads, rows), brief),
+            jax.ShapeDtypeStruct((width, rows), brief),
+            jax.ShapeDtypeStruct((width, rows), brief),
+        ],
+        [core],
+        [cols, at[None], out_weights, other_out_weights],
+        flops=4 * heads * peers * width * rows,
+    )
+    first_trip = swap(payload, "chip")
     other_trip = moved(first_trip, "core", 1)
-    brief, full = jnp.bfloat16, jnp.float32
     half = jax.ShapeDtypeStruct((chips, width, rows), brief)
     value_grads, mine, other = on_core(
         functools.partial(dnormed_kernel, width, heads),
@@ -219,7 +288,7 @@
             jax.ShapeDtypeStruct((SPARE, rows), full),
         ],
         [core],
-        [first_trip, other_trip, gain_col, weights, value_grads],
+        [first_trip, other_trip, gain, weights, value_grads],
         [pltpu.VMEM((model, rows), brief)],
         flops=4 * model * heads * rows,
     )
@@ -231,6 +300,9 @@
     )
     inverse_rms = inverse[:1]
     second_trip = swap(payload, "chip")
+    kept = (gradient, inverse_rms, stream, cotangent, own_gain, slots, w_value, moment_one, moment_two)
+    second_trip, kept = lax.optimization_barrier((second_trip, kept))
+    gradient, inverse_rms, stream, cotangent, own_gain, slots, w_value, moment_one, moment_two = kept
     norm_grads = jnp.sum(second_trip[:, :width].astype(jnp.float32), axis=0)
     gathered = lax.all_gather(second_trip[:, width:], "core", axis=1)
     extra = jnp.sum(gathered[:, :, heads:].astype(jnp.float32), axis=(0, 1))
@@ -240,7 +312,7 @@
     outputs = (stream.astype(jnp.float32) + mixed).astype(jnp.bfloat16)
     unit = stream.astype(jnp.float32) * inverse_rms
     back = (
-        cotangent.astype(jnp.float32) + inverse_rms * (norm_grads * own_gain.astype(jnp.float32) - unit * inner)
+        cotangent.astype(jnp.float32) + inverse_rms * (norm_grads * own_gain - unit * inner)
     ).astype(jnp.bfloat16)
 
     sections = lax.axis_size("section")
@@ -249,15 +321,19 @@
     ahead = jnp.arange(sections)[:, None, None] == (section_now + 1) % sections
     both = jnp.where(ahead, jnp.concatenate([outputs, parts]), jnp.concatenate([back, parts]))
     third_trip = swap(both, "section")
-    totals = jnp.sum(third_trip[:, width : width + 3].astype(jnp.float32))
     behind = [(section_now + sections - 1) % sections, (section_now + 1) % sections]
     arrived = jnp.stack(
         [lax.dynamic_index_in_dim(third_trip, at, 0, keepdims=False)[:width] for at in behind]
     )
 
-    spread = matmul("sr,kfr->ksf", select, arrived).astype(jnp.bfloat16)
+    every = jnp.arange(peers * slot_rows, dtype=jnp.int32)
+    select = (every[:, None] == slots[None, :]).astype(brief)
+    spread = matmul("sr,kfr->ksf", select, arrived).astype(brief)
     spread = spread.reshape(2, peers, slot_rows, width).transpose(1, 0, 2, 3)
-    final = swap(spread.reshape(peers, 2 * slot_rows, width), PEER)
+    spread = spread.reshape(peers, 2 * slot_rows, width)
+    spread, third_trip = lax.optimization_barrier((spread, third_trip))
+    final = swap(spread, PEER)
+    totals = jnp.sum(third_trip[:, width : width + 3].astype(full))
     passed, returned = on_core(
         join_kernel,
         [jax.ShapeDtypeStruct(acts.shape, brief)] * 2,
@@ -270,7 +346,7 @@
     clipped = gradient * clip_scale
     first = BETA_ONE * moment_one[0] + (1.0 - BETA_ONE) * clipped
     second = BETA_TWO * moment_two[0] + (1.0 - BETA_TWO) * clipped * clipped
-    wide = weights.astype(jnp.float32)
+    wide = w_value[0].astype(jnp.float32)
     updated = wide - LEARN_RATE * (first / (jnp.sqrt(second) + ADAM_EPS) + DECAY * wide)
     return passed, returned, updated.astype(jnp.bfloat16)[None], first[None], second[None]
 

time: 165 us -> 158 us (0.958)
  local copies, waits for them, and re-layouts: 7.19 us -> 3.42 us
  waiting for transfers between devices: 58.2 us -> 55.7 us
  starting transfers between devices: 44.6 us -> 46.4 us
    all_to_all x2 -> x1, blocking collectives: 37.2 us -> 32.2 us  [swap(): return lax.all_to_all(blocks, axis, split_axis=0, concat_axis=0, tiled=True)]
    all_gather x0 -> x1, blocking collectives: none -> 3.73 us  [body(): lax.all_gather(cols, 'core', axis=0)]
    ppermute x2 -> x3, starting transfers between devices: 5.86 us -> 8.77 us  [moved(): lax.ppermute(block, axis, [(i, (i + distance) % count) for i in range(cou...]
    all_to_all x4, waiting for transfers between devices: 57.8 us -> 55.1 us  [swap(): return lax.all_to_all(blocks, axis, split_axis=0, concat_axis=0, tiled=True)]
    broadcast_in_dim x3 -> x1, local copies, waits for them, and re-layouts: 2.65 us -> 0.07 us  [body(): own_gain = jnp.broadcast_to(own_gain[:, None], (width, rows))]
    pallas_call x5 -> x6, Pallas kernels: 5.03 us -> 5.69 us  [on_core(): pl.pallas_call(kernel, out_shape=out_shape, in_specs=[pl.BlockSpec(memory...]
  transfers between devices with their start and end apart: 6 -> 7, of which waited for: 5 -> 5; matrix products, arithmetic and copies ran while one was open for 4% -> 3% of each run, Pallas kernels for 1% -> 1%
where the time goes in v4:
time: 158 us; the launch traced here: 157 us
  waiting for transfers between devices  55.7 us (35%)
  starting transfers between devices  46.4 us (29%)
  blocking collectives  38.6 us (24%)
  Pallas kernels  5.69 us (4%)
  other arithmetic  5.15 us (3%)
  local copies, waits for them, and re-layouts  3.42 us (2%)
  between operations  1.59 us (1%)
    all_to_all x4, waiting for transfers between devices, swap(): return lax.all_to_all(blocks, axis, split_axis=0, concat_axis=0, tiled=True)  55.1 us
    all_to_all x4, starting transfers between devices, swap(): return lax.all_to_all(blocks, axis, split_axis=0, concat_axis=0, tiled=True)  37.6 us
    all_to_all x1, blocking collectives, swap(): return lax.all_to_all(blocks, axis, split_axis=0, concat_axis=0, tiled=True)  32.2 us
    ppermute x3, starting transfers between devices, moved(): lax.ppermute(block, axis, [(i, (i + distance) % count) for i in range(cou...  8.77 us
    pallas_call x6, Pallas kernels, on_core(): pl.pallas_call(kernel, out_shape=out_shape, in_specs=[pl.BlockSpec(memory...  5.69 us
    all_gather x1, blocking collectives, body(): lax.all_gather(cols, 'core', axis=0)  3.73 us
  transfers between devices with their start and end apart: 7, of which 5 were waited for; matrix products, arithmetic and copies ran while one was open for 3% of the time, Pallas kernels for 1%

profile of v4, /device:TPU:1, one launch (start us, length us, event | category | flops | bytes accessed | tf_op | source)
XLA Modules:
  0.0 156.9 jit_solution(16879162453935818519)
XLA Ops:
  0.6 0.0 copy-start.1
  0.6 0.0 copy-start.2
  0.7 0.8 copy-done.2
  1.5 0.0 copy-start.3
  1.5 0.8 copy-done.3
  2.3 0.9 shard_map.119
  3.1 16.5 %all-to-all-start = ((bf16[32,8,160]{2,1,0:T(8,128)(2,1)}), bf16[32,8,160]{2,1,0:T(8,128)(2,1)S(1)}, u32[]{:S(2)}, u32[]{:S(2)}) async-start(bf16[32,8,160]{2,1,0:T(8,128)(2,1)} %shard_map.119), calls=%async_computation | async-start | bytes 262144 | tf_op jit(solution)/shard_map/all_to_all | solution.py:26
  19.7 2.9 %collective-permute-start = (bf16[80,2560]{1,0:T(8,128)(2,1)}, bf16[80,2560]{1,0:T(8,128)(2,1)S(1)}, u32[]{:S(2)}, u32[]{:S(2)}) collective-permute-start(bf16[80,2560]{1,0:T(8,128)(2,1)} %bitcast.67), channel_id=1, source_target_pairs={{0,1},{1,0},{2,3},{3,2},{4,5},{5,4},{6,7},{7,6},{8,9},{9,8},{10,11... | collective-permute-start | bytes 1228808 | tf_op jit(solution)/shard_map/ppermute | solution.py:31
  22.5 0.7 fusion.29
  23.2 0.1 convert_reduce_fusion.2
  23.3 0.7 add_multiply_fusion
  24.0 0.1 iota_add_fusion
  24.0 0.1 add.108
  24.2 0.8 fusion.31
  25.0 6.1 %all-to-all-done = bf16[32,8,160]{2,1,0:T(8,128)(2,1)S(1)} async-done(((bf16[32,8,160]{2,1,0:T(8,128)(2,1)}), bf16[32,8,160]{2,1,0:T(8,128)(2,1)S(1)}, u32[]{:S(2)}, u32[]{:S(2)}) %all-to-all-start) | async-done | bytes 81952 | tf_op jit(solution)/shard_map/all_to_all | solution.py:26
  31.1 0.1 broadcast_in_dim.27
  31.2 3.7 %all-gather = bf16[64,8,160]{2,1,0:T(8,128)(2,1)S(1)} all-gather(bf16[32,8,160]{2,1,0:T(8,128)(2,1)S(1)} %all-to-all-done), channel_id=2, replica_groups=mesh['section'=8,'chip'=32,'core'=2] {'core'}, dimensions={0}, use_global_device_ids=true | all-gather | bytes 245760 | tf_op jit(solution)/shard_map/all_gather | solution.py:259
  34.9 0.0 collective-permute-done.other_weight_ref
  34.9 0.0 copy-done.1
  34.9 0.8 shard_map.120
  35.7 0.0 copy-start
  35.7 32.2 %all_to_all.25.trip_ref.mine_ref = bf16[32,120,128]{2,1,0:T(8,128)(2,1)S(1)} all-to-all(bf16[32,120,128]{2,1,0:T(8,128)(2,1)S(1)} %get-tuple-element.34), channel_id=1, replica_groups=mesh['section'=8,'chip'=32,'core'=2] {'chip'}, dimensions={0} | all-to-all | bytes 1966080 | tf_op jit(solution)/shard_map/all_to_all | solution.py:26
  67.9 0.0 copy-start.4
  67.9 4.0 %collective-permute-start.2 = (bf16[32,120,128]{2,1,0:T(8,128)(2,1)S(1)}, bf16[32,120,128]{2,1,0:T(8,128)(2,1)S(1)}, u32[]{:S(2)}, u32[]{:S(2)}) collective-permute-start(bf16[32,120,128]{2,1,0:T(8,128)(2,1)S(1)} %all_to_all.25.trip_ref.mine_ref), channel_id=1, source_target_pairs={{0,1},{1,0},{2,3},{3,2},{4,5},{5,4},{6,7},{7,6},{8,9},{9,8},{10,11... | collective-permute-start | bytes 2949128 | tf_op jit(solution)/shard_map/ppermute | solution.py:31
  71.9 0.0 copy-done
  71.9 0.6 shard_map.121
  72.5 1.9 %collective-permute-start.1 = (bf16[32,80,128]{2,1,0:T(8,128)(2,1)S(1)}, bf16[32,80,128]{2,1,0:T(8,128)(2,1)S(1)}, u32[]{:S(2)}, u32[]{:S(2)}) collective-permute-start(bf16[32,80,128]{2,1,0:T(8,128)(2,1)S(1)} %get-tuple-element.36), channel_id=1, source_target_pairs={{0,1},{1,0},{2,3},{3,2},{4,5},{5,4},{6,7},{7,6},{8,9},{9,8},{10,11... | collective-permute-start | bytes 1966088 | tf_op jit(solution)/shard_map/ppermute | solution.py:31
  74.5 0.0 collective-permute-done.2.other_ref
  74.5 0.0 copy-done.4
  74.5 1.5 shard_map.122
  76.0 0.6 collective-permute-done.1.arrived_ref
  76.5 1.2 shard_map.123
  77.7 7.0 %all-to-all-start.2 = ((bf16[32,128,128]{2,1,0:T(8,128)(2,1)}), bf16[32,128,128]{2,1,0:T(8,128)(2,1)S(1)}, u32[]{:S(2)}, u32[]{:S(2)}) async-start(bf16[32,128,128]{2,1,0:T(8,128)(2,1)} %shard_map.123), calls=%async_computation.2 | async-start | bytes 2097152 | tf_op jit(solution)/shard_map/all_to_all | solution.py:26
  84.8 33.8 %all-to-all-done.2 = bf16[32,128,128]{2,1,0:T(8,128)(2,1)S(1)} async-done(((bf16[32,128,128]{2,1,0:T(8,128)(2,1)}), bf16[32,128,128]{2,1,0:T(8,128)(2,1)S(1)}, u32[]{:S(2)}, u32[]{:S(2)}) %all-to-all-start.2) | async-done | bytes 1048608 | tf_op jit(solution)/shard_map/all_to_all | solution.py:26
  118.7 2.6 %all-gather.1 = bf16[32,96,128]{2,1,0:T(8,128)(2,1)S(1)} all-gather(bf16[32,48,128]{2,1,0:T(8,128)(2,1)S(1)} %slice.33), channel_id=3, replica_groups=mesh['section'=8,'chip'=32,'core'=2] {'core'}, dimensions={1}, use_global_device_ids=true | all-gather | bytes 1179648 | tf_op jit(solution)/shard_map/all_gather | solution.py:307
  121.3 0.1 convert_reduce_fusion.1
  121.3 0.1 slice.42
  121.4 0.1 convert_reduce_fusion
  121.6 0.3 fusion.2
  121.8 0.0 copy-start.5
  121.8 0.0 copy-start.6
  121.9 0.8 broadcast_select_fusion
  122.7 4.2 %all-to-all-start.3 = ((bf16[8,88,128]{2,1,0:T(8,128)(2,1)}), bf16[8,88,128]{2,1,0:T(8,128)(2,1)S(1)}, u32[]{:S(2)}, u32[]{:S(2)}) async-start(bf16[8,88,128]{2,1,0:T(8,128)(2,1)} %broadcast_select_fusion), calls=%async_computation.3 | async-start | bytes 360448 | tf_op jit(solution)/shard_map/all_to_all | solution.py:26
  126.8 5.8 %all-to-all-done.3 = bf16[8,88,128]{2,1,0:T(8,128)(2,1)S(1)} async-done(((bf16[8,88,128]{2,1,0:T(8,128)(2,1)}), bf16[8,88,128]{2,1,0:T(8,128)(2,1)S(1)}, u32[]{:S(2)}, u32[]{:S(2)}) %all-to-all-start.3) | async-done | bytes 180256 | tf_op jit(solution)/shard_map/all_to_all | solution.py:26
  132.7 0.2 fusion
  132.9 0.1 copy.18
  133.0 0.7 copy.19
  133.7 9.9 %all-to-all-start.4 = ((bf16[64,8,80]{2,1,0:T(8,128)(2,1)}), bf16[64,8,80]{2,1,0:T(8,128)(2,1)S(1)}, u32[]{:S(2)}, u32[]{:S(2)}) async-start(bf16[64,8,80]{2,1,0:T(8,128)(2,1)} %bitcast.16), calls=%async_computation.4 | async-start | bytes 262144 | tf_op jit(solution)/shard_map/all_to_all | solution.py:26
  143.6 0.6 convert_reduce_fusion.3
  144.9 0.0 copy-done.5
  144.9 0.0 copy-done.6
  144.9 1.9 %fusion.9 = (f32[1,40,5120]{2,1,0:T(8,128)}, bf16[1,40,5120]{2,1,0:T(8,128)(2,1)}, f32[1,40,5120]{2,1,0:T(8,128)}) fusion(f32[40,5120]{1,0:T(8,128)S(1)} %get-tuple-element.56, f32[]{:T(128)S(6)} %min.3, f32[1,40,5120]{2,1,0:T(8,128)S(1)} %copy-done.5, f32[1,40,5120]{2,1,0:T(8,128)S(1)} %copy-done.6, bf16[1,40,5120]{2,1,0:T(8,128)(2,1)S(1)} %copy-done), kind=kLoop, calls=%fused_computation.18 | loop fusion | flops 3276800 | bytes 4915204 | tf_op jit(solution)/shard_map/broadcast_in_dim | solution.py:351
  146.8 9.3 %all-to-all-done.4.trip_ref = bf16[64,8,80]{2,1,0:T(8,128)(2,1)S(1)} async-done(((bf16[64,8,80]{2,1,0:T(8,128)(2,1)}), bf16[64,8,80]{2,1,0:T(8,128)(2,1)S(1)}, u32[]{:S(2)}, u32[]{:S(2)}) %all-to-all-start.4) | async-done | bytes 81952 | tf_op jit(solution)/shard_map/all_to_all | solution.py:26
  156.2 0.8 shard_map.124
  (11 shorter events, 0.1 us)
Async XLA Ops:
  0.6 34.3 %copy-start.1 = (bf16[1,80,2560]{2,1,0:T(8,128)(2,1)S(1)}, bf16[1,80,2560]{2,1,0:T(8,128)(2,1)}, u32[]{:S(2)}) copy-start(bf16[1,80,2560]{2,1,0:T(8,128)(2,1)} %param.13) | copy-start | bytes 1228804
  0.6 0.8 copy-start.2
  1.5 0.8 copy-start.3
  3.1 28.0 %all-to-all-start = ((bf16[32,8,160]{2,1,0:T(8,128)(2,1)}), bf16[32,8,160]{2,1,0:T(8,128)(2,1)S(1)}, u32[]{:S(2)}, u32[]{:S(2)}) async-start(bf16[32,8,160]{2,1,0:T(8,128)(2,1)} %shard_map.119), calls=%async_computation | async-start | bytes 262144 | tf_op jit(solution)/shard_map/all_to_all | solution.py:26
  19.7 15.3 %collective-permute-start = (bf16[80,2560]{1,0:T(8,128)(2,1)}, bf16[80,2560]{1,0:T(8,128)(2,1)S(1)}, u32[]{:S(2)}, u32[]{:S(2)}) collective-permute-start(bf16[80,2560]{1,0:T(8,128)(2,1)} %bitcast.67), channel_id=1, source_target_pairs={{0,1},{1,0},{2,3},{3,2},{4,5},{5,4},{6,7},{7,6},{8,9},{9,8},{10,11... | collective-permute-start | bytes 1228808 | tf_op jit(solution)/shard_map/ppermute | solution.py:31
  35.7 36.2 %copy-start = (bf16[1,40,5120]{2,1,0:T(8,128)(2,1)S(1)}, bf16[1,40,5120]{2,1,0:T(8,128)(2,1)}, u32[]{:S(2)}) copy-start(bf16[1,40,5120]{2,1,0:T(8,128)(2,1)} %param.12) | copy-start | bytes 1228804
  67.9 6.5 %copy-start.4 = (bf16[1,5120]{1,0:T(2,128)(2,1)S(1)}, bf16[1,5120]{1,0:T(2,128)(2,1)}, u32[]{:S(2)}) copy-start(bf16[1,5120]{1,0:T(2,128)(2,1)} %gain_ref.1) | copy-start | bytes 30724
  67.9 6.5 %collective-permute-start.2 = (bf16[32,120,128]{2,1,0:T(8,128)(2,1)S(1)}, bf16[32,120,128]{2,1,0:T(8,128)(2,1)S(1)}, u32[]{:S(2)}, u32[]{:S(2)}) collective-permute-start(bf16[32,120,128]{2,1,0:T(8,128)(2,1)S(1)} %all_to_all.25.trip_ref.mine_ref), channel_id=1, source_target_pairs={{0,1},{1,0},{2,3},{3,2},{4,5},{5,4},{6,7},{7,6},{8,9},{9,8},{10,11... | collective-permute-start | bytes 2949128 | tf_op jit(solution)/shard_map/ppermute | solution.py:31
  72.5 4.0 %collective-permute-start.1 = (bf16[32,80,128]{2,1,0:T(8,128)(2,1)S(1)}, bf16[32,80,128]{2,1,0:T(8,128)(2,1)S(1)}, u32[]{:S(2)}, u32[]{:S(2)}) collective-permute-start(bf16[32,80,128]{2,1,0:T(8,128)(2,1)S(1)} %get-tuple-element.36), channel_id=1, source_target_pairs={{0,1},{1,0},{2,3},{3,2},{4,5},{5,4},{6,7},{7,6},{8,9},{9,8},{10,11... | collective-permute-start | bytes 1966088 | tf_op jit(solution)/shard_map/ppermute | solution.py:31
  77.7 40.9 %all-to-all-start.2 = ((bf16[32,128,128]{2,1,0:T(8,128)(2,1)}), bf16[32,128,128]{2,1,0:T(8,128)(2,1)S(1)}, u32[]{:S(2)}, u32[]{:S(2)}) async-start(bf16[32,128,128]{2,1,0:T(8,128)(2,1)} %shard_map.123), calls=%async_computation.2 | async-start | bytes 2097152 | tf_op jit(solution)/shard_map/all_to_all | solution.py:26
  121.8 23.1 %copy-start.5 = (f32[1,40,5120]{2,1,0:T(8,128)S(1)}, f32[1,40,5120]{2,1,0:T(8,128)}, u32[]{:S(2)}) copy-start(f32[1,40,5120]{2,1,0:T(8,128)} %param.15) | copy-start | bytes 2457604
  121.8 23.1 %copy-start.6 = (f32[1,40,5120]{2,1,0:T(8,128)S(1)}, f32[1,40,5120]{2,1,0:T(8,128)}, u32[]{:S(2)}) copy-start(f32[1,40,5120]{2,1,0:T(8,128)} %param.14) | copy-start | bytes 2457604
  122.7 10.0 %all-to-all-start.3 = ((bf16[8,88,128]{2,1,0:T(8,128)(2,1)}), bf16[8,88,128]{2,1,0:T(8,128)(2,1)S(1)}, u32[]{:S(2)}, u32[]{:S(2)}) async-start(bf16[8,88,128]{2,1,0:T(8,128)(2,1)} %broadcast_select_fusion), calls=%async_computation.3 | async-start | bytes 360448 | tf_op jit(solution)/shard_map/all_to_all | solution.py:26
  133.7 22.5 %all-to-all-start.4 = ((bf16[64,8,80]{2,1,0:T(8,128)(2,1)}), bf16[64,8,80]{2,1,0:T(8,128)(2,1)S(1)}, u32[]{:S(2)}, u32[]{:S(2)}) async-start(bf16[64,8,80]{2,1,0:T(8,128)(2,1)} %bitcast.16), calls=%async_computation.4 | async-start | bytes 262144 | tf_op jit(solution)/shard_map/all_to_all | solution.py:26

commit v5 on v4

--- a/solution.py
+++ b/solution.py
@@ -42,7 +42,7 @@
     return (slots[:, None] * micro_rows + jnp.arange(micro_rows, dtype=jnp.int32)).reshape(-1)
 
 
-def on_core(kernel, out_shape, scalars, arrays, scratch=(), flops=0, held_in=pltpu.VMEM):
+def on_core(kernel, out_shape, scalars, arrays, scratch=(), flops=0, held_in=pltpu.VMEM, limit=24 * 2**20):
     size = sum(a.size * a.dtype.itemsize for a in arrays)
     size += sum(o.size * o.dtype.itemsize for o in out_shape)
     return pl.pallas_call(
@@ -52,7 +52,7 @@
         + [pl.BlockSpec(memory_space=held_in)] * len(arrays),
         out_specs=[pl.BlockSpec(memory_space=pltpu.VMEM)] * len(out_shape),
         scratch_shapes=list(scratch),
-        compiler_params=pltpu.CompilerParams(vmem_limit_bytes=24 * 2**20),
+        compiler_params=pltpu.CompilerParams(vmem_limit_bytes=limit),
         cost_estimate=pl.CostEstimate(flops=flops, bytes_accessed=size, transcendentals=0),
     )(*scalars, *arrays)
 
@@ -245,7 +245,8 @@
         [],
         [acts, cotan],
         [pltpu.VMEM(acts.shape, brief), pltpu.VMEM(cotan.shape, brief), pltpu.SemaphoreType.DMA((2,))],
-        held_in=pltpu.HBM,
+        held_in=pl.ANY,
+        limit=None,
     )
     other_out_weights = moved(out_weights, "core", 1)
     cols = swap(held, "chip")
@@ -298,11 +299,13 @@
         [],
         [mine, arrived, own],
     )
+    second_trip = swap(payload, "chip")
+    kept = (gradient, inverse, stream, cotangent, own_gain, slots, section_now, w_value)
+    kept = kept + (moment_one, moment_two)
+    second_trip, kept = lax.optimization_barrier((second_trip, kept))
+    gradient, inverse, stream, cotangent, own_gain, slots, section_now, w_value = kept[:8]
+    moment_one, moment_two = kept[8:]
     inverse_rms = inverse[:1]
-    second_trip = swap(payload, "chip")
-    kept = (gradient, inverse_rms, stream, cotangent, own_gain, slots, w_value, moment_one, moment_two)
-    second_trip, kept = lax.optimization_barrier((second_trip, kept))
-    gradient, inverse_rms, stream, cotangent, own_gain, slots, w_value, moment_one, moment_two = kept
     norm_grads = jnp.sum(second_trip[:, :width].astype(jnp.float32), axis=0)
     gathered = lax.all_gather(second_trip[:, width:], "core", axis=1)
     extra = jnp.sum(gathered[:, :, heads:].astype(jnp.float32), axis=(0, 1))
@@ -318,18 +321,25 @@
     sections = lax.axis_size("section")
     parts = jnp.concatenate(parts_of(square)).astype(jnp.bfloat16)
     parts = jnp.pad(parts, ((0, SPARE - parts.shape[0]), (0, 0)))
-    ahead = jnp.arange(sections)[:, None, None] == (section_now + 1) % sections
-    both = jnp.where(ahead, jnp.concatenate([outputs, parts]), jnp.concatenate([back, parts]))
+    both = jnp.broadcast_to(jnp.concatenate([back, parts])[None], (sections, width + SPARE, rows))
+    ahead = jnp.concatenate([outputs, parts])
+    both = lax.dynamic_update_index_in_dim(both, ahead, (section_now + 1) % sections, 0)
     third_trip = swap(both, "section")
+    kept = (third_trip, section_now, slots, gradient, w_value, moment_one, moment_two)
+    third_trip, section_now, slots, gradient, w_value, moment_one, moment_two = (
+        lax.optimization_barrier(kept)
+    )
     behind = [(section_now + sections - 1) % sections, (section_now + 1) % sections]
-    arrived = jnp.stack(
-        [lax.dynamic_index_in_dim(third_trip, at, 0, keepdims=False)[:width] for at in behind]
-    )
-
-    every = jnp.arange(peers * slot_rows, dtype=jnp.int32)
-    select = (every[:, None] == slots[None, :]).astype(brief)
-    spread = matmul("sr,kfr->ksf", select, arrived).astype(brief)
-    spread = spread.reshape(2, peers, slot_rows, width).transpose(1, 0, 2, 3)
+    arrived = jnp.concatenate(
+        [lax.dynamic_index_in_dim(third_trip, at, 0, keepdims=False)[:width] for at in behind],
+        axis=1,
+    )
+
+    at = slots // slot_rows * (2 * slot_rows) + slots % slot_rows
+    at = jnp.concatenate([at, at + slot_rows])
+    every = jnp.arange(peers * 2 * slot_rows, dtype=jnp.int32)
+    select = (every[:, None] == at[None, :]).astype(brief)
+    spread = matmul("sr,fr->sf", select, arrived).astype(brief)
     spread = spread.reshape(peers, 2 * slot_rows, width)
     spread, third_trip = lax.optimization_barrier((spread, third_trip))
     final = swap(spread, PEER)

time: 158 us -> 156 us (0.987)
  blocking collectives: 38.6 us -> 89.1 us
  waiting for transfers between devices: 55.7 us -> 17.4 us
  starting transfers between devices: 46.4 us -> 35.6 us
  local copies, waits for them, and re-layouts: 3.42 us -> 1.79 us
    all_to_all x1 -> x3, blocking collectives: 32.2 us -> 82.7 us  [swap(): return lax.all_to_all(blocks, axis, split_axis=0, concat_axis=0, tiled=True)]
    all_to_all x4 -> x2, waiting for transfers between devices: 55.1 us -> 16.7 us  [swap(): return lax.all_to_all(blocks, axis, split_axis=0, concat_axis=0, tiled=True)]
    all_to_all x4 -> x2, starting transfers between devices: 37.6 us -> 26.8 us  [swap(): return lax.all_to_all(blocks, axis, split_axis=0, concat_axis=0, tiled=True)]
    unnamed x14 -> x10, local copies, waits for them, and re-layouts: 1.63 us -> 0.03 us
  transfers between devices with their start and end apart: 7 -> 5, of which waited for: 5 -> 3; matrix products, arithmetic and copies ran while one was open for 3% -> 3% of each run, Pallas kernels for 1% -> 1%
where the time goes in v5:
time: 156 us
  blocking collectives  89.1 us (57%)
  starting transfers between devices  35.6 us (23%)
  waiting for transfers between devices  17.4 us (11%)
  Pallas kernels  5.4 us (3%)
  other arithmetic  4.41 us (3%)
  local copies, waits for them, and re-layouts  1.79 us (1%)
  between operations  1.6 us (1%)
    all_to_all x3, blocking collectives, swap(): return lax.all_to_all(blocks, axis, split_axis=0, concat_axis=0, tiled=True)  82.7 us
    all_to_all x2, starting transfers between devices, swap(): return lax.all_to_all(blocks, axis, split_axis=0, concat_axis=0, tiled=True)  26.8 us
    all_to_all x2, waiting for transfers between devices, swap(): return lax.all_to_all(blocks, axis, split_axis=0, concat_axis=0, tiled=True)  16.7 us
    ppermute x3, starting transfers between devices, moved(): lax.ppermute(block, axis, [(i, (i + distance) % count) for i in range(cou...  8.77 us
    pallas_call x6, Pallas kernels, on_core(): pl.pallas_call(kernel, out_shape=out_shape, in_specs=[pl.BlockSpec(memory...  5.4 us
    all_gather x1, blocking collectives, body(): lax.all_gather(cols, 'core', axis=0)  3.73 us
  transfers between devices with their start and end apart: 5, of which 3 were waited for; matrix products, arithmetic and copies ran while one was open for 3% of the time, Pallas kernels for 1%

profile of v5, /device:TPU:1, one launch (start us, length us, event | category | flops | bytes accessed | tf_op | source)
XLA Modules:
  0.0 155.7 jit_solution(11684200125437614343)
XLA Ops:
  0.6 0.0 copy-start.1
  0.6 1.6 %shard_map.119 = bf16[32,8,160]{2,1,0:T(8,128)(2,1)} custom-call(bf16[1,1,2,2,5120]{4,3,2,1,0:T(2,128)(2,1)} %acts_ref.1, bf16[1,1,2,2,5120]{4,3,2,1,0:T(2,128)(2,1)} %cotan_ref.1), custom_call_target="tpu_custom_call" | custom-call | bytes 163840 | tf_op jit(solution)/shard_map/pallas_call | solution.py:48
  2.3 16.5 %all-to-all-start = ((bf16[32,8,160]{2,1,0:T(8,128)(2,1)}), bf16[32,8,160]{2,1,0:T(8,128)(2,1)S(1)}, u32[]{:S(2)}, u32[]{:S(2)}) async-start(bf16[32,8,160]{2,1,0:T(8,128)(2,1)} %shard_map.119), calls=%async_computation | async-start | bytes 262144 | tf_op jit(solution)/shard_map/all_to_all | solution.py:26
  18.8 2.9 %collective-permute-start = (bf16[80,2560]{1,0:T(8,128)(2,1)}, bf16[80,2560]{1,0:T(8,128)(2,1)S(1)}, u32[]{:S(2)}, u32[]{:S(2)}) collective-permute-start(bf16[80,2560]{1,0:T(8,128)(2,1)} %bitcast.68), channel_id=1, source_target_pairs={{0,1},{1,0},{2,3},{3,2},{4,5},{5,4},{6,7},{7,6},{8,9},{9,8},{10,11... | collective-permute-start | bytes 1228808 | tf_op jit(solution)/shard_map/ppermute | solution.py:31
  21.7 0.7 fusion.29
  22.4 0.1 convert_reduce_fusion.2
  22.5 0.7 add_multiply_fusion
  23.1 0.1 iota_add_fusion
  23.2 0.1 add.126
  23.4 0.8 fusion.31
  24.1 6.1 %all-to-all-done = bf16[32,8,160]{2,1,0:T(8,128)(2,1)S(1)} async-done(((bf16[32,8,160]{2,1,0:T(8,128)(2,1)}), bf16[32,8,160]{2,1,0:T(8,128)(2,1)S(1)}, u32[]{:S(2)}, u32[]{:S(2)}) %all-to-all-start) | async-done | bytes 81952 | tf_op jit(solution)/shard_map/all_to_all | solution.py:26
  30.3 0.1 broadcast_in_dim.15
  30.4 3.7 %all-gather = bf16[64,8,160]{2,1,0:T(8,128)(2,1)S(1)} all-gather(bf16[32,8,160]{2,1,0:T(8,128)(2,1)S(1)} %all-to-all-done), channel_id=2, replica_groups=mesh['section'=8,'chip'=32,'core'=2] {'core'}, dimensions={0}, use_global_device_ids=true | all-gather | bytes 245760 | tf_op jit(solution)/shard_map/all_gather | solution.py:260
  34.1 0.0 collective-permute-done.other_weight_ref
  34.1 0.0 copy-done.1
  34.1 0.8 shard_map.120
  34.9 0.0 copy-start
  34.9 32.2 %all_to_all.25.trip_ref.mine_ref = bf16[32,120,128]{2,1,0:T(8,128)(2,1)S(1)} all-to-all(bf16[32,120,128]{2,1,0:T(8,128)(2,1)S(1)} %get-tuple-element.42), channel_id=1, replica_groups=mesh['section'=8,'chip'=32,'core'=2] {'chip'}, dimensions={0} | all-to-all | bytes 1966080 | tf_op jit(solution)/shard_map/all_to_all | solution.py:26
  67.1 0.0 copy-start.2
  67.1 4.0 %collective-permute-start.2 = (bf16[32,120,128]{2,1,0:T(8,128)(2,1)S(1)}, bf16[32,120,128]{2,1,0:T(8,128)(2,1)S(1)}, u32[]{:S(2)}, u32[]{:S(2)}) collective-permute-start(bf16[32,120,128]{2,1,0:T(8,128)(2,1)S(1)} %all_to_all.25.trip_ref.mine_ref), channel_id=1, source_target_pairs={{0,1},{1,0},{2,3},{3,2},{4,5},{5,4},{6,7},{7,6},{8,9},{9,8},{10,11... | collective-permute-start | bytes 2949128 | tf_op jit(solution)/shard_map/ppermute | solution.py:31
  71.1 0.0 copy-done
  71.1 0.6 shard_map.121
  71.7 1.9 %collective-permute-start.1 = (bf16[32,80,128]{2,1,0:T(8,128)(2,1)S(1)}, bf16[32,80,128]{2,1,0:T(8,128)(2,1)S(1)}, u32[]{:S(2)}, u32[]{:S(2)}) collective-permute-start(bf16[32,80,128]{2,1,0:T(8,128)(2,1)S(1)} %get-tuple-element.44), channel_id=1, source_target_pairs={{0,1},{1,0},{2,3},{3,2},{4,5},{5,4},{6,7},{7,6},{8,9},{9,8},{10,11... | collective-permute-start | bytes 1966088 | tf_op jit(solution)/shard_map/ppermute | solution.py:31
  73.6 0.0 collective-permute-done.2.other_ref
  73.6 0.0 copy-done.2
  73.6 1.4 shard_map.122
  75.0 0.7 collective-permute-done.1.arrived_ref
  75.7 0.2 shard_map.123
  75.9 40.7 %all_to_all.26 = bf16[32,128,128]{2,1,0:T(8,128)(2,1)S(1)} all-to-all(bf16[32,128,128]{2,1,0:T(8,128)(2,1)S(1)} %shard_map.123), channel_id=1, replica_groups=mesh['section'=8,'chip'=32,'core'=2] {'chip'}, dimensions={0} | all-to-all | bytes 2097152 | tf_op jit(solution)/shard_map/all_to_all | solution.py:26
  116.6 0.1 convert_reduce_fusion
  116.8 2.6 %all-gather.1 = bf16[32,96,128]{2,1,0:T(8,128)(2,1)S(1)} all-gather(bf16[32,48,128]{2,1,0:T(8,128)(2,1)S(1)} %slice.38), channel_id=3, replica_groups=mesh['section'=8,'chip'=32,'core'=2] {'core'}, dimensions={1}, use_global_device_ids=true | all-gather | bytes 1179648 | tf_op jit(solution)/shard_map/all_gather | solution.py:310
  119.4 0.1 convert_reduce_fusion.1
  119.4 0.1 slice.49
  119.6 0.3 fusion.1
  119.8 0.0 copy-start.3
  119.9 0.0 copy-start.4
  120.0 9.8 %all_to_all.27 = bf16[8,88,128]{2,1,0:T(8,128)(2,1)S(1)} all-to-all(bf16[8,88,128]{2,1,0:T(8,128)(2,1)S(1)} %fusion.20), channel_id=1, replica_groups=mesh['section'=8,'chip'=32,'core'=2] {'section'}, dimensions={0} | all-to-all | bytes 360448 | tf_op jit(solution)/shard_map/all_to_all | solution.py:26
  129.9 0.2 convolution_convert_fusion
  130.1 0.8 copy.16
  130.8 0.6 convert_reduce_fusion.3
  132.1 10.3 %all-to-all-start.4 = ((bf16[64,8,80]{2,1,0:T(8,128)(2,1)}), bf16[64,8,80]{2,1,0:T(8,128)(2,1)S(1)}, u32[]{:S(2)}, u32[]{:S(2)}) async-start(bf16[64,8,80]{2,1,0:T(8,128)(2,1)} %bitcast.15), calls=%async_computation.4 | async-start | bytes 262144 | tf_op jit(solution)/shard_map/all_to_all | solution.py:26
  142.4 0.0 copy-done.3
  142.4 0.0 copy-done.4
  142.4 1.9 %fusion.9 = (f32[1,40,5120]{2,1,0:T(8,128)}, bf16[1,40,5120]{2,1,0:T(8,128)(2,1)}, f32[1,40,5120]{2,1,0:T(8,128)}) fusion(f32[40,5120]{1,0:T(8,128)S(1)} %get-tuple-element.72, f32[]{:T(128)S(6)} %min.3, f32[1,40,5120]{2,1,0:T(8,128)S(1)} %copy-done.3, f32[1,40,5120]{2,1,0:T(8,128)S(1)} %copy-done.4, bf16[1,40,5120]{2,1,0:T(8,128)(2,1)S(1)} %copy-done), kind=kLoop, calls=%fused_computation.18 | loop fusion | flops 3276800 | bytes 4915204 | tf_op jit(solution)/shard_map/broadcast_in_dim | solution.py:361
  144.3 10.6 %all-to-all-done.4.trip_ref = bf16[64,8,80]{2,1,0:T(8,128)(2,1)S(1)} async-done(((bf16[64,8,80]{2,1,0:T(8,128)(2,1)}), bf16[64,8,80]{2,1,0:T(8,128)(2,1)S(1)}, u32[]{:S(2)}, u32[]{:S(2)}) %all-to-all-start.4) | async-done | bytes 81952 | tf_op jit(solution)/shard_map/all_to_all | solution.py:26
  155.0 0.8 shard_map.124
  (14 shorter events, 0.2 us)
Async XLA Ops:
  0.6 33.5 %copy-start.1 = (bf16[1,80,2560]{2,1,0:T(8,128)(2,1)S(1)}, bf16[1,80,2560]{2,1,0:T(8,128)(2,1)}, u32[]{:S(2)}) copy-start(bf16[1,80,2560]{2,1,0:T(8,128)(2,1)} %param.13) | copy-start | bytes 1228804
  2.3 28.0 %all-to-all-start = ((bf16[32,8,160]{2,1,0:T(8,128)(2,1)}), bf16[32,8,160]{2,1,0:T(8,128)(2,1)S(1)}, u32[]{:S(2)}, u32[]{:S(2)}) async-start(bf16[32,8,160]{2,1,0:T(8,128)(2,1)} %shard_map.119), calls=%async_computation | async-start | bytes 262144 | tf_op jit(solution)/shard_map/all_to_all | solution.py:26
  18.8 15.3 %collective-permute-start = (bf16[80,2560]{1,0:T(8,128)(2,1)}, bf16[80,2560]{1,0:T(8,128)(2,1)S(1)}, u32[]{:S(2)}, u32[]{:S(2)}) collective-permute-start(bf16[80,2560]{1,0:T(8,128)(2,1)} %bitcast.68), channel_id=1, source_target_pairs={{0,1},{1,0},{2,3},{3,2},{4,5},{5,4},{6,7},{7,6},{8,9},{9,8},{10,11... | collective-permute-start | bytes 1228808 | tf_op jit(solution)/shard_map/ppermute | solution.py:31
  34.9 36.2 %copy-start = (bf16[1,40,5120]{2,1,0:T(8,128)(2,1)S(1)}, bf16[1,40,5120]{2,1,0:T(8,128)(2,1)}, u32[]{:S(2)}) copy-start(bf16[1,40,5120]{2,1,0:T(8,128)(2,1)} %param.12) | copy-start | bytes 1228804
  67.1 6.5 %copy-start.2 = (bf16[1,5120]{1,0:T(2,128)(2,1)S(1)}, bf16[1,5120]{1,0:T(2,128)(2,1)}, u32[]{:S(2)}) copy-start(bf16[1,5120]{1,0:T(2,128)(2,1)} %gain_ref.1) | copy-start | bytes 30724
  67.1 6.5 %collective-permute-start.2 = (bf16[32,120,128]{2,1,0:T(8,128)(2,1)S(1)}, bf16[32,120,128]{2,1,0:T(8,128)(2,1)S(1)}, u32[]{:S(2)}, u32[]{:S(2)}) collective-permute-start(bf16[32,120,128]{2,1,0:T(8,128)(2,1)S(1)} %all_to_all.25.trip_ref.mine_ref), channel_id=1, source_target_pairs={{0,1},{1,0},{2,3},{3,2},{4,5},{5,4},{6,7},{7,6},{8,9},{9,8},{10,11... | collective-permute-start | bytes 2949128 | tf_op jit(solution)/shard_map/ppermute | solution.py:31
  71.7 4.0 %collective-permute-start.1 = (bf16[32,80,128]{2,1,0:T(8,128)(2,1)S(1)}, bf16[32,80,128]{2,1,0:T(8,128)(2,1)S(1)}, u32[]{:S(2)}, u32[]{:S(2)}) collective-permute-start(bf16[32,80,128]{2,1,0:T(8,128)(2,1)S(1)} %get-tuple-element.44), channel_id=1, source_target_pairs={{0,1},{1,0},{2,3},{3,2},{4,5},{5,4},{6,7},{7,6},{8,9},{9,8},{10,11... | collective-permute-start | bytes 1966088 | tf_op jit(solution)/shard_map/ppermute | solution.py:31
  119.8 22.6 %copy-start.3 = (f32[1,40,5120]{2,1,0:T(8,128)S(1)}, f32[1,40,5120]{2,1,0:T(8,128)}, u32[]{:S(2)}) copy-start(f32[1,40,5120]{2,1,0:T(8,128)} %param.15) | copy-start | bytes 2457604
  119.9 22.6 %copy-start.4 = (f32[1,40,5120]{2,1,0:T(8,128)S(1)}, f32[1,40,5120]{2,1,0:T(8,128)}, u32[]{:S(2)}) copy-start(f32[1,40,5120]{2,1,0:T(8,128)} %param.14) | copy-start | bytes 2457604
  132.1 22.8 %all-to-all-start.4 = ((bf16[64,8,80]{2,1,0:T(8,128)(2,1)}), bf16[64,8,80]{2,1,0:T(8,128)(2,1)S(1)}, u32[]{:S(2)}, u32[]{:S(2)}) async-start(bf16[64,8,80]{2,1,0:T(8,128)(2,1)} %bitcast.15), calls=%async_computation.4 | async-start | bytes 262144 | tf_op jit(solution)/shard_map/all_to_all | solution.py:26

commit v6 on v1

v6 whole, which is shorter than its diff:
```python
import functools

import jax
import jax.numpy as jnp
from jax import lax
from jax.experimental import pallas as pl
from jax.experimental.pallas import tpu as pltpu
from jax.sharding import Mesh, PartitionSpec as P

NORM_EPS = 1e-05
CLIP_NORM = 1.0
LEARN_RATE = 0.001
BETA_ONE = 0.9
BETA_TWO = 0.95
ADAM_EPS = 1e-08
DECAY = 0.1
CHIP = ("far", "pair", "line")
PEER = CHIP + ("core",)
TEAM = ("far", "line")
SPARE = 8
LANES = 128


def swap(blocks, axis):
    return lax.all_to_all(blocks, axis, split_axis=0, concat_axis=0, tiled=True)


def moved(block, axis):
    return lax.ppermute(block, axis, [(0, 1), (1, 0)])


def product(left, right, contract):
    dims = (((contract[0],), (contract[1],)), ((), ()))
    return lax.dot_general(left, right, dims, preferred_element_type=jnp.float32)


def turned(values):
    return pltpu.roll(values, values.shape[1] // 2, 1)


def in_low(shape):
    return lax.broadcasted_iota(jnp.int32, shape, 1) < shape[1] // 2


def pieces_apart(packed, first_pair):
    low, other = in_low(packed.shape), turned(packed)
    ahead, behind = jnp.where(first_pair, packed, other), jnp.where(first_pair, other, packed)
    zero = jnp.zeros_like(packed)
    own = jnp.where(low, ahead, zero), jnp.where(low, zero, behind)
    partner = jnp.where(low, behind, zero), jnp.where(low, zero, ahead)
    return own, partner


def by_pieces(weight_refs, packed_ref, first_pair):
    span = packed_ref.shape[0] // 2
    results = []
    for ref in weight_refs:
        low, high = (
            sum(
                product(
                    ref[:, (2 * far + piece) * span : (2 * far + piece + 1) * span],
                    packed_ref[far * span : (far + 1) * span, :],
                    (1, 0),
                )
                for far in range(2)
            )
            for piece in range(2)
        )
        joined = jnp.where(in_low(low.shape), low, high)
        results.append(joined + turned(joined))
    own, partner = results
    low = in_low(own.shape)
    ahead, behind = jnp.where(first_pair, own, partner), jnp.where(first_pair, partner, own)
    return jnp.where(low, ahead, behind)


def parts_of(values):
    high = lax.reduce_precision(values, 8, 7)
    middle = lax.reduce_precision(values - high, 8, 7)
    return [high, middle, values - high - middle]


def as_rows(parts, shape):
    line = lax.broadcasted_iota(jnp.int32, shape, 0)
    rows = jnp.zeros(shape, jnp.float32)
    for index, part in enumerate(parts):
        rows = jnp.where(line == index, part, rows)
    return rows


def split_kernel(acts_ref, cotan_ref, out_ref, acts_here, cotan_here, arrived):
    chips, _, width = out_ref.shape
    pairs = ((acts_ref, acts_here), (cotan_ref, cotan_here))
    copies = [pltpu.make_async_copy(a, b, arrived.at[n]) for n, (a, b) in enumerate(pairs)]
    for copy in copies:
        copy.start()
    for copy in copies:
        copy.wait()
    capacity = acts_here.shape[2]
    held = [ref[0, 0, slot] for ref in (acts_here, cotan_here) for slot in range(capacity)]
    held = jnp.concatenate([rows.astype(jnp.float32) for rows in held], axis=0)
    half, lines = width // 2, chips // 4
    for far in range(2):
        for line in range(lines):
            at = [((2 * far + piece) * lines + line) * half for piece in range(2)]
            both = jnp.concatenate([held[:, a : a + half] for a in at], axis=1).astype(jnp.bfloat16)
            for pair in range(2):
                out_ref[(2 * far + pair) * lines + line] = both


def store_by_core(part, first_core, chip, width, mine_ref, other_ref):
    for local in range(part.shape[0] // (2 * width)):
        low = part[2 * local * width : (2 * local + 1) * width]
        high = part[(2 * local + 1) * width : (2 * local + 2) * width]
        mine_ref[chip + local] = jnp.where(first_core, low, high).astype(jnp.bfloat16)
        other_ref[chip + local] = jnp.where(first_core, high, low).astype(jnp.bfloat16)


def partial_sums(weight_refs, packed, first_core, first_pair, width, mine_ref, other_ref):
    own, partner = pieces_apart(packed, first_pair)
    own, partner = ([half.astype(jnp.bfloat16) for half in halves] for halves in (own, partner))
    span = weight_refs[0].shape[1] // 4
    for far in range(2):
        part = 0.0
        for piece in range(2):
            at = (2 * far + piece) * span
            for ref, halves in zip(weight_refs, (own, partner)):
                part = part + product(ref[:, at : at + span], halves[piece], (0, 0))
        chip = far * (mine_ref.shape[0] // 2)
        store_by_core(part, first_core, chip, width, mine_ref, other_ref)


def features_kernel(
    heads, core_ref, pair_ref, cols_ref, at_ref, weight_ref, partner_ref,
    mine_ref, other_ref, stream_ref, cotangent_ref,
):
    width, rows = stream_ref.shape
    slot_rows = cols_ref.shape[0] // (8 * mine_ref.shape[0])
    first_core, first_pair = core_ref[0] == 0, pair_ref[0] == 0
    line = lax.broadcasted_iota(jnp.int32, (cols_ref.shape[0], rows), 0)
    cols = cols_ref[...]

    def picked(first):
        total = 0.0
        for piece in range(2):
            select = (line == at_ref[piece : piece + 1, :] + first).astype(jnp.float32)
            both = product(cols, select.astype(jnp.bfloat16), (0, 0))
            total = total + both[2 * piece * width : 2 * (piece + 1) * width]
        return jnp.where(first_core, total[:width], total[width:])

    stream, cotangent = picked(0), picked(slot_rows)
    stream_ref[...] = stream.astype(jnp.bfloat16)
    cotangent_ref[...] = cotangent.astype(jnp.bfloat16)
    refs = (weight_ref, partner_ref)
    partial_sums(refs, cotangent, first_core, first_pair, heads, mine_ref, other_ref)


def payload_kernel(sums_at, own_at, mine_ref, arrived_ref, own_ref, out_ref):
    own = own_ref[...]
    count = mine_ref.shape[1]
    for chip in range(mine_ref.shape[0]):
        block = mine_ref[chip].astype(jnp.float32) + arrived_ref[chip].astype(jnp.float32)
        out_ref[chip, sums_at : sums_at + count, :] = block.astype(jnp.bfloat16)
        out_ref[chip, own_at : own_at + own.shape[0], :] = own


def dnormed_kernel(
    width, heads, core_ref, pair_ref, trip_ref, weight_ref, partner_ref,
    grads_ref, mine_ref, other_ref,
):
    total = trip_ref[0, width : width + heads, :].astype(jnp.float32)
    for chip in range(1, trip_ref.shape[0]):
        total += trip_ref[chip, width : width + heads, :].astype(jnp.float32)
    grads = total.astype(jnp.bfloat16)
    grads_ref[...] = grads
    first_core, first_pair = core_ref[0] == 0, pair_ref[0] == 0
    refs = (weight_ref, partner_ref)
    grads = grads.astype(jnp.float32)
    partial_sums(refs, grads, first_core, first_pair, width, mine_ref, other_ref)


def values_kernel(
    width, heads, core_ref, pair_ref, mine_ref, other_ref, gain_ref, weight_ref, partner_ref,
    grads_ref, own_ref, gradient_ref, partner_gradient_ref, inverse_ref, normed_ref,
):
    chips, _, lanes = mine_ref.shape
    first_core, first_pair = core_ref[0] == 0, pair_ref[0] == 0
    squares = jnp.zeros((width, lanes), jnp.float32)
    for chip in range(chips):
        for ref in (mine_ref, other_ref):
            block = ref[chip, :width, :].astype(jnp.float32)
            squares += block * block
    total = jnp.broadcast_to(jnp.sum(squares, axis=0, keepdims=True), (SPARE, lanes))
    inverses = lax.rsqrt((total + turned(total)) / gain_ref.shape[1] + NORM_EPS)
    inverse_ref[...] = inverses
    inverse = inverses[0:1]
    span = gain_ref.shape[1] // 4
    lines = chips // 2
    top = lax.broadcasted_iota(jnp.int32, (16, lanes), 0) == 0
    low = in_low((16, lanes))
    ones = [jnp.where(top & (low == (piece == 0)), 1.0, 0.0).astype(jnp.bfloat16) for piece in range(2)]
    for far in range(2):
        gains = 0.0
        for piece in range(2):
            at = (2 * far + piece) * span
            rows = jnp.broadcast_to(gain_ref[:, at : at + span], (16, span))
            gains = gains + product(rows, ones[piece], (0, 0))
        for line in range(lines):
            mine, other = (ref[far * lines + line, :width, :] for ref in (mine_ref, other_ref))
            near, beyond = jnp.where(first_core, mine, other), jnp.where(first_core, other, mine)
            for core, block in ((0, near), (1, beyond)):
                at = (2 * line + core) * width
                scaled = block.astype(jnp.float32) * inverse * gains[at : at + width]
                normed_ref[pl.ds(far * span + at, width), :] = scaled.astype(jnp.bfloat16)
    values = by_pieces((weight_ref, partner_ref), normed_ref, first_pair)
    grads = grads_ref[...].astype(jnp.float32)
    own, partner = pieces_apart(grads, first_pair)
    for piece in range(2):
        both = jnp.concatenate([own[piece], partner[piece]], axis=0).astype(jnp.bfloat16)
        for far in range(2):
            block = product(both, normed_ref[far * span : (far + 1) * span, :], (1, 1))
            at = (2 * far + piece) * span
            gradient_ref[:, at : at + span] = block[:heads]
            partner_gradient_ref[:, at : at + span] = block[heads:].astype(jnp.bfloat16)
    inner = jnp.broadcast_to(jnp.sum(grads * values, axis=0, keepdims=True), (SPARE, lanes))
    inner = inner + turned(inner)
    extra = as_rows(parts_of(inner), (SPARE, lanes))
    own_ref[...] = jnp.concatenate([values, extra], axis=0).astype(jnp.bfloat16)


def gradient_kernel(mine_ref, arrived_ref, gradient_ref, norms_ref):
    lanes = norms_ref.shape[1]
    norms = jnp.zeros((mine_ref.shape[0], lanes), jnp.float32)
    for at in range(0, mine_ref.shape[1], lanes):
        block = mine_ref[:, at : at + lanes] + arrived_ref[:, at : at + lanes].astype(jnp.float32)
        gradient_ref[:, at : at + lanes] = block
        norms += block * block
    norms_ref[...] = jnp.broadcast_to(jnp.sum(norms, axis=0, keepdims=True), norms_ref.shape)


def finish_kernel(
    model, pair_ref, ahead_ref, trip_ref, values_ref, extra_ref, weight_ref, partner_ref, stream_ref,
    cotangent_ref, gain_ref, inverse_ref, norms_ref, out_ref,
):
    width, lanes = stream_ref.shape
    first_pair = pair_ref[0] == 0
    norm_grads = trip_ref[0, :width, :].astype(jnp.float32)
    for chip in range(1, trip_ref.shape[0]):
        norm_grads += trip_ref[chip, :width, :].astype(jnp.float32)
    inner = (extra_ref[0:1] + extra_ref[1:2] + extra_ref[2:3]) / model
    inverse = inverse_ref[0:1]
    stream = stream_ref[...].astype(jnp.float32)
    outputs = stream + by_pieces((weight_ref, partner_ref), values_ref, first_pair)
    units = stream * inverse
    back = cotangent_ref[...].astype(jnp.float32)
    back = back + inverse * (norm_grads * gain_ref[...] - units * inner)
    extra = as_rows(parts_of(norms_ref[0:1]), (SPARE, lanes))
    outputs, back = (
        jnp.concatenate([block, extra], axis=0).astype(jnp.bfloat16) for block in (outputs, back)
    )
    for section in range(out_ref.shape[0]):
        out_ref[section] = jnp.where(ahead_ref[0] == section, outputs, back)


def spread_kernel(width, from_ref, trip_ref, code_ref, out_ref):
    rows = trip_ref.shape[2]
    blocks = [trip_ref[from_ref[index], :width, :] for index in range(2)]
    blocks = jnp.concatenate(blocks, axis=1)
    blocks = jnp.concatenate([blocks, jnp.zeros((LANES - width, 2 * rows), jnp.bfloat16)], axis=0)
    line = lax.broadcasted_iota(jnp.int32, (out_ref.shape[0], 2 * rows), 0)
    select = (line == code_ref[...]).astype(jnp.float32).astype(jnp.bfloat16)
    spread = product(select, blocks, (1, 1))
    total = jnp.zeros((SPARE, rows), jnp.float32)
    for section in range(trip_ref.shape[0]):
        total += trip_ref[section, width:, :].astype(jnp.float32)
    total = jnp.sum(jnp.sum(total, axis=0, keepdims=True), axis=1, keepdims=True)
    lane = lax.broadcasted_iota(jnp.int32, (1, LANES), 1)
    for index, part in enumerate(parts_of(total)):
        spread = spread + jnp.where(lane == width + index, part, 0.0)
    out_ref[...] = spread.astype(jnp.bfloat16)


def join_kernel(width, trip_ref, passed_ref, returned_ref, total_ref, rows_ref):
    _, _, capacity, micro_rows, model = passed_ref.shape
    lines = trip_ref.shape[0] // 8
    slots = 2 * capacity * micro_rows
    norms = jnp.zeros((1, LANES), jnp.float32)
    for far in range(2):
        for at in range(2 * lines):
            peers = [(2 * far + pair) * 2 * lines + at for pair in range(2)]
            block = trip_ref[peers[0]].astype(jnp.float32) + trip_ref[peers[1]].astype(jnp.float32)
            norms += block[0:1]
            for piece in range(2):
                first = ((2 * far + piece) * 2 * lines + at) * width
                rows_ref[:, first : first + width] = block[piece * slots : (piece + 1) * slots, :width]
    lane = lax.broadcasted_iota(jnp.int32, (1, LANES), 1)
    inside = (lane >= width) & (lane < width + 3)
    total = jnp.sum(jnp.where(inside, norms, 0.0), axis=1, keepdims=True)
    total_ref[...] = jnp.broadcast_to(total, total_ref.shape)
    at = 0
    for ref in (passed_ref, returned_ref):
        for slot in range(capacity):
            ref[0, 0, slot] = rows_ref[at : at + micro_rows, :].astype(jnp.bfloat16)
            at += micro_rows


def slot_rows_of(placed, capacity, micro_rows):
    ids = jnp.arange(placed.shape[0], dtype=jnp.int32)
    twins = (placed[:, None] == placed[None, :]) & (ids[:, None] < ids[None, :])
    slots = placed * capacity + jnp.sum(twins.astype(jnp.int32), axis=0)
    return (slots[:, None] * micro_rows + jnp.arange(micro_rows, dtype=jnp.int32)).reshape(-1)


def on_core(kernel, out_shape, scalars, arrays, scratch=(), held_in=pltpu.VMEM, limit=24 * 2**20):
    size = sum(a.size * a.dtype.itemsize for a in arrays)
    size += sum(o.size * o.dtype.itemsize for o in out_shape)
    return pl.pallas_call(
        kernel,
        out_shape=out_shape,
        in_specs=[pl.BlockSpec(memory_space=pltpu.SMEM)] * len(scalars)
        + [pl.BlockSpec(memory_space=held_in)] * len(arrays),
        out_specs=[pl.BlockSpec(memory_space=pltpu.VMEM)] * len(out_shape),
        scratch_shapes=list(scratch),
        compiler_params=pltpu.CompilerParams(vmem_limit_bytes=limit),
        cost_estimate=pl.CostEstimate(flops=0, bytes_accessed=size, transcendentals=0),
    )(*scalars, *arrays)


def body(placing, acts, cotan, gain, w_value, w_out, moment_one, moment_two):
    lines = lax.axis_size("line")
    chips, team = 4 * lines, 2 * lines
    peers = 2 * chips
    sections = lax.axis_size("section")
    section_now, pair_now = lax.axis_index("section"), lax.axis_index("pair")
    far_now, line_now = lax.axis_index("far"), lax.axis_index("line")
    _, _, capacity, micro_rows, model = acts.shape
    slot_rows = capacity * micro_rows
    width = model // peers
    heads = w_value.shape[1]
    rows = peers * micro_rows
    half = rows // 2
    weights, out_weights = w_value[0], w_out[0]
    brief, full = jnp.bfloat16, jnp.float32
    core = lax.axis_index("core").astype(jnp.int32).reshape(1)
    pair = pair_now.astype(jnp.int32).reshape(1)

    def shape(dims, kind=brief):
        return jax.ShapeDtypeStruct(dims, kind)

    (held,) = on_core(
        split_kernel,
        [shape((chips, 2 * slot_rows, 4 * width))],
        [],
        [acts, cotan],
        [pltpu.VMEM(acts.shape, brief), pltpu.VMEM(cotan.shape, brief), pltpu.SemaphoreType.DMA((2,))],
        held_in=pl.ANY,
        limit=None,
    )
    pair_out_weights, pair_weights = moved(out_weights, "pair"), moved(weights, "pair")
    cols = swap(held, CHIP)
    placed = lax.dynamic_index_in_dim(placing[:, :, 0], section_now, 0, keepdims=False)
    slots = slot_rows_of(placed, capacity, micro_rows)
    slots = lax.dynamic_slice_in_dim(slots, pair_now * half, half, 0)
    holder, place = slots // slot_rows, slots % slot_rows
    at = ((holder % 2) * chips + holder // 2) * (2 * slot_rows) + place
    none = jnp.full_like(at, -(2**20))
    at = jnp.stack([jnp.concatenate([at, none]), jnp.concatenate([none, at])])
    code = holder * (4 * slot_rows) + place
    code = [code + kind * slot_rows + piece * 2 * slot_rows for kind in range(2) for piece in range(2)]
    code = jnp.concatenate(code)[None]
    own_gain = [
        lax.dynamic_slice_in_dim(
            gain[0], ((2 * far_now + piece) * lines + line_now) * 2 * width + core[0] * width, width, 0
        )
        for piece in range(2)
    ]
    own_gain = jnp.concatenate(
        [jnp.broadcast_to(part.astype(full)[:, None], (width, half)) for part in own_gain], axis=1
    )
    cols, at, code, own_gain = lax.optimization_barrier((cols, at, code, own_gain))
    cols = lax.all_gather(cols, "core", axis=0).reshape(peers * 2 * slot_rows, 4 * width)

    mine, other, stream, cotangent = on_core(
        functools.partial(features_kernel, heads),
        [shape((team, heads, rows))] * 2 + [shape((width, rows))] * 2,
        [core, pair],
        [cols, at, out_weights, pair_out_weights],
    )
    arrived = moved(other, "core")
    (payload,) = on_core(
        functools.partial(payload_kernel, width, 0),
        [shape((team, width + heads, rows))],
        [],
        [mine, arrived, stream],
    )
    first_trip = swap(payload, TEAM)
    other_trip = moved(first_trip, "core")
    value_grads, mine, other = on_core(
        functools.partial(dnormed_kernel, width, heads),
        [shape((heads, rows))] + [shape((team, width, rows))] * 2,
        [core, pair],
        [first_trip, weights, pair_weights],
    )
    arrived = moved(other, "core")
    own, gradient, pair_gradient, inverse = on_core(
        functools.partial(values_kernel, width, heads),
        [
            shape((heads + SPARE, rows)),
            shape((heads, model), full),
            shape((heads, model)),
            shape((SPARE, rows), full),
        ],
        [core, pair],
        [first_trip, other_trip, gain, weights, pair_weights, value_grads],
        [pltpu.VMEM((model // 2, rows), brief)],
    )
    (payload,) = on_core(
        functools.partial(payload_kernel, 0, width),
        [shape((team, width + heads + SPARE, rows))],
        [],
        [mine, arrived, own],
    )
    payload, pair_gradient = lax.optimization_barrier((payload, pair_gradient))
    second_trip = swap(payload, TEAM)
    gradient, norms = on_core(
        gradient_kernel,
        [shape((heads, model), full), shape((SPARE, rows), full)],
        [],
        [gradient, moved(pair_gradient, "pair")],
    )
    gathered = lax.all_gather(second_trip[:, width:], "core", axis=1)
    extra = jnp.sum(gathered[:, :, heads:].astype(full), axis=(0, 1))

    ahead = ((section_now + 1) % sections).astype(jnp.int32).reshape(1)
    (both,) = on_core(
        functools.partial(finish_kernel, model),
        [shape((sections, width + SPARE, rows))],
        [pair, ahead],
        [
            second_trip,
            gathered[:, :, :heads].reshape(-1, rows),
            extra,
            out_weights,
            pair_out_weights,
            stream,
            cotangent,
            own_gain,
            inverse,
            norms,
        ],
    )
    third_trip = swap(both, "section")
    behind = jnp.stack([(section_now + sections - 1) % sections, (section_now + 1) % sections])

    (spread,) = on_core(
        functools.partial(spread_kernel, width),
        [shape((peers * 4 * slot_rows, LANES))],
        [behind.astype(jnp.int32)],
        [third_trip, code],
    )
    final = swap(spread.reshape(peers, 4 * slot_rows, LANES), PEER)
    passed, returned, totals = on_core(
        functools.partial(join_kernel, width),
        [shape(acts.shape)] * 2 + [shape((SPARE, LANES), full)],
        [],
        [final],
        [pltpu.VMEM((2 * slot_rows, model), full)],
    )

    clip_scale = jnp.minimum(1.0, CLIP_NORM / jnp.sqrt(totals[0, 0] + 1e-06))
    clipped = gradient * clip_scale
    first = BETA_ONE * moment_one[0] + (1.0 - BETA_ONE) * clipped
    second = BETA_TWO * moment_two[0] + (1.0 - BETA_TWO) * clipped * clipped
    wide = weights.astype(full)
    updated = wide - LEARN_RATE * (first / (jnp.sqrt(second) + ADAM_EPS) + DECAY * wide)
    return passed, returned, updated.astype(brief)[None], first[None], second[None]


def solution(mesh):
    sections, peers = mesh.devices.shape
    fine = Mesh(mesh.devices.reshape(sections, 2, 2, peers // 8, 2), ("section",) + PEER)
    slots = P("section", PEER, None, None, None)
    matrix = P("section", PEER, None)
    return jax.shard_map(
        body,
        mesh=fine,
        in_specs=(P(), slots, slots, P("section", None), matrix, matrix, matrix, matrix),
        out_specs=(slots, slots, matrix, matrix, matrix),
        check_vma=False,
    )
```

time: 206 us -> 184 us (0.89)
  between operations: 20.1 us -> 1.56 us
  blocking collectives: 47.6 us -> 31.8 us
  waiting for transfers between devices: 58.9 us -> 74.6 us
  Pallas kernels: 0 us -> 9.91 us
  other arithmetic: 14 us -> 4.36 us
  starting transfers between devices: 50.4 us -> 56.7 us
  local copies, waits for them, and re-layouts: 9.77 us -> 4.08 us
  matrix products: 4.24 us -> 0 us
    ppermute x2 -> x6, waiting for transfers between devices: 0.01 us -> 49.5 us  [moved(): return lax.ppermute(block, axis, [(0, 1), (1, 0)])]
    all_to_all x4, waiting for transfers between devices: 52.1 us -> 25.2 us  [swap(): return lax.all_to_all(blocks, axis, split_axis=0, concat_axis=0, tiled=True)]
    all_to_all x3 -> x1, blocking collectives: 43.6 us -> 25.2 us  [swap(): return lax.all_to_all(blocks, axis, split_axis=0, concat_axis=0, tiled=True)]
    ppermute x2 -> x6, starting transfers between devices: 5.41 us -> 17.6 us  [moved(): return lax.ppermute(block, axis, [(0, 1), (1, 0)])]
    pallas_call x0 -> x10, Pallas kernels: none -> 9.91 us  [on_core(): pl.pallas_call(kernel, out_shape=out_shape, in_specs=[pl.BlockSpec(memory...]
    all_gather x1 -> x0, waiting for transfers between devices: 6.79 us -> none  [body(): lax.all_gather(first_trip[:, :width], 'core', axis=1).reshape(model, rows)]
    all_to_all x4, starting transfers between devices: 45 us -> 39.1 us  [swap(): return lax.all_to_all(blocks, axis, split_axis=0, concat_axis=0, tiled=True)]
    all_gather x0 -> x1, blocking collectives: none -> 4.45 us  [body(): lax.all_gather(cols, 'core', axis=0)]
  transfers between devices with their start and end apart: 7 -> 10, of which waited for: 5 -> 7; matrix products, arithmetic and copies ran while one was open for 6% -> 1% of each run, Pallas kernels for 0% -> 1%
where the time goes in v6:
time: 184 us; the launch traced here: 183 us
  waiting for transfers between devices  74.6 us (41%)
  starting transfers between devices  56.7 us (31%)
  blocking collectives  31.8 us (17%)
  Pallas kernels  9.91 us (5%)
  other arithmetic  4.36 us (2%)
  local copies, waits for them, and re-layouts  4.08 us (2%)
    ppermute x6, waiting for transfers between devices, moved(): return lax.ppermute(block, axis, [(0, 1), (1, 0)])  49.5 us
    all_to_all x4, starting transfers between devices, swap(): return lax.all_to_all(blocks, axis, split_axis=0, concat_axis=0, tiled=True)  39.1 us
    all_to_all x4, waiting for transfers between devices, swap(): return lax.all_to_all(blocks, axis, split_axis=0, concat_axis=0, tiled=True)  25.2 us
    all_to_all x1, blocking collectives, swap(): return lax.all_to_all(blocks, axis, split_axis=0, concat_axis=0, tiled=True)  25.2 us
    ppermute x6, starting transfers between devices, moved(): return lax.ppermute(block, axis, [(0, 1), (1, 0)])  17.6 us
    pallas_call x10, Pallas kernels, on_core(): pl.pallas_call(kernel, out_shape=out_shape, in_specs=[pl.BlockSpec(memory...  9.91 us
    all_gather x1, blocking collectives, body(): lax.all_gather(cols, 'core', axis=0)  4.45 us
  transfers between devices with their start and end apart: 10, of which 7 were waited for; matrix products, arithmetic and copies ran while one was open for 1% of the time, Pallas kernels for 1%

profile of v6, /device:TPU:1, one launch (start us, length us, event | category | flops | bytes accessed | tf_op | source)
XLA Modules:
  0.0 183.0 jit_solution(8029295963773187104)
XLA Ops:
  0.6 0.0 copy-start.1
  0.6 1.7 shard_map.119
  2.3 16.5 %all-to-all-start = ((bf16[32,8,320]{2,1,0:T(8,128)(2,1)}), bf16[32,8,320]{2,1,0:T(8,128)(2,1)S(1)}, u32[]{:S(2)}, u32[]{:S(2)}) async-start(bf16[32,8,320]{2,1,0:T(8,128)(2,1)} %shard_map.119), calls=%async_computation | async-start | bytes 393216 | tf_op jit(solution)/shard_map/all_to_all | solution.py:25
  18.9 0.0 copy-done.1
  18.9 4.0 %collective-permute-start = (bf16[80,2560]{1,0:T(8,128)(2,1)S(1)}, bf16[80,2560]{1,0:T(8,128)(2,1)S(1)}, u32[]{:S(2)}, u32[]{:S(2)}) collective-permute-start(bf16[80,2560]{1,0:T(8,128)(2,1)S(1)} %bitcast.52), channel_id=1, source_target_pairs={{0,16},{16,0},{1,17},{17,1},{2,18},{18,2},{3,19},{19,3},{4,20},{20... | collective-permute-start | bytes 1228808 | tf_op jit(solution)/shard_map/ppermute | solution.py:29
  22.9 0.7 fusion.8
  23.6 0.1 convert_reduce_fusion.1
  23.7 0.7 add_multiply_fusion
  24.4 0.1 iota_add_fusion
  24.4 0.1 add.134
  24.6 0.0 copy-start.4
  24.6 0.1 broadcast_add_fusion.2
  24.7 0.1 pad_bitcast_fusion.1
  24.8 0.1 pad_add_fusion.1
  24.9 0.4 copy-done.4
  25.3 0.1 fusion.10
  25.4 0.1 broadcast_in_dim.13
  25.5 0.1 broadcast_in_dim.14
  25.5 0.1 pad_maximum_fusion.gain_ref
  25.6 5.1 %all-to-all-done = bf16[32,8,320]{2,1,0:T(8,128)(2,1)S(1)} async-done(((bf16[32,8,320]{2,1,0:T(8,128)(2,1)}), bf16[32,8,320]{2,1,0:T(8,128)(2,1)S(1)}, u32[]{:S(2)}, u32[]{:S(2)}) %all-to-all-start) | async-done | bytes 163872 | tf_op jit(solution)/shard_map/all_to_all | solution.py:25
  30.7 4.4 %all-gather = bf16[64,8,320]{2,1,0:T(8,128)(2,1)S(1)} all-gather(bf16[32,8,320]{2,1,0:T(8,128)(2,1)S(1)} %all-to-all-done), channel_id=2, replica_groups=mesh['section'=8,'far'=2,'pair'=2,'line'=8,'core'=2] {'core'}, dimensions={0}, use_global_device_ids=true | all-gather | bytes 491520 | tf_op jit(solution)/shard_map/all_gather | solution.py:381
  35.2 8.5 %collective-permute-done.partner_ref = bf16[80,2560]{1,0:T(8,128)(2,1)S(1)} collective-permute-done((bf16[80,2560]{1,0:T(8,128)(2,1)S(1)}, bf16[80,2560]{1,0:T(8,128)(2,1)S(1)}, u32[]{:S(2)}, u32[]{:S(2)}) %collective-permute-start) | collective-permute-done | bytes 409632 | tf_op jit(solution)/shard_map/ppermute | solution.py:29
  43.7 1.1 shard_map.120
  44.8 2.7 %collective-permute-start.1 = (bf16[16,40,128]{2,1,0:T(8,128)(2,1)S(1)}, bf16[16,40,128]{2,1,0:T(8,128)(2,1)S(1)}, u32[]{:S(2)}, u32[]{:S(2)}) collective-permute-start(bf16[16,40,128]{2,1,0:T(8,128)(2,1)S(1)} %get-tuple-element.30), channel_id=1, source_target_pairs={{0,1},{1,0},{2,3},{3,2},{4,5},{5,4},{6,7},{7,6},{8,9},{9,8},{10,11... | collective-permute-start | bytes 491528 | tf_op jit(solution)/shard_map/ppermute | solution.py:29
  47.5 1.0 collective-permute-done.1.arrived_ref
  48.5 0.9 shard_map.121
  49.4 0.0 copy-start
  49.4 9.7 %all-to-all-start.1 = ((bf16[16,120,128]{2,1,0:T(8,128)(2,1)}), bf16[16,120,128]{2,1,0:T(8,128)(2,1)S(1)}, u32[]{:S(2)}, u32[]{:S(2)}) async-start(bf16[16,120,128]{2,1,0:T(8,128)(2,1)} %shard_map.121), calls=%async_computation.1 | async-start | bytes 983040 | tf_op jit(solution)/shard_map/all_to_all | solution.py:25
  59.1 0.0 copy-done
  59.1 1.9 %collective-permute-start.2 = (bf16[40,5120]{1,0:T(8,128)(2,1)S(1)}, bf16[40,5120]{1,0:T(8,128)(2,1)S(1)}, u32[]{:S(2)}, u32[]{:S(2)}) collective-permute-start(bf16[40,5120]{1,0:T(8,128)(2,1)S(1)} %bitcast.49), channel_id=1, source_target_pairs={{0,16},{16,0},{1,17},{17,1},{2,18},{18,2},{3,19},{19,3},{4,20},{20... | collective-permute-start | bytes 1228808 | tf_op jit(solution)/shard_map/ppermute | solution.py:29
  61.0 14.3 %all-to-all-done.1.trip_ref.mine_ref = bf16[16,120,128]{2,1,0:T(8,128)(2,1)S(1)} async-done(((bf16[16,120,128]{2,1,0:T(8,128)(2,1)}), bf16[16,120,128]{2,1,0:T(8,128)(2,1)S(1)}, u32[]{:S(2)}, u32[]{:S(2)}) %all-to-all-start.1) | async-done | bytes 491552 | tf_op jit(solution)/shard_map/all_to_all | solution.py:25
  75.3 4.6 %collective-permute-start.4 = (bf16[16,120,128]{2,1,0:T(8,128)(2,1)S(1)}, bf16[16,120,128]{2,1,0:T(8,128)(2,1)S(1)}, u32[]{:S(2)}, u32[]{:S(2)}) collective-permute-start(bf16[16,120,128]{2,1,0:T(8,128)(2,1)S(1)} %all-to-all-done.1.trip_ref.mine_ref), channel_id=1, source_target_pairs={{0,1},{1,0},{2,3},{3,2},{4,5},{5,4},{6,7},{7,6},{8,9},{9,8},{10,11... | collective-permute-start | bytes 1474568 | tf_op jit(solution)/shard_map/ppermute | solution.py:29
  79.9 10.9 %collective-permute-done.2.partner_ref = bf16[40,5120]{1,0:T(8,128)(2,1)S(1)} collective-permute-done((bf16[40,5120]{1,0:T(8,128)(2,1)S(1)}, bf16[40,5120]{1,0:T(8,128)(2,1)S(1)}, u32[]{:S(2)}, u32[]{:S(2)}) %collective-permute-start.2) | collective-permute-done | bytes 409632 | tf_op jit(solution)/shard_map/ppermute | solution.py:29
  90.9 0.9 shard_map.122
  91.8 2.4 %collective-permute-start.3 = (bf16[16,80,128]{2,1,0:T(8,128)(2,1)S(1)}, bf16[16,80,128]{2,1,0:T(8,128)(2,1)S(1)}, u32[]{:S(2)}, u32[]{:S(2)}) collective-permute-start(bf16[16,80,128]{2,1,0:T(8,128)(2,1)S(1)} %get-tuple-element.33), channel_id=1, source_target_pairs={{0,1},{1,0},{2,3},{3,2},{4,5},{5,4},{6,7},{7,6},{8,9},{9,8},{10,11... | collective-permute-start | bytes 983048 | tf_op jit(solution)/shard_map/ppermute | solution.py:29
  94.2 0.0 collective-permute-done.4.other_ref
  94.2 1.5 shard_map.123
  95.8 0.0 copy-start.2
  95.8 0.9 copy-done.2
  96.7 0.0 collective-permute-done.3.arrived_ref
  96.7 0.9 shard_map.124
  97.6 8.7 %all-to-all-start.2 = ((bf16[16,128,128]{2,1,0:T(8,128)(2,1)}), bf16[16,128,128]{2,1,0:T(8,128)(2,1)S(1)}, u32[]{:S(2)}, u32[]{:S(2)}) async-start(bf16[16,128,128]{2,1,0:T(8,128)(2,1)} %shard_map.124), calls=%async_computation.2 | async-start | bytes 1048576 | tf_op jit(solution)/shard_map/all_to_all | solution.py:25
  106.3 1.9 %collective-permute-start.5 = (bf16[40,5120]{1,0:T(8,128)(2,1)S(1)}, bf16[40,5120]{1,0:T(8,128)(2,1)S(1)}, u32[]{:S(2)}, u32[]{:S(2)}) collective-permute-start(bf16[40,5120]{1,0:T(8,128)(2,1)S(1)} %get-tuple-element.42), channel_id=1, source_target_pairs={{0,16},{16,0},{1,17},{17,1},{2,18},{18,2},{3,19},{19,3},{4,20},{20... | collective-permute-start | bytes 1228808 | tf_op jit(solution)/shard_map/ppermute | solution.py:29
  108.2 29.0 %collective-permute-done.5.arrived_ref = bf16[40,5120]{1,0:T(8,128)(2,1)S(1)} collective-permute-done((bf16[40,5120]{1,0:T(8,128)(2,1)S(1)}, bf16[40,5120]{1,0:T(8,128)(2,1)S(1)}, u32[]{:S(2)}, u32[]{:S(2)}) %collective-permute-start.5) | collective-permute-done | bytes 409632 | tf_op jit(solution)/shard_map/ppermute | solution.py:29
  137.2 0.0 copy-start.3
  137.2 1.1 copy-done.3
  138.4 0.1 shard_map.125
  138.5 0.0 all-to-all-done.2.trip_ref
  138.6 2.2 %all-gather.1 = bf16[16,96,128]{2,1,0:T(8,128)(2,1)S(1)} all-gather(bf16[16,48,128]{2,1,0:T(8,128)(2,1)S(1)} %slice.16), channel_id=3, replica_groups=mesh['section'=8,'far'=2,'pair'=2,'line'=8,'core'=2] {'core'}, dimensions={1}, use_global_device_ids=true | all-gather | bytes 589824 | tf_op jit(solution)/shard_map/all_gather | solution.py:431
  140.8 1.2 shard_map.126
  142.0 0.0 copy-start.5
  142.0 4.1 %all-to-all-start.3 = ((bf16[8,88,128]{2,1,0:T(8,128)(2,1)}), bf16[8,88,128]{2,1,0:T(8,128)(2,1)S(1)}, u32[]{:S(2)}, u32[]{:S(2)}) async-start(bf16[8,88,128]{2,1,0:T(8,128)(2,1)} %shard_map.126), calls=%async_computation.3 | async-start | bytes 360448 | tf_op jit(solution)/shard_map/all_to_all | solution.py:25
  146.1 0.1 pad_add_fusion.2.from_ref
  146.2 5.8 %all-to-all-done.3.trip_ref = bf16[8,88,128]{2,1,0:T(8,128)(2,1)S(1)} async-done(((bf16[8,88,128]{2,1,0:T(8,128)(2,1)}), bf16[8,88,128]{2,1,0:T(8,128)(2,1)S(1)}, u32[]{:S(2)}, u32[]{:S(2)}) %all-to-all-start.3) | async-done | bytes 180256 | tf_op jit(solution)/shard_map/all_to_all | solution.py:25
  152.0 0.8 shard_map.127
  152.8 25.2 %all_to_all.25.trip_ref = bf16[64,16,128]{2,1,0:T(8,128)(2,1)S(1)} all-to-all(bf16[64,16,128]{2,1,0:T(8,128)(2,1)S(1)} %bitcast.57), channel_id=1, replica_groups=mesh['section'=8,'far'=2,'pair'=2,'line'=8,'core'=2] {'far','pair','line..., dimensions={0} | all-to-all | bytes 524288 | tf_op jit(solution)/shard_map/all_to_all | solution.py:25
  178.0 0.8 shard_map.128
  178.7 0.5 slice.15
  179.9 0.0 copy-done.5
  180.0 3.1 %fusion.6 = (f32[1,40,5120]{2,1,0:T(8,128)}, bf16[1,40,5120]{2,1,0:T(8,128)(2,1)}, f32[1,40,5120]{2,1,0:T(8,128)}) fusion(f32[40,5120]{1,0:T(8,128)S(1)} %get-tuple-element.47, f32[]{:T(128)} %bitcast.17, f32[1,40,5120]{2,1,0:T(8,128)S(1)} %copy-done.5, f32[1,40,5120]{2,1,0:T(8,128)} %param.14, bf16[1,40,5120]{2,1,0:T(8,128)(2,1)S(1)} %copy-done), kind=kLoop, calls=%fused_computation.10 | loop fusion | flops 3276800 | bytes 4915204 | tf_op jit(solution)/shard_map/broadcast_in_dim | solution.py:476
  (5 shorter events, 0.1 us)
Async XLA Ops:
  0.6 18.2 %copy-start.1 = (bf16[1,80,2560]{2,1,0:T(8,128)(2,1)S(1)}, bf16[1,80,2560]{2,1,0:T(8,128)(2,1)}, u32[]{:S(2)}) copy-start(bf16[1,80,2560]{2,1,0:T(8,128)(2,1)} %param.13) | copy-start | bytes 1228804
  2.3 28.4 %all-to-all-start = ((bf16[32,8,320]{2,1,0:T(8,128)(2,1)}), bf16[32,8,320]{2,1,0:T(8,128)(2,1)S(1)}, u32[]{:S(2)}, u32[]{:S(2)}) async-start(bf16[32,8,320]{2,1,0:T(8,128)(2,1)} %shard_map.119), calls=%async_computation | async-start | bytes 393216 | tf_op jit(solution)/shard_map/all_to_all | solution.py:25
  18.9 24.8 %collective-permute-start = (bf16[80,2560]{1,0:T(8,128)(2,1)S(1)}, bf16[80,2560]{1,0:T(8,128)(2,1)S(1)}, u32[]{:S(2)}, u32[]{:S(2)}) collective-permute-start(bf16[80,2560]{1,0:T(8,128)(2,1)S(1)} %bitcast.52), channel_id=1, source_target_pairs={{0,16},{16,0},{1,17},{17,1},{2,18},{18,2},{3,19},{19,3},{4,20},{20... | collective-permute-start | bytes 1228808 | tf_op jit(solution)/shard_map/ppermute | solution.py:29
  24.6 0.7 copy-start.4
  44.8 3.7 %collective-permute-start.1 = (bf16[16,40,128]{2,1,0:T(8,128)(2,1)S(1)}, bf16[16,40,128]{2,1,0:T(8,128)(2,1)S(1)}, u32[]{:S(2)}, u32[]{:S(2)}) collective-permute-start(bf16[16,40,128]{2,1,0:T(8,128)(2,1)S(1)} %get-tuple-element.30), channel_id=1, source_target_pairs={{0,1},{1,0},{2,3},{3,2},{4,5},{5,4},{6,7},{7,6},{8,9},{9,8},{10,11... | collective-permute-start | bytes 491528 | tf_op jit(solution)/shard_map/ppermute | solution.py:29
  49.4 9.7 %copy-start = (bf16[1,40,5120]{2,1,0:T(8,128)(2,1)S(1)}, bf16[1,40,5120]{2,1,0:T(8,128)(2,1)}, u32[]{:S(2)}) copy-start(bf16[1,40,5120]{2,1,0:T(8,128)(2,1)} %param.12) | copy-start | bytes 1228804
  49.4 25.9 %all-to-all-start.1 = ((bf16[16,120,128]{2,1,0:T(8,128)(2,1)}), bf16[16,120,128]{2,1,0:T(8,128)(2,1)S(1)}, u32[]{:S(2)}, u32[]{:S(2)}) async-start(bf16[16,120,128]{2,1,0:T(8,128)(2,1)} %shard_map.121), calls=%async_computation.1 | async-start | bytes 983040 | tf_op jit(solution)/shard_map/all_to_all | solution.py:25
  59.1 31.8 %collective-permute-start.2 = (bf16[40,5120]{1,0:T(8,128)(2,1)S(1)}, bf16[40,5120]{1,0:T(8,128)(2,1)S(1)}, u32[]{:S(2)}, u32[]{:S(2)}) collective-permute-start(bf16[40,5120]{1,0:T(8,128)(2,1)S(1)} %bitcast.49), channel_id=1, source_target_pairs={{0,16},{16,0},{1,17},{17,1},{2,18},{18,2},{3,19},{19,3},{4,20},{20... | collective-permute-start | bytes 1228808 | tf_op jit(solution)/shard_map/ppermute | solution.py:29
  75.3 18.9 %collective-permute-start.4 = (bf16[16,120,128]{2,1,0:T(8,128)(2,1)S(1)}, bf16[16,120,128]{2,1,0:T(8,128)(2,1)S(1)}, u32[]{:S(2)}, u32[]{:S(2)}) collective-permute-start(bf16[16,120,128]{2,1,0:T(8,128)(2,1)S(1)} %all-to-all-done.1.trip_ref.mine_ref), channel_id=1, source_target_pairs={{0,1},{1,0},{2,3},{3,2},{4,5},{5,4},{6,7},{7,6},{8,9},{9,8},{10,11... | collective-permute-start | bytes 1474568 | tf_op jit(solution)/shard_map/ppermute | solution.py:29
  91.8 4.8 %collective-permute-start.3 = (bf16[16,80,128]{2,1,0:T(8,128)(2,1)S(1)}, bf16[16,80,128]{2,1,0:T(8,128)(2,1)S(1)}, u32[]{:S(2)}, u32[]{:S(2)}) collective-permute-start(bf16[16,80,128]{2,1,0:T(8,128)(2,1)S(1)} %get-tuple-element.33), channel_id=1, source_target_pairs={{0,1},{1,0},{2,3},{3,2},{4,5},{5,4},{6,7},{7,6},{8,9},{9,8},{10,11... | collective-permute-start | bytes 983048 | tf_op jit(solution)/shard_map/ppermute | solution.py:29
  95.8 0.9 copy-start.2
  97.6 41.0 %all-to-all-start.2 = ((bf16[16,128,128]{2,1,0:T(8,128)(2,1)}), bf16[16,128,128]{2,1,0:T(8,128)(2,1)S(1)}, u32[]{:S(2)}, u32[]{:S(2)}) async-start(bf16[16,128,128]{2,1,0:T(8,128)(2,1)} %shard_map.124), calls=%async_computation.2 | async-start | bytes 1048576 | tf_op jit(solution)/shard_map/all_to_all | solution.py:25
  106.3 31.0 %collective-permute-start.5 = (bf16[40,5120]{1,0:T(8,128)(2,1)S(1)}, bf16[40,5120]{1,0:T(8,128)(2,1)S(1)}, u32[]{:S(2)}, u32[]{:S(2)}) collective-permute-start(bf16[40,5120]{1,0:T(8,128)(2,1)S(1)} %get-tuple-element.42), channel_id=1, source_target_pairs={{0,16},{16,0},{1,17},{17,1},{2,18},{18,2},{3,19},{19,3},{4,20},{20... | collective-permute-start | bytes 1228808 | tf_op jit(solution)/shard_map/ppermute | solution.py:29
  137.2 1.1 copy-start.3
  142.0 38.0 %copy-start.5 = (f32[1,40,5120]{2,1,0:T(8,128)S(1)}, f32[1,40,5120]{2,1,0:T(8,128)}, u32[]{:S(2)}) copy-start(f32[1,40,5120]{2,1,0:T(8,128)} %param.15) | copy-start | bytes 2457604
  142.0 10.0 %all-to-all-start.3 = ((bf16[8,88,128]{2,1,0:T(8,128)(2,1)}), bf16[8,88,128]{2,1,0:T(8,128)(2,1)S(1)}, u32[]{:S(2)}, u32[]{:S(2)}) async-start(bf16[8,88,128]{2,1,0:T(8,128)(2,1)} %shard_map.126), calls=%async_computation.3 | async-start | bytes 360448 | tf_op jit(solution)/shard_map/all_to_all | solution.py:25

commit v7 on v6

--- a/solution.py
+++ b/solution.py
@@ -14,9 +14,9 @@
 BETA_TWO = 0.95
 ADAM_EPS = 1e-08
 DECAY = 0.1
-CHIP = ("far", "pair", "line")
+CHIP = ("team", "pair")
 PEER = CHIP + ("core",)
-TEAM = ("far", "line")
+TEAM = "team"
 SPARE = 8
 LANES = 128
 
@@ -44,30 +44,15 @@
 
 def pieces_apart(packed, first_pair):
     low, other = in_low(packed.shape), turned(packed)
-    ahead, behind = jnp.where(first_pair, packed, other), jnp.where(first_pair, other, packed)
-    zero = jnp.zeros_like(packed)
-    own = jnp.where(low, ahead, zero), jnp.where(low, zero, behind)
-    partner = jnp.where(low, behind, zero), jnp.where(low, zero, ahead)
-    return own, partner
-
-
-def by_pieces(weight_refs, packed_ref, first_pair):
-    span = packed_ref.shape[0] // 2
+    first, second = jnp.where(low, packed, other), jnp.where(low, other, packed)
+    return jnp.where(first_pair, first, second), jnp.where(first_pair, second, first)
+
+
+def by_pieces(weight_refs, features, first_pair):
     results = []
     for ref in weight_refs:
-        low, high = (
-            sum(
-                product(
-                    ref[:, (2 * far + piece) * span : (2 * far + piece + 1) * span],
-                    packed_ref[far * span : (far + 1) * span, :],
-                    (1, 0),
-                )
-                for far in range(2)
-            )
-            for piece in range(2)
-        )
-        joined = jnp.where(in_low(low.shape), low, high)
-        results.append(joined + turned(joined))
+        both = product(ref[...], features, (1, 0))
+        results.append(both + turned(both))
     own, partner = results
     low = in_low(own.shape)
     ahead, behind = jnp.where(first_pair, own, partner), jnp.where(first_pair, partner, own)
@@ -99,35 +84,25 @@
     capacity = acts_here.shape[2]
     held = [ref[0, 0, slot] for ref in (acts_here, cotan_here) for slot in range(capacity)]
     held = jnp.concatenate([rows.astype(jnp.float32) for rows in held], axis=0)
-    half, lines = width // 2, chips // 4
-    for far in range(2):
-        for line in range(lines):
-            at = [((2 * far + piece) * lines + line) * half for piece in range(2)]
-            both = jnp.concatenate([held[:, a : a + half] for a in at], axis=1).astype(jnp.bfloat16)
-            for pair in range(2):
-                out_ref[(2 * far + pair) * lines + line] = both
-
-
-def store_by_core(part, first_core, chip, width, mine_ref, other_ref):
-    for local in range(part.shape[0] // (2 * width)):
-        low = part[2 * local * width : (2 * local + 1) * width]
-        high = part[(2 * local + 1) * width : (2 * local + 2) * width]
-        mine_ref[chip + local] = jnp.where(first_core, low, high).astype(jnp.bfloat16)
-        other_ref[chip + local] = jnp.where(first_core, high, low).astype(jnp.bfloat16)
+    for chip in range(chips):
+        at = chip // 2 * width
+        out_ref[chip] = held[:, at : at + width].astype(jnp.bfloat16)
 
 
 def partial_sums(weight_refs, packed, first_core, first_pair, width, mine_ref, other_ref):
-    own, partner = pieces_apart(packed, first_pair)
-    own, partner = ([half.astype(jnp.bfloat16) for half in halves] for halves in (own, partner))
-    span = weight_refs[0].shape[1] // 4
-    for far in range(2):
-        part = 0.0
-        for piece in range(2):
-            at = (2 * far + piece) * span
-            for ref, halves in zip(weight_refs, (own, partner)):
-                part = part + product(ref[:, at : at + span], halves[piece], (0, 0))
-        chip = far * (mine_ref.shape[0] // 2)
-        store_by_core(part, first_core, chip, width, mine_ref, other_ref)
+    pieces = [piece.astype(jnp.bfloat16) for piece in pieces_apart(packed, first_pair)]
+    team, span = mine_ref.shape[0], 4 * width
+    group = min(team, 640 // span)
+    low = in_low((width, packed.shape[1]))
+    for first in range(0, team, group):
+        columns = slice(first * span, (first + group) * span)
+        part = sum(product(ref[:, columns], p, (0, 0)) for ref, p in zip(weight_refs, pieces))
+        for local in range(group):
+            parts = [part[local * span + n * width : local * span + (n + 1) * width] for n in range(4)]
+            near, beyond = jnp.where(low, parts[0], parts[2]), jnp.where(low, parts[1], parts[3])
+            mine, other = jnp.where(first_core, near, beyond), jnp.where(first_core, beyond, near)
+            mine_ref[first + local] = mine.astype(jnp.bfloat16)
+            other_ref[first + local] = other.astype(jnp.bfloat16)
 
 
 def features_kernel(
@@ -194,34 +169,31 @@
     inverses = lax.rsqrt((total + turned(total)) / gain_ref.shape[1] + NORM_EPS)
     inverse_ref[...] = inverses
     inverse = inverses[0:1]
-    span = gain_ref.shape[1] // 4
-    lines = chips // 2
     top = lax.broadcasted_iota(jnp.int32, (16, lanes), 0) == 0
-    low = in_low((16, lanes))
-    ones = [jnp.where(top & (low == (piece == 0)), 1.0, 0.0).astype(jnp.bfloat16) for piece in range(2)]
-    for far in range(2):
-        gains = 0.0
-        for piece in range(2):
-            at = (2 * far + piece) * span
-            rows = jnp.broadcast_to(gain_ref[:, at : at + span], (16, span))
-            gains = gains + product(rows, ones[piece], (0, 0))
-        for line in range(lines):
-            mine, other = (ref[far * lines + line, :width, :] for ref in (mine_ref, other_ref))
+    one = top.astype(jnp.float32).astype(jnp.bfloat16)
+    low = in_low((width, lanes))
+    span = 8 * width
+    for first in range(0, chips, 2):
+        at = first // 2 * span
+        gains = jnp.broadcast_to(gain_ref[:, at : at + span], (16, span))
+        gains = product(gains, one, (0, 0))
+        for local in range(2):
+            mine, other = (ref[first + local, :width, :] for ref in (mine_ref, other_ref))
             near, beyond = jnp.where(first_core, mine, other), jnp.where(first_core, other, mine)
             for core, block in ((0, near), (1, beyond)):
-                at = (2 * line + core) * width
-                scaled = block.astype(jnp.float32) * inverse * gains[at : at + width]
-                normed_ref[pl.ds(far * span + at, width), :] = scaled.astype(jnp.bfloat16)
-    values = by_pieces((weight_ref, partner_ref), normed_ref, first_pair)
+                units = block.astype(jnp.float32) * inverse
+                for piece in range(2):
+                    line = ((local * 2 + piece) * 2 + core) * width
+                    scaled = units * gains[line : line + width]
+                    scaled = jnp.where(low == (piece == 0), scaled, 0.0)
+                    normed_ref[pl.ds(at + line, width), :] = scaled.astype(jnp.bfloat16)
+    values = by_pieces((weight_ref, partner_ref), normed_ref[...], first_pair)
     grads = grads_ref[...].astype(jnp.float32)
-    own, partner = pieces_apart(grads, first_pair)
-    for piece in range(2):
-        both = jnp.concatenate([own[piece], partner[piece]], axis=0).astype(jnp.bfloat16)
-        for far in range(2):
-            block = product(both, normed_ref[far * span : (far + 1) * span, :], (1, 1))
-            at = (2 * far + piece) * span
-            gradient_ref[:, at : at + span] = block[:heads]
-            partner_gradient_ref[:, at : at + span] = block[heads:].astype(jnp.bfloat16)
+    both = jnp.concatenate(pieces_apart(grads, first_pair), axis=0).astype(jnp.bfloat16)
+    for at in range(0, gain_ref.shape[1], span):
+        block = product(both, normed_ref[at : at + span, :], (1, 1))
+        gradient_ref[:, at : at + span] = block[:heads]
+        partner_gradient_ref[:, at : at + span] = block[heads:].astype(jnp.bfloat16)
     inner = jnp.broadcast_to(jnp.sum(grads * values, axis=0, keepdims=True), (SPARE, lanes))
     inner = inner + turned(inner)
     extra = as_rows(parts_of(inner), (SPARE, lanes))
@@ -240,7 +212,7 @@
 
 def finish_kernel(
     model, pair_ref, ahead_ref, trip_ref, values_ref, extra_ref, weight_ref, partner_ref, stream_ref,
-    cotangent_ref, gain_ref, inverse_ref, norms_ref, out_ref,
+    cotangent_ref, gain_ref, inverse_ref, norms_ref, out_ref, features_ref,
 ):
     width, lanes = stream_ref.shape
     first_pair = pair_ref[0] == 0
@@ -250,7 +222,16 @@
     inner = (extra_ref[0:1] + extra_ref[1:2] + extra_ref[2:3]) / model
     inverse = inverse_ref[0:1]
     stream = stream_ref[...].astype(jnp.float32)
-    outputs = stream + by_pieces((weight_ref, partner_ref), values_ref, first_pair)
+    heads = values_ref.shape[2] - SPARE
+    low = in_low((heads, lanes))
+    for chip in range(values_ref.shape[0]):
+        for core in range(2):
+            block = values_ref[chip, core].astype(jnp.float32)[:heads]
+            for piece in range(2):
+                at = ((chip * 2 + piece) * 2 + core) * heads
+                features_ref[at : at + heads, :] = jnp.where(low == (piece == 0), block, 0.0)
+    features = features_ref[...].astype(jnp.bfloat16)
+    outputs = stream + by_pieces((weight_ref, partner_ref), features, first_pair)
     units = stream * inverse
     back = cotangent_ref[...].astype(jnp.float32)
     back = back + inverse * (norm_grads * gain_ref[...] - units * inner)
@@ -280,28 +261,41 @@
     out_ref[...] = spread.astype(jnp.bfloat16)
 
 
-def join_kernel(width, trip_ref, passed_ref, returned_ref, total_ref, rows_ref):
-    _, _, capacity, micro_rows, model = passed_ref.shape
-    lines = trip_ref.shape[0] // 8
+def join_kernel(
+    width, trip_ref, gradient_ref, weight_ref, first_ref, second_ref,
+    passed_ref, returned_ref, new_weight_ref, new_first_ref, new_second_ref, rows_ref,
+):
+    _, _, capacity, micro_rows, _ = passed_ref.shape
     slots = 2 * capacity * micro_rows
     norms = jnp.zeros((1, LANES), jnp.float32)
-    for far in range(2):
-        for at in range(2 * lines):
-            peers = [(2 * far + pair) * 2 * lines + at for pair in range(2)]
+    for chip in range(trip_ref.shape[0] // 4):
+        for core in range(2):
+            peers = [(chip * 2 + pair) * 2 + core for pair in range(2)]
             block = trip_ref[peers[0]].astype(jnp.float32) + trip_ref[peers[1]].astype(jnp.float32)
             norms += block[0:1]
             for piece in range(2):
-                first = ((2 * far + piece) * 2 * lines + at) * width
-                rows_ref[:, first : first + width] = block[piece * slots : (piece + 1) * slots, :width]
-    lane = lax.broadcasted_iota(jnp.int32, (1, LANES), 1)
-    inside = (lane >= width) & (lane < width + 3)
-    total = jnp.sum(jnp.where(inside, norms, 0.0), axis=1, keepdims=True)
-    total_ref[...] = jnp.broadcast_to(total, total_ref.shape)
+                at = peers[piece] * width
+                rows_ref[:, at : at + width] = block[piece * slots : (piece + 1) * slots, :width]
     at = 0
     for ref in (passed_ref, returned_ref):
         for slot in range(capacity):
             ref[0, 0, slot] = rows_ref[at : at + micro_rows, :].astype(jnp.bfloat16)
             at += micro_rows
+    lane = lax.broadcasted_iota(jnp.int32, (1, LANES), 1)
+    inside = (lane >= width) & (lane < width + 3)
+    total = jnp.sum(jnp.where(inside, norms, 0.0), axis=1, keepdims=True)
+    scale = jnp.minimum(1.0, CLIP_NORM / jnp.sqrt(total + 1e-06))
+    span = 8 * width
+    for at in range(0, gradient_ref.shape[1], span):
+        here = slice(at, at + span)
+        clipped = gradient_ref[:, here] * scale
+        first = BETA_ONE * first_ref[0, :, here] + (1.0 - BETA_ONE) * clipped
+        second = BETA_TWO * second_ref[0, :, here] + (1.0 - BETA_TWO) * clipped * clipped
+        wide = weight_ref[0, :, here].astype(jnp.float32)
+        updated = wide - LEARN_RATE * (first / (jnp.sqrt(second) + ADAM_EPS) + DECAY * wide)
+        new_weight_ref[0, :, here] = updated.astype(jnp.bfloat16)
+        new_first_ref[0, :, here] = first
+        new_second_ref[0, :, here] = second
 
 
 def slot_rows_of(placed, capacity, micro_rows):
@@ -327,12 +321,12 @@
 
 
 def body(placing, acts, cotan, gain, w_value, w_out, moment_one, moment_two):
-    lines = lax.axis_size("line")
-    chips, team = 4 * lines, 2 * lines
+    team = lax.axis_size("team")
+    chips = 2 * team
     peers = 2 * chips
     sections = lax.axis_size("section")
     section_now, pair_now = lax.axis_index("section"), lax.axis_index("pair")
-    far_now, line_now = lax.axis_index("far"), lax.axis_index("line")
+    team_now = lax.axis_index("team")
     _, _, capacity, micro_rows, model = acts.shape
     slot_rows = capacity * micro_rows
     width = model // peers
@@ -370,7 +364,7 @@
     code = jnp.concatenate(code)[None]
     own_gain = [
         lax.dynamic_slice_in_dim(
-            gain[0], ((2 * far_now + piece) * lines + line_now) * 2 * width + core[0] * width, width, 0
+            gain[0], ((2 * team_now + piece) * 2 + core[0]) * width, width, 0
         )
         for piece in range(2)
     ]
@@ -393,6 +387,7 @@
         [],
         [mine, arrived, stream],
     )
+    payload, pair_weights = lax.optimization_barrier((payload, pair_weights))
     first_trip = swap(payload, TEAM)
     other_trip = moved(first_trip, "core")
     value_grads, mine, other = on_core(
@@ -412,7 +407,7 @@
         ],
         [core, pair],
         [first_trip, other_trip, gain, weights, pair_weights, value_grads],
-        [pltpu.VMEM((model // 2, rows), brief)],
+        [pltpu.VMEM((model, rows), brief)],
     )
     (payload,) = on_core(
         functools.partial(payload_kernel, 0, width),
@@ -438,7 +433,7 @@
         [pair, ahead],
         [
             second_trip,
-            gathered[:, :, :heads].reshape(-1, rows),
+            gathered,
             extra,
             out_weights,
             pair_out_weights,
@@ -448,6 +443,7 @@
             inverse,
             norms,
         ],
+        [pltpu.VMEM((model // 2, rows), full)],
     )
     third_trip = swap(both, "section")
     behind = jnp.stack([(section_now + sections - 1) % sections, (section_now + 1) % sections])
@@ -459,26 +455,19 @@
         [third_trip, code],
     )
     final = swap(spread.reshape(peers, 4 * slot_rows, LANES), PEER)
-    passed, returned, totals = on_core(
+    return on_core(
         functools.partial(join_kernel, width),
-        [shape(acts.shape)] * 2 + [shape((SPARE, LANES), full)],
+        [shape(acts.shape)] * 2
+        + [shape(w_value.shape), shape(moment_one.shape, full), shape(moment_two.shape, full)],
         [],
-        [final],
+        [final, gradient, w_value, moment_one, moment_two],
         [pltpu.VMEM((2 * slot_rows, model), full)],
     )
-
-    clip_scale = jnp.minimum(1.0, CLIP_NORM / jnp.sqrt(totals[0, 0] + 1e-06))
-    clipped = gradient * clip_scale
-    first = BETA_ONE * moment_one[0] + (1.0 - BETA_ONE) * clipped
-    second = BETA_TWO * moment_two[0] + (1.0 - BETA_TWO) * clipped * clipped
-    wide = weights.astype(full)
-    updated = wide - LEARN_RATE * (first / (jnp.sqrt(second) + ADAM_EPS) + DECAY * wide)
-    return passed, returned, updated.astype(brief)[None], first[None], second[None]
 
 
 def solution(mesh):
     sections, peers = mesh.devices.shape
-    fine = Mesh(mesh.devices.reshape(sections, 2, 2, peers // 8, 2), ("section",) + PEER)
+    fine = Mesh(mesh.devices.reshape(sections, peers // 4, 2, 2), ("section",) + PEER)
     slots = P("section", PEER, None, None, None)
     matrix = P("section", PEER, None)
     return jax.shard_map(

time: 184 us -> 154 us (0.84)
  waiting for transfers between devices: 74.6 us -> 32.9 us
  blocking collectives: 31.8 us -> 61.9 us
  starting transfers between devices: 56.7 us -> 43.2 us
  other arithmetic: 4.36 us -> 1.3 us
    all_to_all x1 -> x2, blocking collectives: 25.2 us -> 55.1 us  [swap(): return lax.all_to_all(blocks, axis, split_axis=0, concat_axis=0, tiled=True)]
    ppermute x6, waiting for transfers between devices: 49.5 us -> 23.2 us  [moved(): return lax.ppermute(block, axis, [(0, 1), (1, 0)])]
    all_to_all x4 -> x3, waiting for transfers between devices: 25.2 us -> 9.68 us  [swap(): return lax.all_to_all(blocks, axis, split_axis=0, concat_axis=0, tiled=True)]
    all_to_all x4 -> x3, starting transfers between devices: 39.1 us -> 25 us  [swap(): return lax.all_to_all(blocks, axis, split_axis=0, concat_axis=0, tiled=True)]
    broadcast_in_dim x1 -> x0, other arithmetic: 3.06 us -> none  [body(): second[None]]
  transfers between devices with their start and end apart: 10 -> 9, of which waited for: 7 -> 6; matrix products, arithmetic and copies ran while one was open for 1% -> 1% of each run, Pallas kernels for 1% -> 3%
where the time goes in v7:
time: 154 us
  blocking collectives  61.9 us (40%)
  starting transfers between devices  43.2 us (28%)
  waiting for transfers between devices  32.9 us (21%)
  Pallas kernels  9.64 us (6%)
  local copies, waits for them, and re-layouts  3.92 us (3%)
    all_to_all x2, blocking collectives, swap(): return lax.all_to_all(blocks, axis, split_axis=0, concat_axis=0, tiled=True)  55.1 us
    all_to_all x3, starting transfers between devices, swap(): return lax.all_to_all(blocks, axis, split_axis=0, concat_axis=0, tiled=True)  25 us
    ppermute x6, waiting for transfers between devices, moved(): return lax.ppermute(block, axis, [(0, 1), (1, 0)])  23.2 us
    ppermute x6, starting transfers between devices, moved(): return lax.ppermute(block, axis, [(0, 1), (1, 0)])  18.2 us
    all_to_all x3, waiting for transfers between devices, swap(): return lax.all_to_all(blocks, axis, split_axis=0, concat_axis=0, tiled=True)  9.68 us
    pallas_call x10, Pallas kernels, on_core(): pl.pallas_call(kernel, out_shape=out_shape, in_specs=[pl.BlockSpec(memory...  9.64 us
    all_gather x1, blocking collectives, body(): lax.all_gather(cols, 'core', axis=0)  4.09 us
  transfers between devices with their start and end apart: 9, of which 6 were waited for; matrix products, arithmetic and copies ran while one was open for 1% of the time, Pallas kernels for 3%

profile of v7, /device:TPU:1, one launch (start us, length us, event | category | flops | bytes accessed | tf_op | source)
XLA Modules:
  0.0 153.7 jit_solution(7638188460047398246)
XLA Ops:
  0.6 0.0 copy-start
  0.6 1.7 %shard_map.119 = bf16[32,8,320]{2,1,0:T(8,128)(2,1)} custom-call(bf16[1,1,2,2,5120]{4,3,2,1,0:T(2,128)(2,1)} %acts_ref.1, bf16[1,1,2,2,5120]{4,3,2,1,0:T(2,128)(2,1)} %cotan_ref.1), custom_call_target="tpu_custom_call" | custom-call | bytes 245760 | tf_op jit(solution)/shard_map/pallas_call | solution.py:311
  2.3 16.5 %all-to-all-start = ((bf16[32,8,320]{2,1,0:T(8,128)(2,1)}), bf16[32,8,320]{2,1,0:T(8,128)(2,1)S(1)}, u32[]{:S(2)}, u32[]{:S(2)}) async-start(bf16[32,8,320]{2,1,0:T(8,128)(2,1)} %shard_map.119), calls=%async_computation | async-start | bytes 393216 | tf_op jit(solution)/shard_map/all_to_all | solution.py:25
  18.9 3.1 %collective-permute-start = (bf16[80,2560]{1,0:T(8,128)(2,1)}, bf16[80,2560]{1,0:T(8,128)(2,1)S(1)}, u32[]{:S(2)}, u32[]{:S(2)}) collective-permute-start(bf16[80,2560]{1,0:T(8,128)(2,1)} %bitcast.33), channel_id=1, source_target_pairs={{0,2},{2,0},{1,3},{3,1},{4,6},{6,4},{5,7},{7,5},{8,10},{10,8},{9,1... | collective-permute-start | bytes 1228808 | tf_op jit(solution)/shard_map/ppermute | solution.py:29
  22.0 0.0 copy-done
  22.0 2.1 %collective-permute-start.2 = (bf16[40,5120]{1,0:T(8,128)(2,1)S(1)}, bf16[40,5120]{1,0:T(8,128)(2,1)S(1)}, u32[]{:S(2)}, u32[]{:S(2)}) collective-permute-start(bf16[40,5120]{1,0:T(8,128)(2,1)S(1)} %bitcast.28), channel_id=1, source_target_pairs={{0,2},{2,0},{1,3},{3,1},{4,6},{6,4},{5,7},{7,5},{8,10},{10,8},{9,1... | collective-permute-start | bytes 1228808 | tf_op jit(solution)/shard_map/ppermute | solution.py:29
  24.2 0.7 fusion.1
  24.8 0.1 convert_reduce_fusion.1
  24.9 0.7 add_multiply_fusion
  25.6 0.1 iota_add_fusion
  25.7 0.1 add.109
  25.8 0.0 copy-start.7
  25.8 0.1 broadcast_add_fusion.2
  25.9 0.1 pad_bitcast_fusion.1
  26.0 0.0 copy-start.1
  26.0 0.1 pad_add_fusion.1
  26.1 0.4 copy-done.7
  26.6 0.1 fusion.3
  26.6 0.1 broadcast_in_dim.7
  26.7 0.1 broadcast_in_dim.8
  26.8 0.1 pad_maximum_fusion.gain_ref
  26.9 3.9 %all-to-all-done = bf16[32,8,320]{2,1,0:T(8,128)(2,1)S(1)} async-done(((bf16[32,8,320]{2,1,0:T(8,128)(2,1)}), bf16[32,8,320]{2,1,0:T(8,128)(2,1)S(1)}, u32[]{:S(2)}, u32[]{:S(2)}) %all-to-all-start) | async-done | bytes 163872 | tf_op jit(solution)/shard_map/all_to_all | solution.py:25
  30.8 4.1 %all-gather = bf16[64,8,320]{2,1,0:T(8,128)(2,1)S(1)} all-gather(bf16[32,8,320]{2,1,0:T(8,128)(2,1)S(1)} %all-to-all-done), channel_id=2, replica_groups=mesh['section'=8,'team'=16,'pair'=2,'core'=2] {'core'}, dimensions={0}, use_global_device_ids=true | all-gather | bytes 491520 | tf_op jit(solution)/shard_map/all_gather | solution.py:375
  34.9 0.2 collective-permute-done.partner_ref
  35.1 0.0 copy-done.1
  35.1 1.1 shard_map.120
  36.2 3.8 %collective-permute-start.1 = (bf16[16,40,128]{2,1,0:T(8,128)(2,1)S(1)}, bf16[16,40,128]{2,1,0:T(8,128)(2,1)S(1)}, u32[]{:S(2)}, u32[]{:S(2)}) collective-permute-start(bf16[16,40,128]{2,1,0:T(8,128)(2,1)S(1)} %get-tuple-element.29), channel_id=1, source_target_pairs={{0,1},{1,0},{2,3},{3,2},{4,5},{5,4},{6,7},{7,6},{8,9},{9,8},{10,11... | collective-permute-start | bytes 491528 | tf_op jit(solution)/shard_map/ppermute | solution.py:29
  39.9 1.0 collective-permute-done.1.arrived_ref
  40.9 0.1 shard_map.121
  41.0 2.8 %collective-permute-done.2.partner_ref = bf16[40,5120]{1,0:T(8,128)(2,1)S(1)} collective-permute-done((bf16[40,5120]{1,0:T(8,128)(2,1)S(1)}, bf16[40,5120]{1,0:T(8,128)(2,1)S(1)}, u32[]{:S(2)}, u32[]{:S(2)}) %collective-permute-start.2) | collective-permute-done | bytes 409632 | tf_op jit(solution)/shard_map/ppermute | solution.py:29
  43.8 28.1 %all_to_all.25.trip_ref.mine_ref = bf16[16,120,128]{2,1,0:T(8,128)(2,1)S(1)} all-to-all(bf16[16,120,128]{2,1,0:T(8,128)(2,1)S(1)} %shard_map.121), channel_id=1, replica_groups=mesh['section'=8,'team'=16,'pair'=2,'core'=2] {'team'}, dimensions={0} | all-to-all | bytes 983040 | tf_op jit(solution)/shard_map/all_to_all | solution.py:25
  71.9 4.0 %collective-permute-start.4 = (bf16[16,120,128]{2,1,0:T(8,128)(2,1)S(1)}, bf16[16,120,128]{2,1,0:T(8,128)(2,1)S(1)}, u32[]{:S(2)}, u32[]{:S(2)}) collective-permute-start(bf16[16,120,128]{2,1,0:T(8,128)(2,1)S(1)} %all_to_all.25.trip_ref.mine_ref), channel_id=1, source_target_pairs={{0,1},{1,0},{2,3},{3,2},{4,5},{5,4},{6,7},{7,6},{8,9},{9,8},{10,11... | collective-permute-start | bytes 1474568 | tf_op jit(solution)/shard_map/ppermute | solution.py:29
  76.0 1.0 shard_map.122
  76.9 1.9 %collective-permute-start.3 = (bf16[16,80,128]{2,1,0:T(8,128)(2,1)S(1)}, bf16[16,80,128]{2,1,0:T(8,128)(2,1)S(1)}, u32[]{:S(2)}, u32[]{:S(2)}) collective-permute-start(bf16[16,80,128]{2,1,0:T(8,128)(2,1)S(1)} %get-tuple-element.34), channel_id=1, source_target_pairs={{0,1},{1,0},{2,3},{3,2},{4,5},{5,4},{6,7},{7,6},{8,9},{9,8},{10,11... | collective-permute-start | bytes 983048 | tf_op jit(solution)/shard_map/ppermute | solution.py:29
  78.9 0.0 collective-permute-done.4.other_ref
  78.9 1.6 %shard_map.123 = (bf16[48,128]{1,0:T(8,128)(2,1)S(1)}, f32[40,5120]{1,0:T(8,128)S(1)}, bf16[40,5120]{1,0:T(8,128)(2,1)S(1)}, f32[8,128]{1,0:T(8,128)S(1)}) custom-call(s32[1]{0:T(128)} %bitcast.3.core_ref, s32[1]{0:T(128)} %bitcast.2.pair_ref, bf16[16,120,128]{2,1,0:T(8,128)(2,1)S(1)} %all_to_all.25.trip_ref.mine_ref, ...), custom_call_target="tpu_custom_call" | custom-call | bytes 3067904 | tf_op jit(solution)/shard_map/pallas_call | solution.py:311
  80.5 0.0 collective-permute-done.3.arrived_ref
  80.5 0.9 shard_map.124
  81.4 4.4 %all-to-all-start.2 = ((bf16[16,128,128]{2,1,0:T(8,128)(2,1)}), bf16[16,128,128]{2,1,0:T(8,128)(2,1)S(1)}, u32[]{:S(2)}, u32[]{:S(2)}) async-start(bf16[16,128,128]{2,1,0:T(8,128)(2,1)} %shard_map.124), calls=%async_computation.2 | async-start | bytes 1048576 | tf_op jit(solution)/shard_map/all_to_all | solution.py:25
  85.8 3.2 %collective-permute-start.5 = (bf16[40,5120]{1,0:T(8,128)(2,1)S(1)}, bf16[40,5120]{1,0:T(8,128)(2,1)S(1)}, u32[]{:S(2)}, u32[]{:S(2)}) collective-permute-start(bf16[40,5120]{1,0:T(8,128)(2,1)S(1)} %get-tuple-element.43), channel_id=1, source_target_pairs={{0,2},{2,0},{1,3},{3,1},{4,6},{6,4},{5,7},{7,5},{8,10},{10,8},{9,1... | collective-permute-start | bytes 1228808 | tf_op jit(solution)/shard_map/ppermute | solution.py:29
  89.0 19.2 %collective-permute-done.5.arrived_ref = bf16[40,5120]{1,0:T(8,128)(2,1)S(1)} collective-permute-done((bf16[40,5120]{1,0:T(8,128)(2,1)S(1)}, bf16[40,5120]{1,0:T(8,128)(2,1)S(1)}, u32[]{:S(2)}, u32[]{:S(2)}) %collective-permute-start.5) | collective-permute-done | bytes 409632 | tf_op jit(solution)/shard_map/ppermute | solution.py:29
  108.2 0.0 copy-start.5
  108.2 0.7 copy-done.5
  108.9 0.0 copy-start.6
  109.0 1.0 copy-done.6
  110.0 0.1 shard_map.125
  110.1 0.0 all-to-all-done.2.trip_ref
  110.1 2.6 %all-gather.1 = bf16[16,96,128]{2,1,0:T(8,128)(2,1)S(1)} all-gather(bf16[16,48,128]{2,1,0:T(8,128)(2,1)S(1)} %slice.8), channel_id=3, replica_groups=mesh['section'=8,'team'=16,'pair'=2,'core'=2] {'core'}, dimensions={1}, use_global_device_ids=true | all-gather | bytes 589824 | tf_op jit(solution)/shard_map/all_gather | solution.py:426
  112.8 0.0 copy-start.3
  112.8 0.5 shard_map.126
  113.2 0.0 copy-start.4
  113.3 0.7 copy-done.4
  113.9 0.0 copy-start.2
  113.9 4.2 %all-to-all-start.3 = ((bf16[8,88,128]{2,1,0:T(8,128)(2,1)}), bf16[8,88,128]{2,1,0:T(8,128)(2,1)S(1)}, u32[]{:S(2)}, u32[]{:S(2)}) async-start(bf16[8,88,128]{2,1,0:T(8,128)(2,1)} %copy-done.4), calls=%async_computation.3 | async-start | bytes 360448 | tf_op jit(solution)/shard_map/all_to_all | solution.py:25
  118.1 0.1 pad_add_fusion.2.from_ref
  118.2 5.8 %all-to-all-done.3.trip_ref = bf16[8,88,128]{2,1,0:T(8,128)(2,1)S(1)} async-done(((bf16[8,88,128]{2,1,0:T(8,128)(2,1)}), bf16[8,88,128]{2,1,0:T(8,128)(2,1)S(1)}, u32[]{:S(2)}, u32[]{:S(2)}) %all-to-all-start.3) | async-done | bytes 180256 | tf_op jit(solution)/shard_map/all_to_all | solution.py:25
  123.9 0.8 shard_map.127
  124.7 27.0 %all_to_all.26.trip_ref = bf16[64,16,128]{2,1,0:T(8,128)(2,1)S(1)} all-to-all(bf16[64,16,128]{2,1,0:T(8,128)(2,1)S(1)} %bitcast.37), channel_id=1, replica_groups=mesh['section'=8,'team'=16,'pair'=2,'core'=2] {'team','pair','core'}, dimensions={0} | all-to-all | bytes 524288 | tf_op jit(solution)/shard_map/all_to_all | solution.py:25
  151.8 0.0 copy-done.3
  151.8 0.0 copy-done.2
  151.8 1.9 %shard_map.128 = (bf16[1,1,2,2,5120]{4,3,2,1,0:T(2,128)(2,1)}, bf16[1,1,2,2,5120]{4,3,2,1,0:T(2,128)(2,1)}, bf16[1,40,5120]{2,1,0:T(8,128)(2,1)}, f32[1,40,5120]{2,1,0:T(8,128)}, f32[1,40,5120]{2,1,0:T(8,128)}) custom-call(bf16[64,16,128]{2,1,0:T(8,128)(2,1)S(1)} %all_to_all.26.trip_ref, f32[40,5120]{1,0:T(8,128)S(1)} %get-tuple-element.46.gradient_ref, ...), custom_call_target="tpu_custom_call" | custom-call | bytes 5259264 | tf_op jit(solution)/shard_map/pallas_call | solution.py:311
  (4 shorter events, 0.1 us)
Async XLA Ops:
  0.6 21.4 %copy-start = (bf16[1,40,5120]{2,1,0:T(8,128)(2,1)S(1)}, bf16[1,40,5120]{2,1,0:T(8,128)(2,1)}, u32[]{:S(2)}) copy-start(bf16[1,40,5120]{2,1,0:T(8,128)(2,1)} %weight_ref.1) | copy-start | bytes 1228804
  2.3 28.5 %all-to-all-start = ((bf16[32,8,320]{2,1,0:T(8,128)(2,1)}), bf16[32,8,320]{2,1,0:T(8,128)(2,1)S(1)}, u32[]{:S(2)}, u32[]{:S(2)}) async-start(bf16[32,8,320]{2,1,0:T(8,128)(2,1)} %shard_map.119), calls=%async_computation | async-start | bytes 393216 | tf_op jit(solution)/shard_map/all_to_all | solution.py:25
  18.9 16.2 %collective-permute-start = (bf16[80,2560]{1,0:T(8,128)(2,1)}, bf16[80,2560]{1,0:T(8,128)(2,1)S(1)}, u32[]{:S(2)}, u32[]{:S(2)}) collective-permute-start(bf16[80,2560]{1,0:T(8,128)(2,1)} %bitcast.33), channel_id=1, source_target_pairs={{0,2},{2,0},{1,3},{3,1},{4,6},{6,4},{5,7},{7,5},{8,10},{10,8},{9,1... | collective-permute-start | bytes 1228808 | tf_op jit(solution)/shard_map/ppermute | solution.py:29
  22.0 21.8 %collective-permute-start.2 = (bf16[40,5120]{1,0:T(8,128)(2,1)S(1)}, bf16[40,5120]{1,0:T(8,128)(2,1)S(1)}, u32[]{:S(2)}, u32[]{:S(2)}) collective-permute-start(bf16[40,5120]{1,0:T(8,128)(2,1)S(1)} %bitcast.28), channel_id=1, source_target_pairs={{0,2},{2,0},{1,3},{3,1},{4,6},{6,4},{5,7},{7,5},{8,10},{10,8},{9,1... | collective-permute-start | bytes 1228808 | tf_op jit(solution)/shard_map/ppermute | solution.py:29
  25.8 0.7 copy-start.7
  26.0 9.0 %copy-start.1 = (bf16[1,80,2560]{2,1,0:T(8,128)(2,1)S(1)}, bf16[1,80,2560]{2,1,0:T(8,128)(2,1)}, u32[]{:S(2)}) copy-start(bf16[1,80,2560]{2,1,0:T(8,128)(2,1)} %param.13) | copy-start | bytes 1228804
  36.2 4.8 %collective-permute-start.1 = (bf16[16,40,128]{2,1,0:T(8,128)(2,1)S(1)}, bf16[16,40,128]{2,1,0:T(8,128)(2,1)S(1)}, u32[]{:S(2)}, u32[]{:S(2)}) collective-permute-start(bf16[16,40,128]{2,1,0:T(8,128)(2,1)S(1)} %get-tuple-element.29), channel_id=1, source_target_pairs={{0,1},{1,0},{2,3},{3,2},{4,5},{5,4},{6,7},{7,6},{8,9},{9,8},{10,11... | collective-permute-start | bytes 491528 | tf_op jit(solution)/shard_map/ppermute | solution.py:29
  71.9 6.9 %collective-permute-start.4 = (bf16[16,120,128]{2,1,0:T(8,128)(2,1)S(1)}, bf16[16,120,128]{2,1,0:T(8,128)(2,1)S(1)}, u32[]{:S(2)}, u32[]{:S(2)}) collective-permute-start(bf16[16,120,128]{2,1,0:T(8,128)(2,1)S(1)} %all_to_all.25.trip_ref.mine_ref), channel_id=1, source_target_pairs={{0,1},{1,0},{2,3},{3,2},{4,5},{5,4},{6,7},{7,6},{8,9},{9,8},{10,11... | collective-permute-start | bytes 1474568 | tf_op jit(solution)/shard_map/ppermute | solution.py:29
  76.9 3.6 %collective-permute-start.3 = (bf16[16,80,128]{2,1,0:T(8,128)(2,1)S(1)}, bf16[16,80,128]{2,1,0:T(8,128)(2,1)S(1)}, u32[]{:S(2)}, u32[]{:S(2)}) collective-permute-start(bf16[16,80,128]{2,1,0:T(8,128)(2,1)S(1)} %get-tuple-element.34), channel_id=1, source_target_pairs={{0,1},{1,0},{2,3},{3,2},{4,5},{5,4},{6,7},{7,6},{8,9},{9,8},{10,11... | collective-permute-start | bytes 983048 | tf_op jit(solution)/shard_map/ppermute | solution.py:29
  81.4 28.6 %all-to-all-start.2 = ((bf16[16,128,128]{2,1,0:T(8,128)(2,1)}), bf16[16,128,128]{2,1,0:T(8,128)(2,1)S(1)}, u32[]{:S(2)}, u32[]{:S(2)}) async-start(bf16[16,128,128]{2,1,0:T(8,128)(2,1)} %shard_map.124), calls=%async_computation.2 | async-start | bytes 1048576 | tf_op jit(solution)/shard_map/all_to_all | solution.py:25
  85.8 22.4 %collective-permute-start.5 = (bf16[40,5120]{1,0:T(8,128)(2,1)S(1)}, bf16[40,5120]{1,0:T(8,128)(2,1)S(1)}, u32[]{:S(2)}, u32[]{:S(2)}) collective-permute-start(bf16[40,5120]{1,0:T(8,128)(2,1)S(1)} %get-tuple-element.43), channel_id=1, source_target_pairs={{0,2},{2,0},{1,3},{3,1},{4,6},{6,4},{5,7},{7,5},{8,10},{10,8},{9,1... | collective-permute-start | bytes 1228808 | tf_op jit(solution)/shard_map/ppermute | solution.py:29
  108.2 0.8 copy-start.5
  108.9 1.0 copy-start.6
  112.8 39.0 %copy-start.3 = (f32[1,40,5120]{2,1,0:T(8,128)S(1)}, f32[1,40,5120]{2,1,0:T(8,128)}, u32[]{:S(2)}) copy-start(f32[1,40,5120]{2,1,0:T(8,128)} %second_ref.1) | copy-start | bytes 2457604
  113.2 0.7 copy-start.4
  113.9 37.9 %copy-start.2 = (f32[1,40,5120]{2,1,0:T(8,128)S(1)}, f32[1,40,5120]{2,1,0:T(8,128)}, u32[]{:S(2)}) copy-start(f32[1,40,5120]{2,1,0:T(8,128)} %first_ref.1) | copy-start | bytes 2457604
  113.9 10.0 %all-to-all-start.3 = ((bf16[8,88,128]{2,1,0:T(8,128)(2,1)}), bf16[8,88,128]{2,1,0:T(8,128)(2,1)S(1)}, u32[]{:S(2)}, u32[]{:S(2)}) async-start(bf16[8,88,128]{2,1,0:T(8,128)(2,1)} %copy-done.4), calls=%async_computation.3 | async-start | bytes 360448 | tf_op jit(solution)/shard_map/all_to_all | solution.py:25

commit v8 on v7

--- a/solution.py
+++ b/solution.py
@@ -154,12 +154,8 @@
     partial_sums(refs, grads, first_core, first_pair, width, mine_ref, other_ref)
 
 
-def values_kernel(
-    width, heads, core_ref, pair_ref, mine_ref, other_ref, gain_ref, weight_ref, partner_ref,
-    grads_ref, own_ref, gradient_ref, partner_gradient_ref, inverse_ref, normed_ref,
-):
+def normalise(width, first_core, mine_ref, other_ref, gain_ref, normed_ref):
     chips, _, lanes = mine_ref.shape
-    first_core, first_pair = core_ref[0] == 0, pair_ref[0] == 0
     squares = jnp.zeros((width, lanes), jnp.float32)
     for chip in range(chips):
         for ref in (mine_ref, other_ref):
@@ -167,7 +163,6 @@
             squares += block * block
     total = jnp.broadcast_to(jnp.sum(squares, axis=0, keepdims=True), (SPARE, lanes))
     inverses = lax.rsqrt((total + turned(total)) / gain_ref.shape[1] + NORM_EPS)
-    inverse_ref[...] = inverses
     inverse = inverses[0:1]
     top = lax.broadcasted_iota(jnp.int32, (16, lanes), 0) == 0
     one = top.astype(jnp.float32).astype(jnp.bfloat16)
@@ -187,26 +182,44 @@
                     scaled = units * gains[line : line + width]
                     scaled = jnp.where(low == (piece == 0), scaled, 0.0)
                     normed_ref[pl.ds(at + line, width), :] = scaled.astype(jnp.bfloat16)
+    return inverses
+
+
+def values_kernel(
+    width, heads, core_ref, pair_ref, mine_ref, other_ref, gain_ref, weight_ref, partner_ref,
+    grads_ref, own_ref, gradient_ref, inverse_ref, normed_ref,
+):
+    lanes = mine_ref.shape[2]
+    first_core, first_pair = core_ref[0] == 0, pair_ref[0] == 0
+    inverse_ref[...] = normalise(width, first_core, mine_ref, other_ref, gain_ref, normed_ref)
     values = by_pieces((weight_ref, partner_ref), normed_ref[...], first_pair)
     grads = grads_ref[...].astype(jnp.float32)
-    both = jnp.concatenate(pieces_apart(grads, first_pair), axis=0).astype(jnp.bfloat16)
+    own = pieces_apart(grads, first_pair)[0].astype(jnp.bfloat16)
+    span = 8 * width
     for at in range(0, gain_ref.shape[1], span):
-        block = product(both, normed_ref[at : at + span, :], (1, 1))
-        gradient_ref[:, at : at + span] = block[:heads]
-        partner_gradient_ref[:, at : at + span] = block[heads:].astype(jnp.bfloat16)
+        gradient_ref[:, at : at + span] = product(own, normed_ref[at : at + span, :], (1, 1))
     inner = jnp.broadcast_to(jnp.sum(grads * values, axis=0, keepdims=True), (SPARE, lanes))
     inner = inner + turned(inner)
     extra = as_rows(parts_of(inner), (SPARE, lanes))
     own_ref[...] = jnp.concatenate([values, extra], axis=0).astype(jnp.bfloat16)
 
 
-def gradient_kernel(mine_ref, arrived_ref, gradient_ref, norms_ref):
+def gradient_kernel(
+    width, core_ref, pair_ref, mine_ref, other_ref, gain_ref, grads_ref, half_ref,
+    gradient_ref, norms_ref, normed_ref,
+):
     lanes = norms_ref.shape[1]
-    norms = jnp.zeros((mine_ref.shape[0], lanes), jnp.float32)
-    for at in range(0, mine_ref.shape[1], lanes):
-        block = mine_ref[:, at : at + lanes] + arrived_ref[:, at : at + lanes].astype(jnp.float32)
-        gradient_ref[:, at : at + lanes] = block
-        norms += block * block
+    first_core, first_pair = core_ref[0] == 0, pair_ref[0] == 0
+    normalise(width, first_core, mine_ref, other_ref, gain_ref, normed_ref)
+    grads = grads_ref[...].astype(jnp.float32)
+    own = pieces_apart(grads, first_pair)[0].astype(jnp.bfloat16)
+    norms = jnp.zeros((half_ref.shape[0], lanes), jnp.float32)
+    span = 8 * width
+    for at in range(0, gain_ref.shape[1], span):
+        block = product(own, normed_ref[at : at + span, :], (1, 1)) + half_ref[:, at : at + span]
+        gradient_ref[:, at : at + span] = block
+        for lane in range(0, span, lanes):
+            norms += block[:, lane : lane + lanes] * block[:, lane : lane + lanes]
     norms_ref[...] = jnp.broadcast_to(jnp.sum(norms, axis=0, keepdims=True), norms_ref.shape)
 
 
@@ -390,6 +403,7 @@
     payload, pair_weights = lax.optimization_barrier((payload, pair_weights))
     first_trip = swap(payload, TEAM)
     other_trip = moved(first_trip, "core")
+    pair_mine = moved(first_trip[:, :width], "pair")
     value_grads, mine, other = on_core(
         functools.partial(dnormed_kernel, width, heads),
         [shape((heads, rows))] + [shape((team, width, rows))] * 2,
@@ -397,12 +411,11 @@
         [first_trip, weights, pair_weights],
     )
     arrived = moved(other, "core")
-    own, gradient, pair_gradient, inverse = on_core(
+    own, half_gradient, inverse = on_core(
         functools.partial(values_kernel, width, heads),
         [
             shape((heads + SPARE, rows)),
             shape((heads, model), full),
-            shape((heads, model)),
             shape((SPARE, rows), full),
         ],
         [core, pair],
@@ -415,13 +428,14 @@
         [],
         [mine, arrived, own],
     )
-    payload, pair_gradient = lax.optimization_barrier((payload, pair_gradient))
+    payload, pair_mine, pair_grads = lax.optimization_barrier((payload, pair_mine, value_grads))
     second_trip = swap(payload, TEAM)
     gradient, norms = on_core(
-        gradient_kernel,
+        functools.partial(gradient_kernel, width),
         [shape((heads, model), full), shape((SPARE, rows), full)],
-        [],
-        [gradient, moved(pair_gradient, "pair")],
+        [core, pair],
+        [pair_mine, moved(pair_mine, "core"), gain, moved(pair_grads, "pair"), half_gradient],
+        [pltpu.VMEM((model, rows), brief)],
     )
     gathered = lax.all_gather(second_trip[:, width:], "core", axis=1)
     extra = jnp.sum(gathered[:, :, heads:].astype(full), axis=(0, 1))

time: 154 us -> 156 us (1.013)
  starting transfers between devices: 43.2 us -> 49.4 us
  waiting for transfers between devices: 32.9 us -> 29.3 us
  blocking collectives: 61.9 us -> 59.1 us
    ppermute x6 -> x8, waiting for transfers between devices: 23.2 us -> 11 us  [moved(): return lax.ppermute(block, axis, [(0, 1), (1, 0)])]
    all_to_all x3, waiting for transfers between devices: 9.68 us -> 18.3 us  [swap(): return lax.all_to_all(blocks, axis, split_axis=0, concat_axis=0, tiled=True)]
    ppermute x6 -> x8, starting transfers between devices: 18.2 us -> 24.4 us  [moved(): return lax.ppermute(block, axis, [(0, 1), (1, 0)])]
    all_to_all x2, blocking collectives: 55.1 us -> 52.1 us  [swap(): return lax.all_to_all(blocks, axis, split_axis=0, concat_axis=0, tiled=True)]
    unnamed x16 -> x20, local copies, waits for them, and re-layouts: 2.88 us -> 3.8 us
  transfers between devices with their start and end apart: 9 -> 11, of which waited for: 6 -> 8; matrix products, arithmetic and copies ran while one was open for 1% -> 1% of each run, Pallas kernels for 3% -> 4%
where the time goes in v8:
time: 156 us
  blocking collectives  59.1 us (38%)
  starting transfers between devices  49.4 us (32%)
  waiting for transfers between devices  29.3 us (19%)
  Pallas kernels  10.7 us (7%)
  local copies, waits for them, and re-layouts  4.87 us (3%)
    all_to_all x2, blocking collectives, swap(): return lax.all_to_all(blocks, axis, split_axis=0, concat_axis=0, tiled=True)  52.1 us
    all_to_all x3, starting transfers between devices, swap(): return lax.all_to_all(blocks, axis, split_axis=0, concat_axis=0, tiled=True)  25 us
    ppermute x8, starting transfers between devices, moved(): return lax.ppermute(block, axis, [(0, 1), (1, 0)])  24.4 us
    all_to_all x3, waiting for transfers between devices, swap(): return lax.all_to_all(blocks, axis, split_axis=0, concat_axis=0, tiled=True)  18.3 us
    ppermute x8, waiting for transfers between devices, moved(): return lax.ppermute(block, axis, [(0, 1), (1, 0)])  11 us
    pallas_call x10, Pallas kernels, on_core(): pl.pallas_call(kernel, out_shape=out_shape, in_specs=[pl.BlockSpec(memory...  10.7 us
    all_gather x1, blocking collectives, body(): lax.all_gather(cols, 'core', axis=0)  4.09 us
    unnamed x20, local copies, waits for them, and re-layouts  3.8 us
  transfers between devices with their start and end apart: 11, of which 8 were waited for; matrix products, arithmetic and copies ran while one was open for 1% of the time, Pallas kernels for 4%

profile of v8, /device:TPU:1, one launch (start us, length us, event | category | flops | bytes accessed | tf_op | source)
XLA Modules:
  0.0 155.6 jit_solution(10641039934908433096)
XLA Ops:
  0.6 0.0 copy-start
  0.6 1.7 %shard_map.119 = bf16[32,8,320]{2,1,0:T(8,128)(2,1)} custom-call(bf16[1,1,2,2,5120]{4,3,2,1,0:T(2,128)(2,1)} %acts_ref.1, bf16[1,1,2,2,5120]{4,3,2,1,0:T(2,128)(2,1)} %cotan_ref.1), custom_call_target="tpu_custom_call" | custom-call | bytes 245760 | tf_op jit(solution)/shard_map/pallas_call | solution.py:324
  2.3 16.5 %all-to-all-start = ((bf16[32,8,320]{2,1,0:T(8,128)(2,1)}), bf16[32,8,320]{2,1,0:T(8,128)(2,1)S(1)}, u32[]{:S(2)}, u32[]{:S(2)}) async-start(bf16[32,8,320]{2,1,0:T(8,128)(2,1)} %shard_map.119), calls=%async_computation | async-start | bytes 393216 | tf_op jit(solution)/shard_map/all_to_all | solution.py:25
  18.9 3.1 %collective-permute-start = (bf16[80,2560]{1,0:T(8,128)(2,1)}, bf16[80,2560]{1,0:T(8,128)(2,1)S(1)}, u32[]{:S(2)}, u32[]{:S(2)}) collective-permute-start(bf16[80,2560]{1,0:T(8,128)(2,1)} %bitcast.33), channel_id=1, source_target_pairs={{0,2},{2,0},{1,3},{3,1},{4,6},{6,4},{5,7},{7,5},{8,10},{10,8},{9,1... | collective-permute-start | bytes 1228808 | tf_op jit(solution)/shard_map/ppermute | solution.py:29
  22.0 0.0 copy-done
  22.0 2.1 %collective-permute-start.2 = (bf16[40,5120]{1,0:T(8,128)(2,1)S(1)}, bf16[40,5120]{1,0:T(8,128)(2,1)S(1)}, u32[]{:S(2)}, u32[]{:S(2)}) collective-permute-start(bf16[40,5120]{1,0:T(8,128)(2,1)S(1)} %bitcast.28), channel_id=1, source_target_pairs={{0,2},{2,0},{1,3},{3,1},{4,6},{6,4},{5,7},{7,5},{8,10},{10,8},{9,1... | collective-permute-start | bytes 1228808 | tf_op jit(solution)/shard_map/ppermute | solution.py:29
  24.2 0.7 fusion.1
  24.8 0.1 convert_reduce_fusion.1
  24.9 0.7 add_multiply_fusion
  25.6 0.1 iota_add_fusion
  25.7 0.1 add.109
  25.8 0.0 copy-start.9
  25.8 0.1 broadcast_add_fusion.2
  25.9 0.1 pad_bitcast_fusion.1
  26.0 0.0 copy-start.1
  26.0 0.1 pad_add_fusion.1
  26.1 0.4 copy-done.9
  26.6 0.1 fusion.3
  26.6 0.1 broadcast_in_dim.7
  26.7 0.1 broadcast_in_dim.8
  26.8 0.1 pad_maximum_fusion.gain_ref
  26.9 3.9 %all-to-all-done = bf16[32,8,320]{2,1,0:T(8,128)(2,1)S(1)} async-done(((bf16[32,8,320]{2,1,0:T(8,128)(2,1)}), bf16[32,8,320]{2,1,0:T(8,128)(2,1)S(1)}, u32[]{:S(2)}, u32[]{:S(2)}) %all-to-all-start) | async-done | bytes 163872 | tf_op jit(solution)/shard_map/all_to_all | solution.py:25
  30.8 4.1 %all-gather = bf16[64,8,320]{2,1,0:T(8,128)(2,1)S(1)} all-gather(bf16[32,8,320]{2,1,0:T(8,128)(2,1)S(1)} %all-to-all-done), channel_id=2, replica_groups=mesh['section'=8,'team'=16,'pair'=2,'core'=2] {'core'}, dimensions={0}, use_global_device_ids=true | all-gather | bytes 491520 | tf_op jit(solution)/shard_map/all_gather | solution.py:388
  34.9 0.2 collective-permute-done.partner_ref
  35.1 0.0 copy-done.1
  35.1 1.1 shard_map.120
  36.2 3.8 %collective-permute-start.1 = (bf16[16,40,128]{2,1,0:T(8,128)(2,1)S(1)}, bf16[16,40,128]{2,1,0:T(8,128)(2,1)S(1)}, u32[]{:S(2)}, u32[]{:S(2)}) collective-permute-start(bf16[16,40,128]{2,1,0:T(8,128)(2,1)S(1)} %get-tuple-element.29), channel_id=1, source_target_pairs={{0,1},{1,0},{2,3},{3,2},{4,5},{5,4},{6,7},{7,6},{8,9},{9,8},{10,11... | collective-permute-start | bytes 491528 | tf_op jit(solution)/shard_map/ppermute | solution.py:29
  39.9 1.0 collective-permute-done.1.arrived_ref
  40.9 0.1 shard_map.121
  41.0 2.8 %collective-permute-done.2.partner_ref = bf16[40,5120]{1,0:T(8,128)(2,1)S(1)} collective-permute-done((bf16[40,5120]{1,0:T(8,128)(2,1)S(1)}, bf16[40,5120]{1,0:T(8,128)(2,1)S(1)}, u32[]{:S(2)}, u32[]{:S(2)}) %collective-permute-start.2) | collective-permute-done | bytes 409632 | tf_op jit(solution)/shard_map/ppermute | solution.py:29
  43.8 28.1 %all_to_all.25.trip_ref.mine_ref = bf16[16,120,128]{2,1,0:T(8,128)(2,1)S(1)} all-to-all(bf16[16,120,128]{2,1,0:T(8,128)(2,1)S(1)} %shard_map.121), channel_id=1, replica_groups=mesh['section'=8,'team'=16,'pair'=2,'core'=2] {'team'}, dimensions={0} | all-to-all | bytes 983040 | tf_op jit(solution)/shard_map/all_to_all | solution.py:25
  71.9 4.0 %collective-permute-start.4 = (bf16[16,120,128]{2,1,0:T(8,128)(2,1)S(1)}, bf16[16,120,128]{2,1,0:T(8,128)(2,1)S(1)}, u32[]{:S(2)}, u32[]{:S(2)}) collective-permute-start(bf16[16,120,128]{2,1,0:T(8,128)(2,1)S(1)} %all_to_all.25.trip_ref.mine_ref), channel_id=1, source_target_pairs={{0,1},{1,0},{2,3},{3,2},{4,5},{5,4},{6,7},{7,6},{8,9},{9,8},{10,11... | collective-permute-start | bytes 1474568 | tf_op jit(solution)/shard_map/ppermute | solution.py:29
  76.0 1.0 shard_map.122
  76.9 1.9 %collective-permute-start.3 = (bf16[16,80,128]{2,1,0:T(8,128)(2,1)S(1)}, bf16[16,80,128]{2,1,0:T(8,128)(2,1)S(1)}, u32[]{:S(2)}, u32[]{:S(2)}) collective-permute-start(bf16[16,80,128]{2,1,0:T(8,128)(2,1)S(1)} %get-tuple-element.34), channel_id=1, source_target_pairs={{0,1},{1,0},{2,3},{3,2},{4,5},{5,4},{6,7},{7,6},{8,9},{9,8},{10,11... | collective-permute-start | bytes 983048 | tf_op jit(solution)/shard_map/ppermute | solution.py:29
  78.9 2.7 %collective-permute-start.5 = (bf16[16,80,128]{2,1,0:T(8,128)(2,1)S(1)}, bf16[16,80,128]{2,1,0:T(8,128)(2,1)S(1)}, u32[]{:S(2)}, u32[]{:S(2)}) collective-permute-start(bf16[16,80,128]{2,1,0:T(8,128)(2,1)S(1)} %slice.12), channel_id=1, source_target_pairs={{0,2},{2,0},{1,3},{3,1},{4,6},{6,4},{5,7},{7,5},{8,10},{10,8},{9,1... | collective-permute-start | bytes 983048 | tf_op jit(solution)/shard_map/ppermute | solution.py:29
  81.6 0.0 collective-permute-done.4.other_ref
  81.6 1.6 %shard_map.123 = (bf16[48,128]{1,0:T(8,128)(2,1)S(1)}, f32[40,5120]{1,0:T(8,128)S(1)}, f32[8,128]{1,0:T(8,128)S(1)}) custom-call(s32[1]{0:T(128)} %bitcast.3.core_ref, s32[1]{0:T(128)} %bitcast.2.pair_ref, bf16[16,120,128]{2,1,0:T(8,128)(2,1)S(1)} %all_to_all.25.trip_ref.mine_ref, bf16[16,120,128]{2,1,0:T(8,128)(2,1)S(1)} %collective-permute-done.4.other_ref, ...), custom_call_target="tpu_custom_call" | custom-call | bytes 2658304 | tf_op jit(solution)/shard_map/pallas_call | solution.py:324
  83.2 0.0 collective-permute-done.3.arrived_ref
  83.2 0.9 shard_map.124
  84.1 5.4 %collective-permute-done.5.mine_ref = bf16[16,80,128]{2,1,0:T(8,128)(2,1)S(1)} collective-permute-done((bf16[16,80,128]{2,1,0:T(8,128)(2,1)S(1)}, bf16[16,80,128]{2,1,0:T(8,128)(2,1)S(1)}, u32[]{:S(2)}, u32[]{:S(2)}) %collective-permute-start.5) | collective-permute-done | bytes 327712 | tf_op jit(solution)/shard_map/ppermute | solution.py:29
  89.6 0.0 copy-start.5
  89.6 4.4 %all-to-all-start.2 = ((bf16[16,128,128]{2,1,0:T(8,128)(2,1)}), bf16[16,128,128]{2,1,0:T(8,128)(2,1)S(1)}, u32[]{:S(2)}, u32[]{:S(2)}) async-start(bf16[16,128,128]{2,1,0:T(8,128)(2,1)} %shard_map.124), calls=%async_computation.2 | async-start | bytes 1048576 | tf_op jit(solution)/shard_map/all_to_all | solution.py:25
  93.9 0.0 copy-done.5
  94.0 3.5 %collective-permute-start.6 = (bf16[16,80,128]{2,1,0:T(8,128)(2,1)S(1)}, bf16[16,80,128]{2,1,0:T(8,128)(2,1)S(1)}, u32[]{:S(2)}, u32[]{:S(2)}) collective-permute-start(bf16[16,80,128]{2,1,0:T(8,128)(2,1)S(1)} %collective-permute-done.5.mine_ref), channel_id=1, source_target_pairs={{0,1},{1,0},{2,3},{3,2},{4,5},{5,4},{6,7},{7,6},{8,9},{9,8},{10,11... | collective-permute-start | bytes 983048 | tf_op jit(solution)/shard_map/ppermute | solution.py:29
  97.5 3.2 %collective-permute-start.7 = (bf16[40,128]{1,0:T(8,128)(2,1)S(1)}, bf16[40,128]{1,0:T(8,128)(2,1)S(1)}, u32[]{:S(2)}, u32[]{:S(2)}) collective-permute-start(bf16[40,128]{1,0:T(8,128)(2,1)S(1)} %get-tuple-element.42.grads_ref), channel_id=1, source_target_pairs={{0,2},{2,0},{1,3},{3,1},{4,6},{6,4},{5,7},{7,5},{8,10},{10,8},{9,1... | collective-permute-start | bytes 30728 | tf_op jit(solution)/shard_map/ppermute | solution.py:29
  100.7 1.5 collective-permute-done.7.grads_ref
  102.2 0.0 collective-permute-done.6.other_ref
  102.2 0.7 copy-done.7
  102.9 1.0 copy-done.6
  103.9 1.0 copy-done.8
  104.9 1.2 shard_map.125
  106.1 8.7 %all-to-all-done.2.trip_ref = bf16[16,128,128]{2,1,0:T(8,128)(2,1)S(1)} async-done(((bf16[16,128,128]{2,1,0:T(8,128)(2,1)}), bf16[16,128,128]{2,1,0:T(8,128)(2,1)S(1)}, u32[]{:S(2)}, u32[]{:S(2)}) %all-to-all-start.2) | async-done | bytes 524320 | tf_op jit(solution)/shard_map/all_to_all | solution.py:25
  114.8 2.9 %all-gather.1 = bf16[16,96,128]{2,1,0:T(8,128)(2,1)S(1)} all-gather(bf16[16,48,128]{2,1,0:T(8,128)(2,1)S(1)} %slice.13), channel_id=3, replica_groups=mesh['section'=8,'team'=16,'pair'=2,'core'=2] {'core'}, dimensions={1}, use_global_device_ids=true | all-gather | bytes 589824 | tf_op jit(solution)/shard_map/all_gather | solution.py:440
  117.8 0.5 shard_map.126
  118.2 0.0 copy-start.4
  118.2 0.7 copy-done.4
  118.9 4.1 %all-to-all-start.3 = ((bf16[8,88,128]{2,1,0:T(8,128)(2,1)}), bf16[8,88,128]{2,1,0:T(8,128)(2,1)S(1)}, u32[]{:S(2)}, u32[]{:S(2)}) async-start(bf16[8,88,128]{2,1,0:T(8,128)(2,1)} %copy-done.4), calls=%async_computation.3 | async-start | bytes 360448 | tf_op jit(solution)/shard_map/all_to_all | solution.py:25
  123.1 0.1 pad_add_fusion.2.from_ref
  123.1 5.8 %all-to-all-done.3.trip_ref = bf16[8,88,128]{2,1,0:T(8,128)(2,1)S(1)} async-done(((bf16[8,88,128]{2,1,0:T(8,128)(2,1)}), bf16[8,88,128]{2,1,0:T(8,128)(2,1)S(1)}, u32[]{:S(2)}, u32[]{:S(2)}) %all-to-all-start.3) | async-done | bytes 180256 | tf_op jit(solution)/shard_map/all_to_all | solution.py:25
  128.9 0.8 shard_map.127
  129.7 24.0 %all_to_all.26.trip_ref = bf16[64,16,128]{2,1,0:T(8,128)(2,1)S(1)} all-to-all(bf16[64,16,128]{2,1,0:T(8,128)(2,1)S(1)} %bitcast.37), channel_id=1, replica_groups=mesh['section'=8,'team'=16,'pair'=2,'core'=2] {'team','pair','core'}, dimensions={0} | all-to-all | bytes 524288 | tf_op jit(solution)/shard_map/all_to_all | solution.py:25
  153.7 0.0 copy-done.3
  153.7 0.0 copy-done.2
  153.7 1.9 %shard_map.128 = (bf16[1,1,2,2,5120]{4,3,2,1,0:T(2,128)(2,1)}, bf16[1,1,2,2,5120]{4,3,2,1,0:T(2,128)(2,1)}, bf16[1,40,5120]{2,1,0:T(8,128)(2,1)}, f32[1,40,5120]{2,1,0:T(8,128)}, f32[1,40,5120]{2,1,0:T(8,128)}) custom-call(bf16[64,16,128]{2,1,0:T(8,128)(2,1)S(1)} %all_to_all.26.trip_ref, f32[40,5120]{1,0:T(8,128)S(1)} %get-tuple-element.46.gradient_ref, ...), custom_call_target="tpu_custom_call" | custom-call | bytes 5259264 | tf_op jit(solution)/shard_map/pallas_call | solution.py:324
  (10 shorter events, 0.1 us)
Async XLA Ops:
  0.6 21.4 %copy-start = (bf16[1,40,5120]{2,1,0:T(8,128)(2,1)S(1)}, bf16[1,40,5120]{2,1,0:T(8,128)(2,1)}, u32[]{:S(2)}) copy-start(bf16[1,40,5120]{2,1,0:T(8,128)(2,1)} %weight_ref.1) | copy-start | bytes 1228804
  2.3 28.5 %all-to-all-start = ((bf16[32,8,320]{2,1,0:T(8,128)(2,1)}), bf16[32,8,320]{2,1,0:T(8,128)(2,1)S(1)}, u32[]{:S(2)}, u32[]{:S(2)}) async-start(bf16[32,8,320]{2,1,0:T(8,128)(2,1)} %shard_map.119), calls=%async_computation | async-start | bytes 393216 | tf_op jit(solution)/shard_map/all_to_all | solution.py:25
  18.9 16.2 %collective-permute-start = (bf16[80,2560]{1,0:T(8,128)(2,1)}, bf16[80,2560]{1,0:T(8,128)(2,1)S(1)}, u32[]{:S(2)}, u32[]{:S(2)}) collective-permute-start(bf16[80,2560]{1,0:T(8,128)(2,1)} %bitcast.33), channel_id=1, source_target_pairs={{0,2},{2,0},{1,3},{3,1},{4,6},{6,4},{5,7},{7,5},{8,10},{10,8},{9,1... | collective-permute-start | bytes 1228808 | tf_op jit(solution)/shard_map/ppermute | solution.py:29
  22.0 21.8 %collective-permute-start.2 = (bf16[40,5120]{1,0:T(8,128)(2,1)S(1)}, bf16[40,5120]{1,0:T(8,128)(2,1)S(1)}, u32[]{:S(2)}, u32[]{:S(2)}) collective-permute-start(bf16[40,5120]{1,0:T(8,128)(2,1)S(1)} %bitcast.28), channel_id=1, source_target_pairs={{0,2},{2,0},{1,3},{3,1},{4,6},{6,4},{5,7},{7,5},{8,10},{10,8},{9,1... | collective-permute-start | bytes 1228808 | tf_op jit(solution)/shard_map/ppermute | solution.py:29
  25.8 0.7 copy-start.9
  26.0 9.0 %copy-start.1 = (bf16[1,80,2560]{2,1,0:T(8,128)(2,1)S(1)}, bf16[1,80,2560]{2,1,0:T(8,128)(2,1)}, u32[]{:S(2)}) copy-start(bf16[1,80,2560]{2,1,0:T(8,128)(2,1)} %param.13) | copy-start | bytes 1228804
  36.2 4.8 %collective-permute-start.1 = (bf16[16,40,128]{2,1,0:T(8,128)(2,1)S(1)}, bf16[16,40,128]{2,1,0:T(8,128)(2,1)S(1)}, u32[]{:S(2)}, u32[]{:S(2)}) collective-permute-start(bf16[16,40,128]{2,1,0:T(8,128)(2,1)S(1)} %get-tuple-element.29), channel_id=1, source_target_pairs={{0,1},{1,0},{2,3},{3,2},{4,5},{5,4},{6,7},{7,6},{8,9},{9,8},{10,11... | collective-permute-start | bytes 491528 | tf_op jit(solution)/shard_map/ppermute | solution.py:29
  71.9 9.7 %collective-permute-start.4 = (bf16[16,120,128]{2,1,0:T(8,128)(2,1)S(1)}, bf16[16,120,128]{2,1,0:T(8,128)(2,1)S(1)}, u32[]{:S(2)}, u32[]{:S(2)}) collective-permute-start(bf16[16,120,128]{2,1,0:T(8,128)(2,1)S(1)} %all_to_all.25.trip_ref.mine_ref), channel_id=1, source_target_pairs={{0,1},{1,0},{2,3},{3,2},{4,5},{5,4},{6,7},{7,6},{8,9},{9,8},{10,11... | collective-permute-start | bytes 1474568 | tf_op jit(solution)/shard_map/ppermute | solution.py:29
  76.9 6.3 %collective-permute-start.3 = (bf16[16,80,128]{2,1,0:T(8,128)(2,1)S(1)}, bf16[16,80,128]{2,1,0:T(8,128)(2,1)S(1)}, u32[]{:S(2)}, u32[]{:S(2)}) collective-permute-start(bf16[16,80,128]{2,1,0:T(8,128)(2,1)S(1)} %get-tuple-element.34), channel_id=1, source_target_pairs={{0,1},{1,0},{2,3},{3,2},{4,5},{5,4},{6,7},{7,6},{8,9},{9,8},{10,11... | collective-permute-start | bytes 983048 | tf_op jit(solution)/shard_map/ppermute | solution.py:29
  78.9 10.7 %collective-permute-start.5 = (bf16[16,80,128]{2,1,0:T(8,128)(2,1)S(1)}, bf16[16,80,128]{2,1,0:T(8,128)(2,1)S(1)}, u32[]{:S(2)}, u32[]{:S(2)}) collective-permute-start(bf16[16,80,128]{2,1,0:T(8,128)(2,1)S(1)} %slice.12), channel_id=1, source_target_pairs={{0,2},{2,0},{1,3},{3,1},{4,6},{6,4},{5,7},{7,5},{8,10},{10,8},{9,1... | collective-permute-start | bytes 983048 | tf_op jit(solution)/shard_map/ppermute | solution.py:29
  89.6 4.4 %copy-start.5 = (bf16[16,80,128]{2,1,0:T(8,128)(2,1)}, bf16[16,80,128]{2,1,0:T(8,128)(2,1)S(1)}, u32[]{:S(2)}) copy-start(bf16[16,80,128]{2,1,0:T(8,128)(2,1)S(1)} %collective-permute-done.5.mine_ref) | copy-start | bytes 983044
  89.6 25.2 %all-to-all-start.2 = ((bf16[16,128,128]{2,1,0:T(8,128)(2,1)}), bf16[16,128,128]{2,1,0:T(8,128)(2,1)S(1)}, u32[]{:S(2)}, u32[]{:S(2)}) async-start(bf16[16,128,128]{2,1,0:T(8,128)(2,1)} %shard_map.124), calls=%async_computation.2 | async-start | bytes 1048576 | tf_op jit(solution)/shard_map/all_to_all | solution.py:25
  94.0 8.3 %collective-permute-start.6 = (bf16[16,80,128]{2,1,0:T(8,128)(2,1)S(1)}, bf16[16,80,128]{2,1,0:T(8,128)(2,1)S(1)}, u32[]{:S(2)}, u32[]{:S(2)}) collective-permute-start(bf16[16,80,128]{2,1,0:T(8,128)(2,1)S(1)} %collective-permute-done.5.mine_ref), channel_id=1, source_target_pairs={{0,1},{1,0},{2,3},{3,2},{4,5},{5,4},{6,7},{7,6},{8,9},{9,8},{10,11... | collective-permute-start | bytes 983048 | tf_op jit(solution)/shard_map/ppermute | solution.py:29
  97.5 4.7 %collective-permute-start.7 = (bf16[40,128]{1,0:T(8,128)(2,1)S(1)}, bf16[40,128]{1,0:T(8,128)(2,1)S(1)}, u32[]{:S(2)}, u32[]{:S(2)}) collective-permute-start(bf16[40,128]{1,0:T(8,128)(2,1)S(1)} %get-tuple-element.42.grads_ref), channel_id=1, source_target_pairs={{0,2},{2,0},{1,3},{3,1},{4,6},{6,4},{5,7},{7,5},{8,10},{10,8},{9,1... | collective-permute-start | bytes 30728 | tf_op jit(solution)/shard_map/ppermute | solution.py:29
  102.2 0.7 copy-start.7
  102.9 1.0 copy-start.6
  103.9 1.0 copy-start.8
  117.8 35.9 %copy-start.3 = (f32[1,40,5120]{2,1,0:T(8,128)S(1)}, f32[1,40,5120]{2,1,0:T(8,128)}, u32[]{:S(2)}) copy-start(f32[1,40,5120]{2,1,0:T(8,128)} %second_ref.1) | copy-start | bytes 2457604
  118.2 0.7 copy-start.4
  118.9 34.8 %copy-start.2 = (f32[1,40,5120]{2,1,0:T(8,128)S(1)}, f32[1,40,5120]{2,1,0:T(8,128)}, u32[]{:S(2)}) copy-start(f32[1,40,5120]{2,1,0:T(8,128)} %first_ref.1) | copy-start | bytes 2457604
  118.9 10.0 %all-to-all-start.3 = ((bf16[8,88,128]{2,1,0:T(8,128)(2,1)}), bf16[8,88,128]{2,1,0:T(8,128)(2,1)S(1)}, u32[]{:S(2)}, u32[]{:S(2)}) async-start(bf16[8,88,128]{2,1,0:T(8,128)(2,1)} %copy-done.4), calls=%async_computation.3 | async-start | bytes 360448 | tf_op jit(solution)/shard_map/all_to_all | solution.py:25

commit v9 on v8

--- a/solution.py
+++ b/solution.py
@@ -139,14 +139,18 @@
         out_ref[chip, own_at : own_at + own.shape[0], :] = own
 
 
+def summed_grads(width, trip_ref):
+    total = trip_ref[0, width:, :].astype(jnp.float32)
+    for chip in range(1, trip_ref.shape[0]):
+        total += trip_ref[chip, width:, :].astype(jnp.float32)
+    return total.astype(jnp.bfloat16)
+
+
 def dnormed_kernel(
-    width, heads, core_ref, pair_ref, trip_ref, weight_ref, partner_ref,
+    width, core_ref, pair_ref, trip_ref, weight_ref, partner_ref,
     grads_ref, mine_ref, other_ref,
 ):
-    total = trip_ref[0, width : width + heads, :].astype(jnp.float32)
-    for chip in range(1, trip_ref.shape[0]):
-        total += trip_ref[chip, width : width + heads, :].astype(jnp.float32)
-    grads = total.astype(jnp.bfloat16)
+    grads = summed_grads(width, trip_ref)
     grads_ref[...] = grads
     first_core, first_pair = core_ref[0] == 0, pair_ref[0] == 0
     refs = (weight_ref, partner_ref)
@@ -205,13 +209,13 @@
 
 
 def gradient_kernel(
-    width, core_ref, pair_ref, mine_ref, other_ref, gain_ref, grads_ref, half_ref,
+    width, core_ref, pair_ref, mine_ref, other_ref, gain_ref, half_ref,
     gradient_ref, norms_ref, normed_ref,
 ):
     lanes = norms_ref.shape[1]
     first_core, first_pair = core_ref[0] == 0, pair_ref[0] == 0
     normalise(width, first_core, mine_ref, other_ref, gain_ref, normed_ref)
-    grads = grads_ref[...].astype(jnp.float32)
+    grads = summed_grads(width, mine_ref).astype(jnp.float32)
     own = pieces_apart(grads, first_pair)[0].astype(jnp.bfloat16)
     norms = jnp.zeros((half_ref.shape[0], lanes), jnp.float32)
     span = 8 * width
@@ -400,12 +404,11 @@
         [],
         [mine, arrived, stream],
     )
-    payload, pair_weights = lax.optimization_barrier((payload, pair_weights))
     first_trip = swap(payload, TEAM)
     other_trip = moved(first_trip, "core")
-    pair_mine = moved(first_trip[:, :width], "pair")
+    pair_trip = moved(first_trip, "pair")
     value_grads, mine, other = on_core(
-        functools.partial(dnormed_kernel, width, heads),
+        functools.partial(dnormed_kernel, width),
         [shape((heads, rows))] + [shape((team, width, rows))] * 2,
         [core, pair],
         [first_trip, weights, pair_weights],
@@ -428,13 +431,12 @@
         [],
         [mine, arrived, own],
     )
-    payload, pair_mine, pair_grads = lax.optimization_barrier((payload, pair_mine, value_grads))
     second_trip = swap(payload, TEAM)
     gradient, norms = on_core(
         functools.partial(gradient_kernel, width),
         [shape((heads, model), full), shape((SPARE, rows), full)],
         [core, pair],
-        [pair_mine, moved(pair_mine, "core"), gain, moved(pair_grads, "pair"), half_gradient],
+        [pair_trip, moved(pair_trip, "core"), gain, half_gradient],
         [pltpu.VMEM((model, rows), brief)],
     )
     gathered = lax.all_gather(second_trip[:, width:], "core", axis=1)

time: 156 us -> 154 us (0.987)
  blocking collectives: 59.1 us -> 28.1 us
  waiting for transfers between devices: 29.3 us -> 44.2 us
  starting transfers between devices: 49.4 us -> 59.3 us
    all_to_all x2 -> x1, blocking collectives: 52.1 us -> 20.8 us  [swap(): return lax.all_to_all(blocks, axis, split_axis=0, concat_axis=0, tiled=True)]
    all_to_all x3 -> x4, waiting for transfers between devices: 18.3 us -> 41.8 us  [swap(): return lax.all_to_all(blocks, axis, split_axis=0, concat_axis=0, tiled=True)]
    all_to_all x3 -> x4, starting transfers between devices: 25 us -> 39.9 us  [swap(): return lax.all_to_all(blocks, axis, split_axis=0, concat_axis=0, tiled=True)]
    ppermute x8 -> x7, waiting for transfers between devices: 11 us -> 2.48 us  [moved(): return lax.ppermute(block, axis, [(0, 1), (1, 0)])]
    ppermute x8 -> x7, starting transfers between devices: 24.4 us -> 19.4 us  [moved(): return lax.ppermute(block, axis, [(0, 1), (1, 0)])]
    unnamed x20 -> x36, local copies, waits for them, and re-layouts: 3.8 us -> 4.73 us
  transfers between devices with their start and end apart: 11 -> 11, of which waited for: 8 -> 6; matrix products, arithmetic and copies ran while one was open for 1% -> 2% of each run, Pallas kernels for 4% -> 3%
where the time goes in v9:
time: 154 us; the launch traced here: 153 us
  starting transfers between devices  59.3 us (39%)
  waiting for transfers between devices  44.2 us (29%)
  blocking collectives  28.1 us (18%)
  Pallas kernels  12.2 us (8%)
  local copies, waits for them, and re-layouts  5.77 us (4%)
  other arithmetic  2.5 us (2%)
    all_to_all x4, waiting for transfers between devices, swap(): return lax.all_to_all(blocks, axis, split_axis=0, concat_axis=0, tiled=True)  41.8 us
    all_to_all x4, starting transfers between devices, swap(): return lax.all_to_all(blocks, axis, split_axis=0, concat_axis=0, tiled=True)  39.9 us
    all_to_all x1, blocking collectives, swap(): return lax.all_to_all(blocks, axis, split_axis=0, concat_axis=0, tiled=True)  20.8 us
    ppermute x7, starting transfers between devices, moved(): return lax.ppermute(block, axis, [(0, 1), (1, 0)])  19.4 us
    pallas_call x10, Pallas kernels, on_core(): pl.pallas_call(kernel, out_shape=out_shape, in_specs=[pl.BlockSpec(memory...  12.2 us
    unnamed x36, local copies, waits for them, and re-layouts  4.73 us
    all_gather x1, blocking collectives, body(): lax.all_gather(cols, 'core', axis=0)  4.1 us
    all_gather x1, blocking collectives, body(): gathered = lax.all_gather(second_trip[:, width:], 'core', axis=1)  3.27 us
  transfers between devices with their start and end apart: 11, of which 6 were waited for; matrix products, arithmetic and copies ran while one was open for 2% of the time, Pallas kernels for 3%

profile of v9, /device:TPU:1, one launch (start us, length us, event | category | flops | bytes accessed | tf_op | source)
XLA Modules:
  0.0 153.1 jit_solution(10078181668761486138)
XLA Ops:
  0.6 0.0 copy-start.1
  0.6 1.7 %shard_map.119 = bf16[32,8,320]{2,1,0:T(8,128)(2,1)} custom-call(bf16[1,1,2,2,5120]{4,3,2,1,0:T(2,128)(2,1)} %acts_ref.1, bf16[1,1,2,2,5120]{4,3,2,1,0:T(2,128)(2,1)} %cotan_ref.1), custom_call_target="tpu_custom_call" | custom-call | bytes 245760 | tf_op jit(solution)/shard_map/pallas_call | solution.py:328
  2.3 16.5 %all-to-all-start = ((bf16[32,8,320]{2,1,0:T(8,128)(2,1)}), bf16[32,8,320]{2,1,0:T(8,128)(2,1)S(1)}, u32[]{:S(2)}, u32[]{:S(2)}) async-start(bf16[32,8,320]{2,1,0:T(8,128)(2,1)} %shard_map.119), calls=%async_computation | async-start | bytes 393216 | tf_op jit(solution)/shard_map/all_to_all | solution.py:25
  18.9 0.0 copy-done.1
  18.9 3.1 %collective-permute-start = (bf16[80,2560]{1,0:T(8,128)(2,1)S(1)}, bf16[80,2560]{1,0:T(8,128)(2,1)S(1)}, u32[]{:S(2)}, u32[]{:S(2)}) collective-permute-start(bf16[80,2560]{1,0:T(8,128)(2,1)S(1)} %bitcast.33), channel_id=1, source_target_pairs={{0,2},{2,0},{1,3},{3,1},{4,6},{6,4},{5,7},{7,5},{8,10},{10,8},{9,1... | collective-permute-start | bytes 1228808 | tf_op jit(solution)/shard_map/ppermute | solution.py:29
  22.0 0.7 fusion.1
  22.7 0.1 convert_reduce_fusion.1
  22.8 0.7 add_multiply_fusion
  23.4 0.1 iota_add_fusion
  23.5 0.1 add.109
  23.7 0.0 copy-start.7
  23.7 0.1 broadcast_add_fusion.2
  23.8 0.1 pad_bitcast_fusion.1
  23.9 0.7 pad_add_fusion.1
  24.5 0.0 copy-done.7
  24.5 0.1 fusion.3
  24.6 0.1 broadcast_in_dim.7
  24.7 0.1 broadcast_in_dim.8
  24.8 0.7 pad_maximum_fusion.gain_ref
  25.5 5.3 %all-to-all-done = bf16[32,8,320]{2,1,0:T(8,128)(2,1)S(1)} async-done(((bf16[32,8,320]{2,1,0:T(8,128)(2,1)}), bf16[32,8,320]{2,1,0:T(8,128)(2,1)S(1)}, u32[]{:S(2)}, u32[]{:S(2)}) %all-to-all-start) | async-done | bytes 163872 | tf_op jit(solution)/shard_map/all_to_all | solution.py:25
  30.8 4.1 %all-gather = bf16[64,8,320]{2,1,0:T(8,128)(2,1)S(1)} all-gather(bf16[32,8,320]{2,1,0:T(8,128)(2,1)S(1)} %all-to-all-done), channel_id=2, replica_groups=mesh['section'=8,'team'=16,'pair'=2,'core'=2] {'core'}, dimensions={0}, use_global_device_ids=true | all-gather | bytes 491520 | tf_op jit(solution)/shard_map/all_gather | solution.py:392
  34.9 0.0 collective-permute-done.partner_ref
  34.9 1.1 shard_map.120
  36.0 0.0 copy-start.11
  36.0 3.0 %collective-permute-start.1 = (bf16[16,40,128]{2,1,0:T(8,128)(2,1)S(1)}, bf16[16,40,128]{2,1,0:T(8,128)(2,1)S(1)}, u32[]{:S(2)}, u32[]{:S(2)}) collective-permute-start(bf16[16,40,128]{2,1,0:T(8,128)(2,1)S(1)} %get-tuple-element.24), channel_id=1, source_target_pairs={{0,1},{1,0},{2,3},{3,2},{4,5},{5,4},{6,7},{7,6},{8,9},{9,8},{10,11... | collective-permute-start | bytes 491528 | tf_op jit(solution)/shard_map/ppermute | solution.py:29
  39.0 1.0 collective-permute-done.1.arrived_ref
  40.0 0.9 shard_map.121
  40.9 0.6 copy-done.9
  41.5 9.3 %all-to-all-start.1 = ((bf16[16,120,128]{2,1,0:T(8,128)(2,1)}), bf16[16,120,128]{2,1,0:T(8,128)(2,1)S(1)}, u32[]{:S(2)}, u32[]{:S(2)}) async-start(bf16[16,120,128]{2,1,0:T(8,128)(2,1)} %shard_map.121), calls=%async_computation.1 | async-start | bytes 983040 | tf_op jit(solution)/shard_map/all_to_all | solution.py:25
  50.9 3.1 %collective-permute-start.2 = (bf16[40,5120]{1,0:T(8,128)(2,1)S(1)}, bf16[40,5120]{1,0:T(8,128)(2,1)S(1)}, u32[]{:S(2)}, u32[]{:S(2)}) collective-permute-start(bf16[40,5120]{1,0:T(8,128)(2,1)S(1)} %bitcast.28), channel_id=1, source_target_pairs={{0,2},{2,0},{1,3},{3,1},{4,6},{6,4},{5,7},{7,5},{8,10},{10,8},{9,1... | collective-permute-start | bytes 1228808 | tf_op jit(solution)/shard_map/ppermute | solution.py:29
  54.0 17.2 %all-to-all-done.1.trip_ref.mine_ref = bf16[16,120,128]{2,1,0:T(8,128)(2,1)S(1)} async-done(((bf16[16,120,128]{2,1,0:T(8,128)(2,1)}), bf16[16,120,128]{2,1,0:T(8,128)(2,1)S(1)}, u32[]{:S(2)}, u32[]{:S(2)}) %all-to-all-start.1) | async-done | bytes 491552 | tf_op jit(solution)/shard_map/all_to_all | solution.py:25
  71.1 3.2 %collective-permute-start.4 = (bf16[16,120,128]{2,1,0:T(8,128)(2,1)S(1)}, bf16[16,120,128]{2,1,0:T(8,128)(2,1)S(1)}, u32[]{:S(2)}, u32[]{:S(2)}) collective-permute-start(bf16[16,120,128]{2,1,0:T(8,128)(2,1)S(1)} %all-to-all-done.1.trip_ref.mine_ref), channel_id=1, source_target_pairs={{0,1},{1,0},{2,3},{3,2},{4,5},{5,4},{6,7},{7,6},{8,9},{9,8},{10,11... | collective-permute-start | bytes 1474568 | tf_op jit(solution)/shard_map/ppermute | solution.py:29
  74.3 0.0 collective-permute-done.2.partner_ref
  74.4 1.0 shard_map.122
  75.3 1.9 %collective-permute-start.3 = (bf16[16,80,128]{2,1,0:T(8,128)(2,1)S(1)}, bf16[16,80,128]{2,1,0:T(8,128)(2,1)S(1)}, u32[]{:S(2)}, u32[]{:S(2)}) collective-permute-start(bf16[16,80,128]{2,1,0:T(8,128)(2,1)S(1)} %get-tuple-element.27), channel_id=1, source_target_pairs={{0,1},{1,0},{2,3},{3,2},{4,5},{5,4},{6,7},{7,6},{8,9},{9,8},{10,11... | collective-permute-start | bytes 983048 | tf_op jit(solution)/shard_map/ppermute | solution.py:29
  77.2 2.6 %collective-permute-start.5 = (bf16[16,120,128]{2,1,0:T(8,128)(2,1)S(1)}, bf16[16,120,128]{2,1,0:T(8,128)(2,1)S(1)}, u32[]{:S(2)}, u32[]{:S(2)}) collective-permute-start(bf16[16,120,128]{2,1,0:T(8,128)(2,1)S(1)} %all-to-all-done.1.trip_ref.mine_ref), channel_id=1, source_target_pairs={{0,2},{2,0},{1,3},{3,1},{4,6},{6,4},{5,7},{7,5},{8,10},{10,8},{9,1... | collective-permute-start | bytes 1474568 | tf_op jit(solution)/shard_map/ppermute | solution.py:29
  79.8 0.0 collective-permute-done.4.other_ref
  79.8 1.6 %shard_map.123 = (bf16[48,128]{1,0:T(8,128)(2,1)S(1)}, f32[40,5120]{1,0:T(8,128)S(1)}, f32[8,128]{1,0:T(8,128)S(1)}) custom-call(s32[1]{0:T(128)} %bitcast.3.core_ref, s32[1]{0:T(128)} %bitcast.2.pair_ref, bf16[16,120,128]{2,1,0:T(8,128)(2,1)S(1)} %all-to-all-done.1.trip_ref.mine_ref, bf16[16,120,128]{2,1,0:T(8,128)(2,1)S(1)} %collective-permute-done.4.other_ref, ...), custom_call_target="tpu_custom_call" | custom-call | bytes 2658304 | tf_op jit(solution)/shard_map/pallas_call | solution.py:328
  81.4 0.0 collective-permute-done.3.arrived_ref
  81.4 0.9 shard_map.124
  82.3 9.9 %all-to-all-start.2 = ((bf16[16,128,128]{2,1,0:T(8,128)(2,1)}), bf16[16,128,128]{2,1,0:T(8,128)(2,1)S(1)}, u32[]{:S(2)}, u32[]{:S(2)}) async-start(bf16[16,128,128]{2,1,0:T(8,128)(2,1)} %shard_map.124), calls=%async_computation.2 | async-start | bytes 1048576 | tf_op jit(solution)/shard_map/all_to_all | solution.py:25
  92.2 0.0 collective-permute-done.5.mine_ref
  92.3 2.5 %collective-permute-start.6 = (bf16[16,120,128]{2,1,0:T(8,128)(2,1)S(1)}, bf16[16,120,128]{2,1,0:T(8,128)(2,1)S(1)}, u32[]{:S(2)}, u32[]{:S(2)}) collective-permute-start(bf16[16,120,128]{2,1,0:T(8,128)(2,1)S(1)} %collective-permute-done.5.mine_ref), channel_id=1, source_target_pairs={{0,1},{1,0},{2,3},{3,2},{4,5},{5,4},{6,7},{7,6},{8,9},{9,8},{10,11... | collective-permute-start | bytes 1474568 | tf_op jit(solution)/shard_map/ppermute | solution.py:29
  94.8 1.5 collective-permute-done.6.other_ref
  96.2 0.7 copy-done.8
  96.9 1.3 shard_map.125
  98.2 0.0 copy-start.4
  98.3 0.9 copy-done.4
  99.1 0.6 copy-done.15
  99.7 13.5 %all-to-all-done.2.trip_ref = bf16[16,128,128]{2,1,0:T(8,128)(2,1)S(1)} async-done(((bf16[16,128,128]{2,1,0:T(8,128)(2,1)}), bf16[16,128,128]{2,1,0:T(8,128)(2,1)S(1)}, u32[]{:S(2)}, u32[]{:S(2)}) %all-to-all-start.2) | async-done | bytes 524320 | tf_op jit(solution)/shard_map/all_to_all | solution.py:25
  113.3 0.0 copy-start.12
  113.3 3.3 %all-gather.1 = bf16[16,96,128]{2,1,0:T(8,128)(2,1)S(1)} all-gather(bf16[16,48,128]{2,1,0:T(8,128)(2,1)S(1)} %slice.8), channel_id=3, replica_groups=mesh['section'=8,'team'=16,'pair'=2,'core'=2] {'core'}, dimensions={1}, use_global_device_ids=true | all-gather | bytes 589824 | tf_op jit(solution)/shard_map/all_gather | solution.py:442
  116.6 0.7 copy-done.6
  117.3 0.0 copy-done.14
  117.3 0.0 copy-start.3
  117.3 1.1 shard_map.126
  118.5 4.1 %all-to-all-start.3 = ((bf16[8,88,128]{2,1,0:T(8,128)(2,1)}), bf16[8,88,128]{2,1,0:T(8,128)(2,1)S(1)}, u32[]{:S(2)}, u32[]{:S(2)}) async-start(bf16[8,88,128]{2,1,0:T(8,128)(2,1)} %shard_map.126), calls=%async_computation.3 | async-start | bytes 360448 | tf_op jit(solution)/shard_map/all_to_all | solution.py:25
  122.6 0.1 pad_add_fusion.2.from_ref
  122.7 5.8 %all-to-all-done.3.trip_ref = bf16[8,88,128]{2,1,0:T(8,128)(2,1)S(1)} async-done(((bf16[8,88,128]{2,1,0:T(8,128)(2,1)}), bf16[8,88,128]{2,1,0:T(8,128)(2,1)S(1)}, u32[]{:S(2)}, u32[]{:S(2)}) %all-to-all-start.3) | async-done | bytes 180256 | tf_op jit(solution)/shard_map/all_to_all | solution.py:25
  128.4 0.8 shard_map.127
  129.3 20.8 %all_to_all.25.trip_ref = bf16[64,16,128]{2,1,0:T(8,128)(2,1)S(1)} all-to-all(bf16[64,16,128]{2,1,0:T(8,128)(2,1)S(1)} %bitcast.37), channel_id=1, replica_groups=mesh['section'=8,'team'=16,'pair'=2,'core'=2] {'team','pair','core'}, dimensions={0} | all-to-all | bytes 524288 | tf_op jit(solution)/shard_map/all_to_all | solution.py:25
  150.1 0.0 copy-done.3
  150.1 1.1 copy-done.5
  151.2 1.9 %shard_map.128 = (bf16[1,1,2,2,5120]{4,3,2,1,0:T(2,128)(2,1)}, bf16[1,1,2,2,5120]{4,3,2,1,0:T(2,128)(2,1)}, bf16[1,40,5120]{2,1,0:T(8,128)(2,1)}, f32[1,40,5120]{2,1,0:T(8,128)}, f32[1,40,5120]{2,1,0:T(8,128)}) custom-call(bf16[64,16,128]{2,1,0:T(8,128)(2,1)S(1)} %all_to_all.25.trip_ref, f32[40,5120]{1,0:T(8,128)S(1)} %copy-done.5, ...), custom_call_target="tpu_custom_call" | custom-call | bytes 5259264 | tf_op jit(solution)/shard_map/pallas_call | solution.py:328
  (24 shorter events, 0.1 us)
Async XLA Ops:
  0.6 18.2 %copy-start.1 = (bf16[1,80,2560]{2,1,0:T(8,128)(2,1)S(1)}, bf16[1,80,2560]{2,1,0:T(8,128)(2,1)}, u32[]{:S(2)}) copy-start(bf16[1,80,2560]{2,1,0:T(8,128)(2,1)} %param.13) | copy-start | bytes 1228804
  2.3 28.5 %all-to-all-start = ((bf16[32,8,320]{2,1,0:T(8,128)(2,1)}), bf16[32,8,320]{2,1,0:T(8,128)(2,1)S(1)}, u32[]{:S(2)}, u32[]{:S(2)}) async-start(bf16[32,8,320]{2,1,0:T(8,128)(2,1)} %shard_map.119), calls=%async_computation | async-start | bytes 393216 | tf_op jit(solution)/shard_map/all_to_all | solution.py:25
  18.9 16.0 %collective-permute-start = (bf16[80,2560]{1,0:T(8,128)(2,1)S(1)}, bf16[80,2560]{1,0:T(8,128)(2,1)S(1)}, u32[]{:S(2)}, u32[]{:S(2)}) collective-permute-start(bf16[80,2560]{1,0:T(8,128)(2,1)S(1)} %bitcast.33), channel_id=1, source_target_pairs={{0,2},{2,0},{1,3},{3,1},{4,6},{6,4},{5,7},{7,5},{8,10},{10,8},{9,1... | collective-permute-start | bytes 1228808 | tf_op jit(solution)/shard_map/ppermute | solution.py:29
  23.7 0.9 copy-start.7
  36.0 4.9 %copy-start.11 = (bf16[80,128]{1,0:T(8,128)(2,1)}, bf16[80,128]{1,0:T(8,128)(2,1)S(1)}, u32[]{:S(2)}) copy-start(bf16[80,128]{1,0:T(8,128)(2,1)S(1)} %get-tuple-element.30.cotangent_ref) | copy-start | bytes 61444
  36.0 4.0 %collective-permute-start.1 = (bf16[16,40,128]{2,1,0:T(8,128)(2,1)S(1)}, bf16[16,40,128]{2,1,0:T(8,128)(2,1)S(1)}, u32[]{:S(2)}, u32[]{:S(2)}) collective-permute-start(bf16[16,40,128]{2,1,0:T(8,128)(2,1)S(1)} %get-tuple-element.24), channel_id=1, source_target_pairs={{0,1},{1,0},{2,3},{3,2},{4,5},{5,4},{6,7},{7,6},{8,9},{9,8},{10,11... | collective-permute-start | bytes 491528 | tf_op jit(solution)/shard_map/ppermute | solution.py:29
  40.9 0.6 copy-start.9
  41.5 9.4 %copy-start = (bf16[1,40,5120]{2,1,0:T(8,128)(2,1)S(1)}, bf16[1,40,5120]{2,1,0:T(8,128)(2,1)}, u32[]{:S(2)}) copy-start(bf16[1,40,5120]{2,1,0:T(8,128)(2,1)} %weight_ref.1) | copy-start | bytes 1228804
  41.5 29.6 %all-to-all-start.1 = ((bf16[16,120,128]{2,1,0:T(8,128)(2,1)}), bf16[16,120,128]{2,1,0:T(8,128)(2,1)S(1)}, u32[]{:S(2)}, u32[]{:S(2)}) async-start(bf16[16,120,128]{2,1,0:T(8,128)(2,1)} %shard_map.121), calls=%async_computation.1 | async-start | bytes 983040 | tf_op jit(solution)/shard_map/all_to_all | solution.py:25
  50.9 23.5 %collective-permute-start.2 = (bf16[40,5120]{1,0:T(8,128)(2,1)S(1)}, bf16[40,5120]{1,0:T(8,128)(2,1)S(1)}, u32[]{:S(2)}, u32[]{:S(2)}) collective-permute-start(bf16[40,5120]{1,0:T(8,128)(2,1)S(1)} %bitcast.28), channel_id=1, source_target_pairs={{0,2},{2,0},{1,3},{3,1},{4,6},{6,4},{5,7},{7,5},{8,10},{10,8},{9,1... | collective-permute-start | bytes 1228808 | tf_op jit(solution)/shard_map/ppermute | solution.py:29
  71.1 8.7 %collective-permute-start.4 = (bf16[16,120,128]{2,1,0:T(8,128)(2,1)S(1)}, bf16[16,120,128]{2,1,0:T(8,128)(2,1)S(1)}, u32[]{:S(2)}, u32[]{:S(2)}) collective-permute-start(bf16[16,120,128]{2,1,0:T(8,128)(2,1)S(1)} %all-to-all-done.1.trip_ref.mine_ref), channel_id=1, source_target_pairs={{0,1},{1,0},{2,3},{3,2},{4,5},{5,4},{6,7},{7,6},{8,9},{9,8},{10,11... | collective-permute-start | bytes 1474568 | tf_op jit(solution)/shard_map/ppermute | solution.py:29
  75.3 6.1 %collective-permute-start.3 = (bf16[16,80,128]{2,1,0:T(8,128)(2,1)S(1)}, bf16[16,80,128]{2,1,0:T(8,128)(2,1)S(1)}, u32[]{:S(2)}, u32[]{:S(2)}) collective-permute-start(bf16[16,80,128]{2,1,0:T(8,128)(2,1)S(1)} %get-tuple-element.27), channel_id=1, source_target_pairs={{0,1},{1,0},{2,3},{3,2},{4,5},{5,4},{6,7},{7,6},{8,9},{9,8},{10,11... | collective-permute-start | bytes 983048 | tf_op jit(solution)/shard_map/ppermute | solution.py:29
  77.2 15.0 %collective-permute-start.5 = (bf16[16,120,128]{2,1,0:T(8,128)(2,1)S(1)}, bf16[16,120,128]{2,1,0:T(8,128)(2,1)S(1)}, u32[]{:S(2)}, u32[]{:S(2)}) collective-permute-start(bf16[16,120,128]{2,1,0:T(8,128)(2,1)S(1)} %all-to-all-done.1.trip_ref.mine_ref), channel_id=1, source_target_pairs={{0,2},{2,0},{1,3},{3,1},{4,6},{6,4},{5,7},{7,5},{8,10},{10,8},{9,1... | collective-permute-start | bytes 1474568 | tf_op jit(solution)/shard_map/ppermute | solution.py:29
  81.4 0.9 copy-start.13
  82.3 30.9 %all-to-all-start.2 = ((bf16[16,128,128]{2,1,0:T(8,128)(2,1)}), bf16[16,128,128]{2,1,0:T(8,128)(2,1)S(1)}, u32[]{:S(2)}, u32[]{:S(2)}) async-start(bf16[16,128,128]{2,1,0:T(8,128)(2,1)} %shard_map.124), calls=%async_computation.2 | async-start | bytes 1048576 | tf_op jit(solution)/shard_map/all_to_all | solution.py:25
  92.3 4.0 %collective-permute-start.6 = (bf16[16,120,128]{2,1,0:T(8,128)(2,1)S(1)}, bf16[16,120,128]{2,1,0:T(8,128)(2,1)S(1)}, u32[]{:S(2)}, u32[]{:S(2)}) collective-permute-start(bf16[16,120,128]{2,1,0:T(8,128)(2,1)S(1)} %collective-permute-done.5.mine_ref), channel_id=1, source_target_pairs={{0,1},{1,0},{2,3},{3,2},{4,5},{5,4},{6,7},{7,6},{8,9},{9,8},{10,11... | collective-permute-start | bytes 1474568 | tf_op jit(solution)/shard_map/ppermute | solution.py:29
  96.2 0.7 copy-start.8
  98.2 0.9 copy-start.4
  99.1 0.6 copy-start.15
  113.3 3.3 %copy-start.12 = (bf16[80,128]{1,0:T(8,128)(2,1)S(1)}, bf16[80,128]{1,0:T(8,128)(2,1)}, u32[]{:S(2)}) copy-start(bf16[80,128]{1,0:T(8,128)(2,1)} %copy-done.11) | copy-start | bytes 61444
  116.5 0.8 copy-start.6
  116.5 0.8 copy-start.10
  116.5 0.8 copy-start.16
  116.6 0.7 copy-start.14
  117.3 11.1 %copy-start.17 = (s32[256]{0:T(256)S(1)}, s32[256]{0:T(256)}, u32[]{:S(2)}) copy-start(s32[256]{0:T(256)} %pad_add_fusion.1) | copy-start | bytes 3076
  117.3 32.7 %copy-start.3 = (f32[1,40,5120]{2,1,0:T(8,128)S(1)}, f32[1,40,5120]{2,1,0:T(8,128)}, u32[]{:S(2)}) copy-start(f32[1,40,5120]{2,1,0:T(8,128)} %second_ref.1) | copy-start | bytes 2457604
  118.5 31.6 %copy-start.2 = (f32[1,40,5120]{2,1,0:T(8,128)S(1)}, f32[1,40,5120]{2,1,0:T(8,128)}, u32[]{:S(2)}) copy-start(f32[1,40,5120]{2,1,0:T(8,128)} %first_ref.1) | copy-start | bytes 2457604
  118.5 10.0 %all-to-all-start.3 = ((bf16[8,88,128]{2,1,0:T(8,128)(2,1)}), bf16[8,88,128]{2,1,0:T(8,128)(2,1)S(1)}, u32[]{:S(2)}, u32[]{:S(2)}) async-start(bf16[8,88,128]{2,1,0:T(8,128)(2,1)} %shard_map.126), calls=%async_computation.3 | async-start | bytes 360448 | tf_op jit(solution)/shard_map/all_to_all | solution.py:25
  150.1 1.1 copy-start.5

commit v10 on v9

--- a/solution.py
+++ b/solution.py
@@ -139,19 +139,20 @@
         out_ref[chip, own_at : own_at + own.shape[0], :] = own
 
 
-def summed_grads(width, trip_ref):
-    total = trip_ref[0, width:, :].astype(jnp.float32)
-    for chip in range(1, trip_ref.shape[0]):
-        total += trip_ref[chip, width:, :].astype(jnp.float32)
-    return total.astype(jnp.bfloat16)
-
-
 def dnormed_kernel(
     width, core_ref, pair_ref, trip_ref, weight_ref, partner_ref,
-    grads_ref, mine_ref, other_ref,
+    grads_ref, mine_ref, other_ref, sent_ref,
 ):
-    grads = summed_grads(width, trip_ref)
+    chips, heads = trip_ref.shape[0], grads_ref.shape[0]
+    total = trip_ref[0, width:, :].astype(jnp.float32)
+    for chip in range(1, chips):
+        total += trip_ref[chip, width:, :].astype(jnp.float32)
+    grads = total.astype(jnp.bfloat16)
     grads_ref[...] = grads
+    for chip in range(chips):
+        sent_ref[chip] = trip_ref[chip, :width, :]
+    rest = jnp.zeros((width - heads, total.shape[1]), jnp.float32)
+    sent_ref[chips] = jnp.concatenate([total, rest], axis=0).astype(jnp.bfloat16)
     first_core, first_pair = core_ref[0] == 0, pair_ref[0] == 0
     refs = (weight_ref, partner_ref)
     grads = grads.astype(jnp.float32)
@@ -159,7 +160,7 @@
 
 
 def normalise(width, first_core, mine_ref, other_ref, gain_ref, normed_ref):
-    chips, _, lanes = mine_ref.shape
+    chips, lanes = gain_ref.shape[1] // (4 * width), mine_ref.shape[2]
     squares = jnp.zeros((width, lanes), jnp.float32)
     for chip in range(chips):
         for ref in (mine_ref, other_ref):
@@ -215,7 +216,8 @@
     lanes = norms_ref.shape[1]
     first_core, first_pair = core_ref[0] == 0, pair_ref[0] == 0
     normalise(width, first_core, mine_ref, other_ref, gain_ref, normed_ref)
-    grads = summed_grads(width, mine_ref).astype(jnp.float32)
+    chips, heads = mine_ref.shape[0] - 1, half_ref.shape[0]
+    grads = mine_ref[chips].astype(jnp.float32)[:heads]
     own = pieces_apart(grads, first_pair)[0].astype(jnp.bfloat16)
     norms = jnp.zeros((half_ref.shape[0], lanes), jnp.float32)
     span = 8 * width
@@ -404,16 +406,19 @@
         [],
         [mine, arrived, stream],
     )
+    payload, pair_weights = lax.optimization_barrier((payload, pair_weights))
     first_trip = swap(payload, TEAM)
     other_trip = moved(first_trip, "core")
-    pair_trip = moved(first_trip, "pair")
-    value_grads, mine, other = on_core(
+    value_grads, mine, other, sent = on_core(
         functools.partial(dnormed_kernel, width),
-        [shape((heads, rows))] + [shape((team, width, rows))] * 2,
+        [shape((heads, rows))]
+        + [shape((team, width, rows))] * 2
+        + [shape((team + 1, width, rows))],
         [core, pair],
         [first_trip, weights, pair_weights],
     )
     arrived = moved(other, "core")
+    pair_trip = moved(sent, "pair")
     own, half_gradient, inverse = on_core(
         functools.partial(values_kernel, width, heads),
         [

time: 154 us -> 159 us (1.032)
  blocking collectives: 28.1 us -> 61.3 us
  starting transfers between devices: 59.3 us -> 46 us
  waiting for transfers between devices: 44.2 us -> 32.1 us
    all_to_all x1 -> x2, blocking collectives: 20.8 us -> 55.2 us  [swap(): return lax.all_to_all(blocks, axis, split_axis=0, concat_axis=0, tiled=True)]
    all_to_all x4 -> x3, waiting for transfers between devices: 41.8 us -> 9.69 us  [swap(): return lax.all_to_all(blocks, axis, split_axis=0, concat_axis=0, tiled=True)]
    ppermute x7, waiting for transfers between devices: 2.48 us -> 22.4 us  [moved(): return lax.ppermute(block, axis, [(0, 1), (1, 0)])]
    all_to_all x4 -> x3, starting transfers between devices: 39.9 us -> 25 us  [swap(): return lax.all_to_all(blocks, axis, split_axis=0, concat_axis=0, tiled=True)]
    unnamed x36 -> x20, local copies, waits for them, and re-layouts: 4.73 us -> 4.55 us
  transfers between devices with their start and end apart: 11 -> 10, of which waited for: 6 -> 7; matrix products, arithmetic and copies ran while one was open for 2% -> 1% of each run, Pallas kernels for 3% -> 3%
where the time goes in v10:
time: 159 us; the launch traced here: 158 us
  blocking collectives  61.3 us (39%)
  starting transfers between devices  46 us (29%)
  waiting for transfers between devices  32.1 us (20%)
  Pallas kernels  10.7 us (7%)
  local copies, waits for them, and re-layouts  5.59 us (4%)
    all_to_all x2, blocking collectives, swap(): return lax.all_to_all(blocks, axis, split_axis=0, concat_axis=0, tiled=True)  55.2 us
    all_to_all x3, starting transfers between devices, swap(): return lax.all_to_all(blocks, axis, split_axis=0, concat_axis=0, tiled=True)  25 us
    ppermute x7, waiting for transfers between devices, moved(): return lax.ppermute(block, axis, [(0, 1), (1, 0)])  22.4 us
    ppermute x7, starting transfers between devices, moved(): return lax.ppermute(block, axis, [(0, 1), (1, 0)])  21 us
    pallas_call x10, Pallas kernels, on_core(): pl.pallas_call(kernel, out_shape=out_shape, in_specs=[pl.BlockSpec(memory...  10.7 us
    all_to_all x3, waiting for transfers between devices, swap(): return lax.all_to_all(blocks, axis, split_axis=0, concat_axis=0, tiled=True)  9.69 us
    unnamed x20, local copies, waits for them, and re-layouts  4.55 us
    all_gather x1, blocking collectives, body(): lax.all_gather(cols, 'core', axis=0)  4.09 us
  transfers between devices with their start and end apart: 10, of which 7 were waited for; matrix products, arithmetic and copies ran while one was open for 1% of the time, Pallas kernels for 3%

profile of v10, /device:TPU:1, one launch (start us, length us, event | category | flops | bytes accessed | tf_op | source)
XLA Modules:
  0.0 157.9 jit_solution(10068480558447857266)
XLA Ops:
  0.6 0.0 copy-start
  0.6 1.7 %shard_map.119 = bf16[32,8,320]{2,1,0:T(8,128)(2,1)} custom-call(bf16[1,1,2,2,5120]{4,3,2,1,0:T(2,128)(2,1)} %acts_ref.1, bf16[1,1,2,2,5120]{4,3,2,1,0:T(2,128)(2,1)} %cotan_ref.1), custom_call_target="tpu_custom_call" | custom-call | bytes 245760 | tf_op jit(solution)/shard_map/pallas_call | solution.py:330
  2.3 16.5 %all-to-all-start = ((bf16[32,8,320]{2,1,0:T(8,128)(2,1)}), bf16[32,8,320]{2,1,0:T(8,128)(2,1)S(1)}, u32[]{:S(2)}, u32[]{:S(2)}) async-start(bf16[32,8,320]{2,1,0:T(8,128)(2,1)} %shard_map.119), calls=%async_computation | async-start | bytes 393216 | tf_op jit(solution)/shard_map/all_to_all | solution.py:25
  18.9 3.1 %collective-permute-start = (bf16[80,2560]{1,0:T(8,128)(2,1)}, bf16[80,2560]{1,0:T(8,128)(2,1)S(1)}, u32[]{:S(2)}, u32[]{:S(2)}) collective-permute-start(bf16[80,2560]{1,0:T(8,128)(2,1)} %bitcast.33), channel_id=1, source_target_pairs={{0,2},{2,0},{1,3},{3,1},{4,6},{6,4},{5,7},{7,5},{8,10},{10,8},{9,1... | collective-permute-start | bytes 1228808 | tf_op jit(solution)/shard_map/ppermute | solution.py:29
  22.0 0.0 copy-done
  22.0 2.1 %collective-permute-start.2 = (bf16[40,5120]{1,0:T(8,128)(2,1)S(1)}, bf16[40,5120]{1,0:T(8,128)(2,1)S(1)}, u32[]{:S(2)}, u32[]{:S(2)}) collective-permute-start(bf16[40,5120]{1,0:T(8,128)(2,1)S(1)} %bitcast.28), channel_id=1, source_target_pairs={{0,2},{2,0},{1,3},{3,1},{4,6},{6,4},{5,7},{7,5},{8,10},{10,8},{9,1... | collective-permute-start | bytes 1228808 | tf_op jit(solution)/shard_map/ppermute | solution.py:29
  24.2 0.7 fusion.1
  24.8 0.1 convert_reduce_fusion.1
  24.9 0.7 add_multiply_fusion
  25.6 0.1 iota_add_fusion
  25.7 0.1 add.109
  25.8 0.0 copy-start.9
  25.8 0.1 broadcast_add_fusion.2
  25.9 0.1 pad_bitcast_fusion.1
  26.0 0.0 copy-start.1
  26.0 0.1 pad_add_fusion.1
  26.1 0.4 copy-done.9
  26.6 0.1 fusion.3
  26.6 0.1 broadcast_in_dim.7
  26.7 0.1 broadcast_in_dim.8
  26.8 0.1 pad_maximum_fusion.gain_ref
  26.9 3.9 %all-to-all-done = bf16[32,8,320]{2,1,0:T(8,128)(2,1)S(1)} async-done(((bf16[32,8,320]{2,1,0:T(8,128)(2,1)}), bf16[32,8,320]{2,1,0:T(8,128)(2,1)S(1)}, u32[]{:S(2)}, u32[]{:S(2)}) %all-to-all-start) | async-done | bytes 163872 | tf_op jit(solution)/shard_map/all_to_all | solution.py:25
  30.8 4.1 %all-gather = bf16[64,8,320]{2,1,0:T(8,128)(2,1)S(1)} all-gather(bf16[32,8,320]{2,1,0:T(8,128)(2,1)S(1)} %all-to-all-done), channel_id=2, replica_groups=mesh['section'=8,'team'=16,'pair'=2,'core'=2] {'core'}, dimensions={0}, use_global_device_ids=true | all-gather | bytes 491520 | tf_op jit(solution)/shard_map/all_gather | solution.py:394
  34.9 0.2 collective-permute-done.partner_ref
  35.1 0.0 copy-done.1
  35.1 1.1 shard_map.120
  36.2 3.8 %collective-permute-start.1 = (bf16[16,40,128]{2,1,0:T(8,128)(2,1)S(1)}, bf16[16,40,128]{2,1,0:T(8,128)(2,1)S(1)}, u32[]{:S(2)}, u32[]{:S(2)}) collective-permute-start(bf16[16,40,128]{2,1,0:T(8,128)(2,1)S(1)} %get-tuple-element.27), channel_id=1, source_target_pairs={{0,1},{1,0},{2,3},{3,2},{4,5},{5,4},{6,7},{7,6},{8,9},{9,8},{10,11... | collective-permute-start | bytes 491528 | tf_op jit(solution)/shard_map/ppermute | solution.py:29
  39.9 1.0 collective-permute-done.1.arrived_ref
  40.9 0.1 shard_map.121
  41.0 2.8 %collective-permute-done.2.partner_ref = bf16[40,5120]{1,0:T(8,128)(2,1)S(1)} collective-permute-done((bf16[40,5120]{1,0:T(8,128)(2,1)S(1)}, bf16[40,5120]{1,0:T(8,128)(2,1)S(1)}, u32[]{:S(2)}, u32[]{:S(2)}) %collective-permute-start.2) | collective-permute-done | bytes 409632 | tf_op jit(solution)/shard_map/ppermute | solution.py:29
  43.8 28.1 %all_to_all.25.trip_ref.mine_ref = bf16[16,120,128]{2,1,0:T(8,128)(2,1)S(1)} all-to-all(bf16[16,120,128]{2,1,0:T(8,128)(2,1)S(1)} %shard_map.121), channel_id=1, replica_groups=mesh['section'=8,'team'=16,'pair'=2,'core'=2] {'team'}, dimensions={0} | all-to-all | bytes 983040 | tf_op jit(solution)/shard_map/all_to_all | solution.py:25
  71.9 4.0 %collective-permute-start.4 = (bf16[16,120,128]{2,1,0:T(8,128)(2,1)S(1)}, bf16[16,120,128]{2,1,0:T(8,128)(2,1)S(1)}, u32[]{:S(2)}, u32[]{:S(2)}) collective-permute-start(bf16[16,120,128]{2,1,0:T(8,128)(2,1)S(1)} %all_to_all.25.trip_ref.mine_ref), channel_id=1, source_target_pairs={{0,1},{1,0},{2,3},{3,2},{4,5},{5,4},{6,7},{7,6},{8,9},{9,8},{10,11... | collective-permute-start | bytes 1474568 | tf_op jit(solution)/shard_map/ppermute | solution.py:29
  76.0 1.0 shard_map.122
  77.0 1.9 %collective-permute-start.3 = (bf16[16,80,128]{2,1,0:T(8,128)(2,1)S(1)}, bf16[16,80,128]{2,1,0:T(8,128)(2,1)S(1)}, u32[]{:S(2)}, u32[]{:S(2)}) collective-permute-start(bf16[16,80,128]{2,1,0:T(8,128)(2,1)S(1)} %get-tuple-element.32), channel_id=1, source_target_pairs={{0,1},{1,0},{2,3},{3,2},{4,5},{5,4},{6,7},{7,6},{8,9},{9,8},{10,11... | collective-permute-start | bytes 983048 | tf_op jit(solution)/shard_map/ppermute | solution.py:29
  78.9 0.0 collective-permute-done.4.other_ref
  78.9 1.6 shard_map.123
  80.5 0.0 collective-permute-done.3.arrived_ref
  80.5 0.9 shard_map.124
  81.4 4.4 %all-to-all-start.2 = ((bf16[16,128,128]{2,1,0:T(8,128)(2,1)}), bf16[16,128,128]{2,1,0:T(8,128)(2,1)S(1)}, u32[]{:S(2)}, u32[]{:S(2)}) async-start(bf16[16,128,128]{2,1,0:T(8,128)(2,1)} %shard_map.124), calls=%async_computation.2 | async-start | bytes 1048576 | tf_op jit(solution)/shard_map/all_to_all | solution.py:25
  85.8 3.2 %collective-permute-start.5 = (bf16[17,80,128]{2,1,0:T(8,128)(2,1)S(1)}, bf16[17,80,128]{2,1,0:T(8,128)(2,1)S(1)}, u32[]{:S(2)}, u32[]{:S(2)}) collective-permute-start(bf16[17,80,128]{2,1,0:T(8,128)(2,1)S(1)} %get-tuple-element.38), channel_id=1, source_target_pairs={{0,2},{2,0},{1,3},{3,1},{4,6},{6,4},{5,7},{7,5},{8,10},{10,8},{9,1... | collective-permute-start | bytes 1044488 | tf_op jit(solution)/shard_map/ppermute | solution.py:29
  88.9 17.9 %collective-permute-done.5.mine_ref = bf16[17,80,128]{2,1,0:T(8,128)(2,1)S(1)} collective-permute-done((bf16[17,80,128]{2,1,0:T(8,128)(2,1)S(1)}, bf16[17,80,128]{2,1,0:T(8,128)(2,1)S(1)}, u32[]{:S(2)}, u32[]{:S(2)}) %collective-permute-start.5) | collective-permute-done | bytes 348192 | tf_op jit(solution)/shard_map/ppermute | solution.py:29
  106.8 2.8 %collective-permute-start.6 = (bf16[17,80,128]{2,1,0:T(8,128)(2,1)S(1)}, bf16[17,80,128]{2,1,0:T(8,128)(2,1)S(1)}, u32[]{:S(2)}, u32[]{:S(2)}) collective-permute-start(bf16[17,80,128]{2,1,0:T(8,128)(2,1)S(1)} %collective-permute-done.5.mine_ref), channel_id=1, source_target_pairs={{0,1},{1,0},{2,3},{3,2},{4,5},{5,4},{6,7},{7,6},{8,9},{9,8},{10,11... | collective-permute-start | bytes 1044488 | tf_op jit(solution)/shard_map/ppermute | solution.py:29
  109.7 0.0 copy-start.5
  109.7 0.7 copy-done.5
  110.4 0.5 collective-permute-done.6.other_ref
  110.9 0.0 copy-start.7
  110.9 0.7 copy-done.7
  111.7 1.0 copy-done.6
  112.6 0.0 copy-start.8
  112.6 1.0 copy-done.8
  113.6 1.2 shard_map.125
  114.8 0.0 all-to-all-done.2.trip_ref
  114.9 2.1 %all-gather.1 = bf16[16,96,128]{2,1,0:T(8,128)(2,1)S(1)} all-gather(bf16[16,48,128]{2,1,0:T(8,128)(2,1)S(1)} %slice.8), channel_id=3, replica_groups=mesh['section'=8,'team'=16,'pair'=2,'core'=2] {'core'}, dimensions={1}, use_global_device_ids=true | all-gather | bytes 589824 | tf_op jit(solution)/shard_map/all_gather | solution.py:447
  117.0 0.5 shard_map.126
  117.5 0.0 copy-start.4
  117.5 0.7 copy-done.4
  118.2 4.1 %all-to-all-start.3 = ((bf16[8,88,128]{2,1,0:T(8,128)(2,1)}), bf16[8,88,128]{2,1,0:T(8,128)(2,1)S(1)}, u32[]{:S(2)}, u32[]{:S(2)}) async-start(bf16[8,88,128]{2,1,0:T(8,128)(2,1)} %copy-done.4), calls=%async_computation.3 | async-start | bytes 360448 | tf_op jit(solution)/shard_map/all_to_all | solution.py:25
  122.3 0.1 pad_add_fusion.2.from_ref
  122.4 5.8 %all-to-all-done.3.trip_ref = bf16[8,88,128]{2,1,0:T(8,128)(2,1)S(1)} async-done(((bf16[8,88,128]{2,1,0:T(8,128)(2,1)}), bf16[8,88,128]{2,1,0:T(8,128)(2,1)S(1)}, u32[]{:S(2)}, u32[]{:S(2)}) %all-to-all-start.3) | async-done | bytes 180256 | tf_op jit(solution)/shard_map/all_to_all | solution.py:25
  128.1 0.8 shard_map.127
  129.0 27.0 %all_to_all.26.trip_ref = bf16[64,16,128]{2,1,0:T(8,128)(2,1)S(1)} all-to-all(bf16[64,16,128]{2,1,0:T(8,128)(2,1)S(1)} %bitcast.37), channel_id=1, replica_groups=mesh['section'=8,'team'=16,'pair'=2,'core'=2] {'team','pair','core'}, dimensions={0} | all-to-all | bytes 524288 | tf_op jit(solution)/shard_map/all_to_all | solution.py:25
  156.0 0.0 copy-done.3
  156.0 0.0 copy-done.2
  156.0 1.9 %shard_map.128 = (bf16[1,1,2,2,5120]{4,3,2,1,0:T(2,128)(2,1)}, bf16[1,1,2,2,5120]{4,3,2,1,0:T(2,128)(2,1)}, bf16[1,40,5120]{2,1,0:T(8,128)(2,1)}, f32[1,40,5120]{2,1,0:T(8,128)}, f32[1,40,5120]{2,1,0:T(8,128)}) custom-call(bf16[64,16,128]{2,1,0:T(8,128)(2,1)S(1)} %all_to_all.26.trip_ref, f32[40,5120]{1,0:T(8,128)S(1)} %get-tuple-element.42.gradient_ref, ...), custom_call_target="tpu_custom_call" | custom-call | bytes 5259264 | tf_op jit(solution)/shard_map/pallas_call | solution.py:330
  (7 shorter events, 0.1 us)
Async XLA Ops:
  0.6 21.4 %copy-start = (bf16[1,40,5120]{2,1,0:T(8,128)(2,1)S(1)}, bf16[1,40,5120]{2,1,0:T(8,128)(2,1)}, u32[]{:S(2)}) copy-start(bf16[1,40,5120]{2,1,0:T(8,128)(2,1)} %weight_ref.1) | copy-start | bytes 1228804
  2.3 28.5 %all-to-all-start = ((bf16[32,8,320]{2,1,0:T(8,128)(2,1)}), bf16[32,8,320]{2,1,0:T(8,128)(2,1)S(1)}, u32[]{:S(2)}, u32[]{:S(2)}) async-start(bf16[32,8,320]{2,1,0:T(8,128)(2,1)} %shard_map.119), calls=%async_computation | async-start | bytes 393216 | tf_op jit(solution)/shard_map/all_to_all | solution.py:25
  18.9 16.2 %collective-permute-start = (bf16[80,2560]{1,0:T(8,128)(2,1)}, bf16[80,2560]{1,0:T(8,128)(2,1)S(1)}, u32[]{:S(2)}, u32[]{:S(2)}) collective-permute-start(bf16[80,2560]{1,0:T(8,128)(2,1)} %bitcast.33), channel_id=1, source_target_pairs={{0,2},{2,0},{1,3},{3,1},{4,6},{6,4},{5,7},{7,5},{8,10},{10,8},{9,1... | collective-permute-start | bytes 1228808 | tf_op jit(solution)/shard_map/ppermute | solution.py:29
  22.0 21.8 %collective-permute-start.2 = (bf16[40,5120]{1,0:T(8,128)(2,1)S(1)}, bf16[40,5120]{1,0:T(8,128)(2,1)S(1)}, u32[]{:S(2)}, u32[]{:S(2)}) collective-permute-start(bf16[40,5120]{1,0:T(8,128)(2,1)S(1)} %bitcast.28), channel_id=1, source_target_pairs={{0,2},{2,0},{1,3},{3,1},{4,6},{6,4},{5,7},{7,5},{8,10},{10,8},{9,1... | collective-permute-start | bytes 1228808 | tf_op jit(solution)/shard_map/ppermute | solution.py:29
  25.8 0.7 copy-start.9
  26.0 9.0 %copy-start.1 = (bf16[1,80,2560]{2,1,0:T(8,128)(2,1)S(1)}, bf16[1,80,2560]{2,1,0:T(8,128)(2,1)}, u32[]{:S(2)}) copy-start(bf16[1,80,2560]{2,1,0:T(8,128)(2,1)} %param.13) | copy-start | bytes 1228804
  36.2 4.8 %collective-permute-start.1 = (bf16[16,40,128]{2,1,0:T(8,128)(2,1)S(1)}, bf16[16,40,128]{2,1,0:T(8,128)(2,1)S(1)}, u32[]{:S(2)}, u32[]{:S(2)}) collective-permute-start(bf16[16,40,128]{2,1,0:T(8,128)(2,1)S(1)} %get-tuple-element.27), channel_id=1, source_target_pairs={{0,1},{1,0},{2,3},{3,2},{4,5},{5,4},{6,7},{7,6},{8,9},{9,8},{10,11... | collective-permute-start | bytes 491528 | tf_op jit(solution)/shard_map/ppermute | solution.py:29
  71.9 6.9 %collective-permute-start.4 = (bf16[16,120,128]{2,1,0:T(8,128)(2,1)S(1)}, bf16[16,120,128]{2,1,0:T(8,128)(2,1)S(1)}, u32[]{:S(2)}, u32[]{:S(2)}) collective-permute-start(bf16[16,120,128]{2,1,0:T(8,128)(2,1)S(1)} %all_to_all.25.trip_ref.mine_ref), channel_id=1, source_target_pairs={{0,1},{1,0},{2,3},{3,2},{4,5},{5,4},{6,7},{7,6},{8,9},{9,8},{10,11... | collective-permute-start | bytes 1474568 | tf_op jit(solution)/shard_map/ppermute | solution.py:29
  77.0 3.5 %collective-permute-start.3 = (bf16[16,80,128]{2,1,0:T(8,128)(2,1)S(1)}, bf16[16,80,128]{2,1,0:T(8,128)(2,1)S(1)}, u32[]{:S(2)}, u32[]{:S(2)}) collective-permute-start(bf16[16,80,128]{2,1,0:T(8,128)(2,1)S(1)} %get-tuple-element.32), channel_id=1, source_target_pairs={{0,1},{1,0},{2,3},{3,2},{4,5},{5,4},{6,7},{7,6},{8,9},{9,8},{10,11... | collective-permute-start | bytes 983048 | tf_op jit(solution)/shard_map/ppermute | solution.py:29
  81.4 33.4 %all-to-all-start.2 = ((bf16[16,128,128]{2,1,0:T(8,128)(2,1)}), bf16[16,128,128]{2,1,0:T(8,128)(2,1)S(1)}, u32[]{:S(2)}, u32[]{:S(2)}) async-start(bf16[16,128,128]{2,1,0:T(8,128)(2,1)} %shard_map.124), calls=%async_computation.2 | async-start | bytes 1048576 | tf_op jit(solution)/shard_map/all_to_all | solution.py:25
  85.8 21.1 %collective-permute-start.5 = (bf16[17,80,128]{2,1,0:T(8,128)(2,1)S(1)}, bf16[17,80,128]{2,1,0:T(8,128)(2,1)S(1)}, u32[]{:S(2)}, u32[]{:S(2)}) collective-permute-start(bf16[17,80,128]{2,1,0:T(8,128)(2,1)S(1)} %get-tuple-element.38), channel_id=1, source_target_pairs={{0,2},{2,0},{1,3},{3,1},{4,6},{6,4},{5,7},{7,5},{8,10},{10,8},{9,1... | collective-permute-start | bytes 1044488 | tf_op jit(solution)/shard_map/ppermute | solution.py:29
  106.8 4.1 %collective-permute-start.6 = (bf16[17,80,128]{2,1,0:T(8,128)(2,1)S(1)}, bf16[17,80,128]{2,1,0:T(8,128)(2,1)S(1)}, u32[]{:S(2)}, u32[]{:S(2)}) collective-permute-start(bf16[17,80,128]{2,1,0:T(8,128)(2,1)S(1)} %collective-permute-done.5.mine_ref), channel_id=1, source_target_pairs={{0,1},{1,0},{2,3},{3,2},{4,5},{5,4},{6,7},{7,6},{8,9},{9,8},{10,11... | collective-permute-start | bytes 1044488 | tf_op jit(solution)/shard_map/ppermute | solution.py:29
  109.7 0.7 copy-start.5
  110.9 0.7 copy-start.7
  111.7 1.0 copy-start.6
  112.6 1.0 copy-start.8
  117.0 39.0 %copy-start.3 = (f32[1,40,5120]{2,1,0:T(8,128)S(1)}, f32[1,40,5120]{2,1,0:T(8,128)}, u32[]{:S(2)}) copy-start(f32[1,40,5120]{2,1,0:T(8,128)} %second_ref.1) | copy-start | bytes 2457604
  117.5 0.7 copy-start.4
  118.2 37.9 %copy-start.2 = (f32[1,40,5120]{2,1,0:T(8,128)S(1)}, f32[1,40,5120]{2,1,0:T(8,128)}, u32[]{:S(2)}) copy-start(f32[1,40,5120]{2,1,0:T(8,128)} %first_ref.1) | copy-start | bytes 2457604
  118.2 10.0 %all-to-all-start.3 = ((bf16[8,88,128]{2,1,0:T(8,128)(2,1)}), bf16[8,88,128]{2,1,0:T(8,128)(2,1)S(1)}, u32[]{:S(2)}, u32[]{:S(2)}) async-start(bf16[8,88,128]{2,1,0:T(8,128)(2,1)} %copy-done.4), calls=%async_computation.3 | async-start | bytes 360448 | tf_op jit(solution)/shard_map/all_to_all | solution.py:25

commit v11 on v9

--- a/solution.py
+++ b/solution.py
@@ -404,6 +404,7 @@
         [],
         [mine, arrived, stream],
     )
+    payload, pair_weights = lax.optimization_barrier((payload, pair_weights))
     first_trip = swap(payload, TEAM)
     other_trip = moved(first_trip, "core")
     pair_trip = moved(first_trip, "pair")

time: 154 us -> 150 us (0.974)
  blocking collectives: 28.1 us -> 53.7 us
  waiting for transfers between devices: 44.2 us -> 27.2 us
  starting transfers between devices: 59.3 us -> 48.3 us
    all_to_all x1 -> x2, blocking collectives: 20.8 us -> 47.1 us  [swap(): return lax.all_to_all(blocks, axis, split_axis=0, concat_axis=0, tiled=True)]
    all_to_all x4 -> x3, waiting for transfers between devices: 41.8 us -> 17.3 us  [swap(): return lax.all_to_all(blocks, axis, split_axis=0, concat_axis=0, tiled=True)]
    all_to_all x4 -> x3, starting transfers between devices: 39.9 us -> 25.6 us  [swap(): return lax.all_to_all(blocks, axis, split_axis=0, concat_axis=0, tiled=True)]
    ppermute x7, waiting for transfers between devices: 2.48 us -> 9.87 us  [moved(): return lax.ppermute(block, axis, [(0, 1), (1, 0)])]
    ppermute x7, starting transfers between devices: 19.4 us -> 22.7 us  [moved(): return lax.ppermute(block, axis, [(0, 1), (1, 0)])]
  transfers between devices with their start and end apart: 11 -> 10, of which waited for: 6 -> 8; matrix products, arithmetic and copies ran while one was open for 2% -> 2% of each run, Pallas kernels for 3% -> 4%
where the time goes in v11:
time: 150 us; the launch traced here: 149 us
  blocking collectives  53.7 us (36%)
  starting transfers between devices  48.3 us (32%)
  waiting for transfers between devices  27.2 us (18%)
  Pallas kernels  11.4 us (8%)
  local copies, waits for them, and re-layouts  5.17 us (3%)
  other arithmetic  2.5 us (2%)
    all_to_all x2, blocking collectives, swap(): return lax.all_to_all(blocks, axis, split_axis=0, concat_axis=0, tiled=True)  47.1 us
    all_to_all x3, starting transfers between devices, swap(): return lax.all_to_all(blocks, axis, split_axis=0, concat_axis=0, tiled=True)  25.6 us
    ppermute x7, starting transfers between devices, moved(): return lax.ppermute(block, axis, [(0, 1), (1, 0)])  22.7 us
    all_to_all x3, waiting for transfers between devices, swap(): return lax.all_to_all(blocks, axis, split_axis=0, concat_axis=0, tiled=True)  17.3 us
    pallas_call x10, Pallas kernels, on_core(): pl.pallas_call(kernel, out_shape=out_shape, in_specs=[pl.BlockSpec(memory...  11.4 us
    ppermute x7, waiting for transfers between devices, moved(): return lax.ppermute(block, axis, [(0, 1), (1, 0)])  9.87 us
    unnamed x36, local copies, waits for them, and re-layouts  4.13 us
    all_gather x1, blocking collectives, body(): lax.all_gather(cols, 'core', axis=0)  4.09 us
  transfers between devices with their start and end apart: 10, of which 8 were waited for; matrix products, arithmetic and copies ran while one was open for 2% of the time, Pallas kernels for 4%

profile of v11, /device:TPU:1, one launch (start us, length us, event | category | flops | bytes accessed | tf_op | source)
XLA Modules:
  0.0 149.3 jit_solution(3247229550138335415)
XLA Ops:
  0.6 0.0 copy-start
  0.6 1.7 %shard_map.119 = bf16[32,8,320]{2,1,0:T(8,128)(2,1)} custom-call(bf16[1,1,2,2,5120]{4,3,2,1,0:T(2,128)(2,1)} %acts_ref.1, bf16[1,1,2,2,5120]{4,3,2,1,0:T(2,128)(2,1)} %cotan_ref.1), custom_call_target="tpu_custom_call" | custom-call | bytes 245760 | tf_op jit(solution)/shard_map/pallas_call | solution.py:328
  2.3 16.5 %all-to-all-start = ((bf16[32,8,320]{2,1,0:T(8,128)(2,1)}), bf16[32,8,320]{2,1,0:T(8,128)(2,1)S(1)}, u32[]{:S(2)}, u32[]{:S(2)}) async-start(bf16[32,8,320]{2,1,0:T(8,128)(2,1)} %shard_map.119), calls=%async_computation | async-start | bytes 393216 | tf_op jit(solution)/shard_map/all_to_all | solution.py:25
  18.9 3.1 %collective-permute-start = (bf16[80,2560]{1,0:T(8,128)(2,1)}, bf16[80,2560]{1,0:T(8,128)(2,1)S(1)}, u32[]{:S(2)}, u32[]{:S(2)}) collective-permute-start(bf16[80,2560]{1,0:T(8,128)(2,1)} %bitcast.33), channel_id=1, source_target_pairs={{0,2},{2,0},{1,3},{3,1},{4,6},{6,4},{5,7},{7,5},{8,10},{10,8},{9,1... | collective-permute-start | bytes 1228808 | tf_op jit(solution)/shard_map/ppermute | solution.py:29
  22.0 0.0 copy-done
  22.0 2.1 %collective-permute-start.2 = (bf16[40,5120]{1,0:T(8,128)(2,1)S(1)}, bf16[40,5120]{1,0:T(8,128)(2,1)S(1)}, u32[]{:S(2)}, u32[]{:S(2)}) collective-permute-start(bf16[40,5120]{1,0:T(8,128)(2,1)S(1)} %bitcast.28), channel_id=1, source_target_pairs={{0,2},{2,0},{1,3},{3,1},{4,6},{6,4},{5,7},{7,5},{8,10},{10,8},{9,1... | collective-permute-start | bytes 1228808 | tf_op jit(solution)/shard_map/ppermute | solution.py:29
  24.2 0.7 fusion.1
  24.8 0.1 convert_reduce_fusion.1
  24.9 0.7 add_multiply_fusion
  25.6 0.1 iota_add_fusion
  25.7 0.1 add.109
  25.8 0.0 copy-start.7
  25.8 0.1 broadcast_add_fusion.2
  25.9 0.1 pad_bitcast_fusion.1
  26.0 0.7 pad_add_fusion.1
  26.7 0.0 copy-done.7
  26.7 0.1 fusion.3
  26.8 0.1 broadcast_in_dim.7
  26.8 0.1 broadcast_in_dim.8
  26.9 0.7 pad_maximum_fusion.gain_ref
  27.6 3.2 %all-to-all-done = bf16[32,8,320]{2,1,0:T(8,128)(2,1)S(1)} async-done(((bf16[32,8,320]{2,1,0:T(8,128)(2,1)}), bf16[32,8,320]{2,1,0:T(8,128)(2,1)S(1)}, u32[]{:S(2)}, u32[]{:S(2)}) %all-to-all-start) | async-done | bytes 163872 | tf_op jit(solution)/shard_map/all_to_all | solution.py:25
  30.8 4.1 %all-gather = bf16[64,8,320]{2,1,0:T(8,128)(2,1)S(1)} all-gather(bf16[32,8,320]{2,1,0:T(8,128)(2,1)S(1)} %all-to-all-done), channel_id=2, replica_groups=mesh['section'=8,'team'=16,'pair'=2,'core'=2] {'core'}, dimensions={0}, use_global_device_ids=true | all-gather | bytes 491520 | tf_op jit(solution)/shard_map/all_gather | solution.py:392
  34.9 0.2 collective-permute-done.partner_ref
  35.1 0.0 copy-done.1
  35.1 1.1 shard_map.120
  36.2 0.0 copy-start.9
  36.2 0.0 copy-start.11
  36.2 3.8 %collective-permute-start.1 = (bf16[16,40,128]{2,1,0:T(8,128)(2,1)S(1)}, bf16[16,40,128]{2,1,0:T(8,128)(2,1)S(1)}, u32[]{:S(2)}, u32[]{:S(2)}) collective-permute-start(bf16[16,40,128]{2,1,0:T(8,128)(2,1)S(1)} %get-tuple-element.26), channel_id=1, source_target_pairs={{0,1},{1,0},{2,3},{3,2},{4,5},{5,4},{6,7},{7,6},{8,9},{9,8},{10,11... | collective-permute-start | bytes 491528 | tf_op jit(solution)/shard_map/ppermute | solution.py:29
  40.0 1.0 collective-permute-done.1.arrived_ref
  41.0 0.1 shard_map.121
  41.1 2.8 %collective-permute-done.2.partner_ref = bf16[40,5120]{1,0:T(8,128)(2,1)S(1)} collective-permute-done((bf16[40,5120]{1,0:T(8,128)(2,1)S(1)}, bf16[40,5120]{1,0:T(8,128)(2,1)S(1)}, u32[]{:S(2)}, u32[]{:S(2)}) %collective-permute-start.2) | collective-permute-done | bytes 409632 | tf_op jit(solution)/shard_map/ppermute | solution.py:29
  43.8 28.1 %all_to_all.25.trip_ref.mine_ref = bf16[16,120,128]{2,1,0:T(8,128)(2,1)S(1)} all-to-all(bf16[16,120,128]{2,1,0:T(8,128)(2,1)S(1)} %shard_map.121), channel_id=1, replica_groups=mesh['section'=8,'team'=16,'pair'=2,'core'=2] {'team'}, dimensions={0} | all-to-all | bytes 983040 | tf_op jit(solution)/shard_map/all_to_all | solution.py:25
  71.9 4.0 %collective-permute-start.4 = (bf16[16,120,128]{2,1,0:T(8,128)(2,1)S(1)}, bf16[16,120,128]{2,1,0:T(8,128)(2,1)S(1)}, u32[]{:S(2)}, u32[]{:S(2)}) collective-permute-start(bf16[16,120,128]{2,1,0:T(8,128)(2,1)S(1)} %all_to_all.25.trip_ref.mine_ref), channel_id=1, source_target_pairs={{0,1},{1,0},{2,3},{3,2},{4,5},{5,4},{6,7},{7,6},{8,9},{9,8},{10,11... | collective-permute-start | bytes 1474568 | tf_op jit(solution)/shard_map/ppermute | solution.py:29
  76.0 1.0 shard_map.122
  76.9 1.9 %collective-permute-start.3 = (bf16[16,80,128]{2,1,0:T(8,128)(2,1)S(1)}, bf16[16,80,128]{2,1,0:T(8,128)(2,1)S(1)}, u32[]{:S(2)}, u32[]{:S(2)}) collective-permute-start(bf16[16,80,128]{2,1,0:T(8,128)(2,1)S(1)} %get-tuple-element.31), channel_id=1, source_target_pairs={{0,1},{1,0},{2,3},{3,2},{4,5},{5,4},{6,7},{7,6},{8,9},{9,8},{10,11... | collective-permute-start | bytes 983048 | tf_op jit(solution)/shard_map/ppermute | solution.py:29
  78.9 2.7 %collective-permute-start.5 = (bf16[16,120,128]{2,1,0:T(8,128)(2,1)S(1)}, bf16[16,120,128]{2,1,0:T(8,128)(2,1)S(1)}, u32[]{:S(2)}, u32[]{:S(2)}) collective-permute-start(bf16[16,120,128]{2,1,0:T(8,128)(2,1)S(1)} %all_to_all.25.trip_ref.mine_ref), channel_id=1, source_target_pairs={{0,2},{2,0},{1,3},{3,1},{4,6},{6,4},{5,7},{7,5},{8,10},{10,8},{9,1... | collective-permute-start | bytes 1474568 | tf_op jit(solution)/shard_map/ppermute | solution.py:29
  81.6 0.0 collective-permute-done.4.other_ref
  81.6 1.6 %shard_map.123 = (bf16[48,128]{1,0:T(8,128)(2,1)S(1)}, f32[40,5120]{1,0:T(8,128)S(1)}, f32[8,128]{1,0:T(8,128)S(1)}) custom-call(s32[1]{0:T(128)} %bitcast.3.core_ref, s32[1]{0:T(128)} %bitcast.2.pair_ref, bf16[16,120,128]{2,1,0:T(8,128)(2,1)S(1)} %all_to_all.25.trip_ref.mine_ref, bf16[16,120,128]{2,1,0:T(8,128)(2,1)S(1)} %collective-permute-done.4.other_ref, ...), custom_call_target="tpu_custom_call" | custom-call | bytes 2658304 | tf_op jit(solution)/shard_map/pallas_call | solution.py:328
  83.2 0.0 collective-permute-done.3.arrived_ref
  83.2 0.9 shard_map.124
  84.1 4.8 %all-to-all-start.2 = ((bf16[16,128,128]{2,1,0:T(8,128)(2,1)}), bf16[16,128,128]{2,1,0:T(8,128)(2,1)S(1)}, u32[]{:S(2)}, u32[]{:S(2)}) async-start(bf16[16,128,128]{2,1,0:T(8,128)(2,1)} %shard_map.124), calls=%async_computation.2 | async-start | bytes 1048576 | tf_op jit(solution)/shard_map/all_to_all | solution.py:25
  88.9 4.5 %collective-permute-done.5.mine_ref = bf16[16,120,128]{2,1,0:T(8,128)(2,1)S(1)} collective-permute-done((bf16[16,120,128]{2,1,0:T(8,128)(2,1)S(1)}, bf16[16,120,128]{2,1,0:T(8,128)(2,1)S(1)}, u32[]{:S(2)}, u32[]{:S(2)}) %collective-permute-start.5) | collective-permute-done | bytes 491552 | tf_op jit(solution)/shard_map/ppermute | solution.py:29
  93.4 5.0 %collective-permute-start.6 = (bf16[16,120,128]{2,1,0:T(8,128)(2,1)S(1)}, bf16[16,120,128]{2,1,0:T(8,128)(2,1)S(1)}, u32[]{:S(2)}, u32[]{:S(2)}) collective-permute-start(bf16[16,120,128]{2,1,0:T(8,128)(2,1)S(1)} %collective-permute-done.5.mine_ref), channel_id=1, source_target_pairs={{0,1},{1,0},{2,3},{3,2},{4,5},{5,4},{6,7},{7,6},{8,9},{9,8},{10,11... | collective-permute-start | bytes 1474568 | tf_op jit(solution)/shard_map/ppermute | solution.py:29
  98.4 1.5 collective-permute-done.6.other_ref
  99.9 0.7 copy-done.8
  100.6 1.3 shard_map.125
  101.9 0.0 copy-start.4
  101.9 0.9 copy-done.4
  102.8 0.6 copy-done.15
  103.4 8.4 %all-to-all-done.2.trip_ref = bf16[16,128,128]{2,1,0:T(8,128)(2,1)S(1)} async-done(((bf16[16,128,128]{2,1,0:T(8,128)(2,1)}), bf16[16,128,128]{2,1,0:T(8,128)(2,1)S(1)}, u32[]{:S(2)}, u32[]{:S(2)}) %all-to-all-start.2) | async-done | bytes 524320 | tf_op jit(solution)/shard_map/all_to_all | solution.py:25
  111.8 0.0 copy-start.12
  111.8 2.5 %all-gather.1 = bf16[16,96,128]{2,1,0:T(8,128)(2,1)S(1)} all-gather(bf16[16,48,128]{2,1,0:T(8,128)(2,1)S(1)} %slice.8), channel_id=3, replica_groups=mesh['section'=8,'team'=16,'pair'=2,'core'=2] {'core'}, dimensions={1}, use_global_device_ids=true | all-gather | bytes 589824 | tf_op jit(solution)/shard_map/all_gather | solution.py:443
  114.4 0.7 copy-done.6
  115.1 0.0 copy-done.10
  115.1 0.0 copy-done.14
  115.2 0.0 copy-start.3
  115.2 1.1 shard_map.126
  116.3 4.2 %all-to-all-start.3 = ((bf16[8,88,128]{2,1,0:T(8,128)(2,1)}), bf16[8,88,128]{2,1,0:T(8,128)(2,1)S(1)}, u32[]{:S(2)}, u32[]{:S(2)}) async-start(bf16[8,88,128]{2,1,0:T(8,128)(2,1)} %shard_map.126), calls=%async_computation.3 | async-start | bytes 360448 | tf_op jit(solution)/shard_map/all_to_all | solution.py:25
  120.5 0.1 pad_add_fusion.2.from_ref
  120.6 5.8 %all-to-all-done.3.trip_ref = bf16[8,88,128]{2,1,0:T(8,128)(2,1)S(1)} async-done(((bf16[8,88,128]{2,1,0:T(8,128)(2,1)}), bf16[8,88,128]{2,1,0:T(8,128)(2,1)S(1)}, u32[]{:S(2)}, u32[]{:S(2)}) %all-to-all-start.3) | async-done | bytes 180256 | tf_op jit(solution)/shard_map/all_to_all | solution.py:25
  126.4 0.8 shard_map.127
  127.2 19.0 %all_to_all.26.trip_ref = bf16[64,16,128]{2,1,0:T(8,128)(2,1)S(1)} all-to-all(bf16[64,16,128]{2,1,0:T(8,128)(2,1)S(1)} %bitcast.37), channel_id=1, replica_groups=mesh['section'=8,'team'=16,'pair'=2,'core'=2] {'team','pair','core'}, dimensions={0} | all-to-all | bytes 524288 | tf_op jit(solution)/shard_map/all_to_all | solution.py:25
  146.2 1.1 copy-done.5
  147.4 1.9 %shard_map.128 = (bf16[1,1,2,2,5120]{4,3,2,1,0:T(2,128)(2,1)}, bf16[1,1,2,2,5120]{4,3,2,1,0:T(2,128)(2,1)}, bf16[1,40,5120]{2,1,0:T(8,128)(2,1)}, f32[1,40,5120]{2,1,0:T(8,128)}, f32[1,40,5120]{2,1,0:T(8,128)}) custom-call(bf16[64,16,128]{2,1,0:T(8,128)(2,1)S(1)} %all_to_all.26.trip_ref, f32[40,5120]{1,0:T(8,128)S(1)} %copy-done.5, ...), custom_call_target="tpu_custom_call" | custom-call | bytes 5259264 | tf_op jit(solution)/shard_map/pallas_call | solution.py:328
  (23 shorter events, 0.1 us)
Async XLA Ops:
  0.6 21.4 %copy-start = (bf16[1,40,5120]{2,1,0:T(8,128)(2,1)S(1)}, bf16[1,40,5120]{2,1,0:T(8,128)(2,1)}, u32[]{:S(2)}) copy-start(bf16[1,40,5120]{2,1,0:T(8,128)(2,1)} %weight_ref.1) | copy-start | bytes 1228804
  2.3 28.5 %all-to-all-start = ((bf16[32,8,320]{2,1,0:T(8,128)(2,1)}), bf16[32,8,320]{2,1,0:T(8,128)(2,1)S(1)}, u32[]{:S(2)}, u32[]{:S(2)}) async-start(bf16[32,8,320]{2,1,0:T(8,128)(2,1)} %shard_map.119), calls=%async_computation | async-start | bytes 393216 | tf_op jit(solution)/shard_map/all_to_all | solution.py:25
  18.9 16.2 %collective-permute-start = (bf16[80,2560]{1,0:T(8,128)(2,1)}, bf16[80,2560]{1,0:T(8,128)(2,1)S(1)}, u32[]{:S(2)}, u32[]{:S(2)}) collective-permute-start(bf16[80,2560]{1,0:T(8,128)(2,1)} %bitcast.33), channel_id=1, source_target_pairs={{0,2},{2,0},{1,3},{3,1},{4,6},{6,4},{5,7},{7,5},{8,10},{10,8},{9,1... | collective-permute-start | bytes 1228808 | tf_op jit(solution)/shard_map/ppermute | solution.py:29
  22.0 21.8 %collective-permute-start.2 = (bf16[40,5120]{1,0:T(8,128)(2,1)S(1)}, bf16[40,5120]{1,0:T(8,128)(2,1)S(1)}, u32[]{:S(2)}, u32[]{:S(2)}) collective-permute-start(bf16[40,5120]{1,0:T(8,128)(2,1)S(1)} %bitcast.28), channel_id=1, source_target_pairs={{0,2},{2,0},{1,3},{3,1},{4,6},{6,4},{5,7},{7,5},{8,10},{10,8},{9,1... | collective-permute-start | bytes 1228808 | tf_op jit(solution)/shard_map/ppermute | solution.py:29
  25.8 0.9 copy-start.7
  26.0 9.0 %copy-start.1 = (bf16[1,80,2560]{2,1,0:T(8,128)(2,1)S(1)}, bf16[1,80,2560]{2,1,0:T(8,128)(2,1)}, u32[]{:S(2)}) copy-start(bf16[1,80,2560]{2,1,0:T(8,128)(2,1)} %param.13) | copy-start | bytes 1228804
  36.2 4.9 %copy-start.9 = (bf16[80,128]{1,0:T(8,128)(2,1)}, bf16[80,128]{1,0:T(8,128)(2,1)S(1)}, u32[]{:S(2)}) copy-start(bf16[80,128]{1,0:T(8,128)(2,1)S(1)} %get-tuple-element.27.own_ref.stream_ref) | copy-start | bytes 61444
  36.2 4.9 %copy-start.11 = (bf16[80,128]{1,0:T(8,128)(2,1)}, bf16[80,128]{1,0:T(8,128)(2,1)S(1)}, u32[]{:S(2)}) copy-start(bf16[80,128]{1,0:T(8,128)(2,1)S(1)} %get-tuple-element.34.cotangent_ref) | copy-start | bytes 61444
  36.2 4.8 %collective-permute-start.1 = (bf16[16,40,128]{2,1,0:T(8,128)(2,1)S(1)}, bf16[16,40,128]{2,1,0:T(8,128)(2,1)S(1)}, u32[]{:S(2)}, u32[]{:S(2)}) collective-permute-start(bf16[16,40,128]{2,1,0:T(8,128)(2,1)S(1)} %get-tuple-element.26), channel_id=1, source_target_pairs={{0,1},{1,0},{2,3},{3,2},{4,5},{5,4},{6,7},{7,6},{8,9},{9,8},{10,11... | collective-permute-start | bytes 491528 | tf_op jit(solution)/shard_map/ppermute | solution.py:29
  71.9 9.6 %collective-permute-start.4 = (bf16[16,120,128]{2,1,0:T(8,128)(2,1)S(1)}, bf16[16,120,128]{2,1,0:T(8,128)(2,1)S(1)}, u32[]{:S(2)}, u32[]{:S(2)}) collective-permute-start(bf16[16,120,128]{2,1,0:T(8,128)(2,1)S(1)} %all_to_all.25.trip_ref.mine_ref), channel_id=1, source_target_pairs={{0,1},{1,0},{2,3},{3,2},{4,5},{5,4},{6,7},{7,6},{8,9},{9,8},{10,11... | collective-permute-start | bytes 1474568 | tf_op jit(solution)/shard_map/ppermute | solution.py:29
  76.9 6.2 %collective-permute-start.3 = (bf16[16,80,128]{2,1,0:T(8,128)(2,1)S(1)}, bf16[16,80,128]{2,1,0:T(8,128)(2,1)S(1)}, u32[]{:S(2)}, u32[]{:S(2)}) collective-permute-start(bf16[16,80,128]{2,1,0:T(8,128)(2,1)S(1)} %get-tuple-element.31), channel_id=1, source_target_pairs={{0,1},{1,0},{2,3},{3,2},{4,5},{5,4},{6,7},{7,6},{8,9},{9,8},{10,11... | collective-permute-start | bytes 983048 | tf_op jit(solution)/shard_map/ppermute | solution.py:29
  78.9 14.5 %collective-permute-start.5 = (bf16[16,120,128]{2,1,0:T(8,128)(2,1)S(1)}, bf16[16,120,128]{2,1,0:T(8,128)(2,1)S(1)}, u32[]{:S(2)}, u32[]{:S(2)}) collective-permute-start(bf16[16,120,128]{2,1,0:T(8,128)(2,1)S(1)} %all_to_all.25.trip_ref.mine_ref), channel_id=1, source_target_pairs={{0,2},{2,0},{1,3},{3,1},{4,6},{6,4},{5,7},{7,5},{8,10},{10,8},{9,1... | collective-permute-start | bytes 1474568 | tf_op jit(solution)/shard_map/ppermute | solution.py:29
  83.2 0.9 copy-start.13
  84.1 27.7 %all-to-all-start.2 = ((bf16[16,128,128]{2,1,0:T(8,128)(2,1)}), bf16[16,128,128]{2,1,0:T(8,128)(2,1)S(1)}, u32[]{:S(2)}, u32[]{:S(2)}) async-start(bf16[16,128,128]{2,1,0:T(8,128)(2,1)} %shard_map.124), calls=%async_computation.2 | async-start | bytes 1048576 | tf_op jit(solution)/shard_map/all_to_all | solution.py:25
  93.4 6.5 %collective-permute-start.6 = (bf16[16,120,128]{2,1,0:T(8,128)(2,1)S(1)}, bf16[16,120,128]{2,1,0:T(8,128)(2,1)S(1)}, u32[]{:S(2)}, u32[]{:S(2)}) collective-permute-start(bf16[16,120,128]{2,1,0:T(8,128)(2,1)S(1)} %collective-permute-done.5.mine_ref), channel_id=1, source_target_pairs={{0,1},{1,0},{2,3},{3,2},{4,5},{5,4},{6,7},{7,6},{8,9},{9,8},{10,11... | collective-permute-start | bytes 1474568 | tf_op jit(solution)/shard_map/ppermute | solution.py:29
  99.9 0.7 copy-start.8
  101.9 0.9 copy-start.4
  102.8 0.6 copy-start.15
  111.8 2.6 %copy-start.12 = (bf16[80,128]{1,0:T(8,128)(2,1)S(1)}, bf16[80,128]{1,0:T(8,128)(2,1)}, u32[]{:S(2)}) copy-start(bf16[80,128]{1,0:T(8,128)(2,1)} %copy-done.11) | copy-start | bytes 61444
  114.4 0.8 copy-start.6
  114.4 0.8 copy-start.10
  114.4 0.8 copy-start.16
  114.4 0.7 copy-start.14
  115.1 11.2 %copy-start.17 = (s32[256]{0:T(256)S(1)}, s32[256]{0:T(256)}, u32[]{:S(2)}) copy-start(s32[256]{0:T(256)} %pad_add_fusion.1) | copy-start | bytes 3076
  115.2 31.1 %copy-start.3 = (f32[1,40,5120]{2,1,0:T(8,128)S(1)}, f32[1,40,5120]{2,1,0:T(8,128)}, u32[]{:S(2)}) copy-start(f32[1,40,5120]{2,1,0:T(8,128)} %second_ref.1) | copy-start | bytes 2457604
  116.3 29.9 %copy-start.2 = (f32[1,40,5120]{2,1,0:T(8,128)S(1)}, f32[1,40,5120]{2,1,0:T(8,128)}, u32[]{:S(2)}) copy-start(f32[1,40,5120]{2,1,0:T(8,128)} %first_ref.1) | copy-start | bytes 2457604
  116.3 10.1 %all-to-all-start.3 = ((bf16[8,88,128]{2,1,0:T(8,128)(2,1)}), bf16[8,88,128]{2,1,0:T(8,128)(2,1)S(1)}, u32[]{:S(2)}, u32[]{:S(2)}) async-start(bf16[8,88,128]{2,1,0:T(8,128)(2,1)} %shard_map.126), calls=%async_computation.3 | async-start | bytes 360448 | tf_op jit(solution)/shard_map/all_to_all | solution.py:25
  146.2 1.1 copy-start.5
